TPU v7x, 32 devices: a whole 2x2x4 slice. The times are simulated.
32 devices in a mesh: stream: 2 (over x), dp: 16 (over z, y, core).
Axes of the slice: x: 2, y: 2, z: 4, core: 2. Of those that a mesh axis runs over, the one named last changes fastest.
Arguments:
- tokens: bfloat16 [2, 8192, 1152], P('stream', 'dp'), may hold values from -6 to 6
- condition: bfloat16 [2, 48, 1152], P('stream', 'dp'), may hold values from -6 to 6
- segments: int32 [2, 8192], P('stream', 'dp'), may hold values from 0 to 2, as said below
- positions: int32 [2, 8192], P('stream', 'dp'), may hold values from 0 to 255, as said below
- buckets: int32 [256, 256], replicated, may hold values from 0 to 960
- modulator: bfloat16 [1152, 6912], P('dp'), may hold values from -0.1875 to 0.1875
- modulator_bias: bfloat16 [6912], P('dp'), may hold values from -3 to 3
- projector: bfloat16 [1152, 3456], P('dp'), may hold values from -0.1875 to 0.1875
- projector_bias: bfloat16 [2304], P('dp'), may hold values from -3 to 3
- position_table: bfloat16 [16, 961], replicated, may hold values from -6 to 6
- output_weight: bfloat16 [1152, 1152], P('dp'), may hold values from -0.75 to 0.75
- output_bias: bfloat16 [1152], P('dp'), may hold values from -3 to 3
- up_weight: bfloat16 [1152, 4608], P('dp'), may hold values from -0.1875 to 0.1875
- up_bias: bfloat16 [4608], P('dp'), may hold values from -3 to 3
- down_weight: bfloat16 [4608, 1152], P('dp'), may hold values from -0.09375 to 0.09375
- down_bias: bfloat16 [1152], P('dp'), may hold values from -3 to 3
- cotangent: bfloat16 [2, 8192, 1152], P('stream', 'dp'), may hold values from -6 to 6
Outputs:
- result: bfloat16 [2, 8192, 1152], P('stream', 'dp')
- grad_tokens: float32 [2, 8192, 1152], P('stream', 'dp')
- grad_condition: float32 [2, 48, 1152], P('stream', 'dp')
- grad_modulator: float32 [1152, 6912], P('dp')
- grad_modulator_bias: float32 [6912], P('dp')
- grad_projector: float32 [1152, 3456], P('dp')
- grad_projector_bias: float32 [2304], P('dp')
- grad_position_table: float32 [16, 961], replicated
- grad_output_weight: float32 [1152, 1152], P('dp')
- grad_output_bias: float32 [1152], P('dp')
- grad_up_weight: float32 [1152, 4608], P('dp')
- grad_up_bias: float32 [4608], P('dp')
- grad_down_weight: float32 [4608, 1152], P('dp')
- grad_down_bias: float32 [1152], P('dp')
Inputs may be any that keep to these rules, and one draw needn't show every extreme that they name: `segments`: rows come in aligned blocks of 512, each holding image slots 0, 1, 2 in this order, an image's rows together. In the first pass each slot holds 1 to 256 rows; in the second pass slots 0 and 1 hold 256 rows each and slot 2 none. `positions`: A row's place among its image's 256 tokens, rising within an image; in the second pass every place in order.
All inputs are finite; a program needn't handle non-finite values.
Results may differ from a plain program's by a relative error of at most 0.014.
The roundings to bfloat16 on the way count: a program that leaves them out, or rounds other values in their place, can miss the bound.
Values may be sent and summed in bfloat16 or wider, within the bound.
A program may use at most 512 MiB of HBM per device.

v0:
```python
import jax
import jax.numpy as jnp
from jax import lax
from jax.sharding import PartitionSpec as P

norm_epsilon = 1e-06
masked_score = -1000000000.0
head_group_size = 4


def normalize(values):
    center = values - jnp.mean(values, axis=-1, keepdims=True)
    inverse = lax.rsqrt(jnp.mean(center * center, axis=-1, keepdims=True) + norm_epsilon)
    return (center * inverse, inverse)


def normalize_back(normed, inverse, upstream):
    return inverse * (
        upstream
        - jnp.mean(upstream, axis=-1, keepdims=True)
        - normed * jnp.mean(upstream * normed, axis=-1, keepdims=True)
    )


def smooth_gelu(values):
    return jax.nn.gelu(values, approximate=True)


def split_heads(packed, head_count):
    model_width = packed.shape[1] // 3
    shaped = packed.reshape(packed.shape[0], 3, head_count, model_width // head_count)
    return (shaped[:, 0], shaped[:, 1], shaped[:, 2])


def place_table(places, image_tokens):
    return (places[:, None] == jnp.arange(image_tokens, dtype=jnp.int32)[None, :]).astype(
        jnp.float32
    )


def group_scores(queries, keys_part, grid_part, place_onehot, same_image, score_scale):
    row_bias = jnp.einsum("qa,hab->hqb", place_onehot, grid_part, precision=lax.Precision.HIGHEST)
    bias_part = jnp.einsum("hqb,kb->hqk", row_bias, place_onehot, precision=lax.Precision.HIGHEST)
    raw_scores = (
        jnp.einsum("qhd,khd->hqk", queries, keys_part, preferred_element_type=jnp.float32)
        * score_scale
        + bias_part
    )
    return jnp.where(same_image[None], raw_scores, masked_score)


def attend_pack(pos_grid, head_count, image_tokens, packed, slot_ids, places):
    queries, keys_all, values_all = split_heads(packed, head_count)
    score_scale = queries.shape[2] ** (-0.5)
    place_onehot = place_table(places, image_tokens)
    same_image = slot_ids[:, None] == slot_ids[None, :]
    outputs = []
    totals = []
    for head_start in range(0, head_count, head_group_size):
        head_stop = head_start + head_group_size
        scores = group_scores(
            queries[:, head_start:head_stop],
            keys_all[:, head_start:head_stop],
            pos_grid[head_start:head_stop],
            place_onehot,
            same_image,
            score_scale,
        )
        maximum = jnp.max(scores, axis=-1, keepdims=True)
        exponent = jnp.exp(scores - maximum)
        denominator = jnp.sum(exponent, axis=-1, keepdims=True)
        weights = (exponent / denominator).astype(jnp.bfloat16)
        outputs.append(
            jnp.einsum(
                "hqk,khd->qhd",
                weights,
                values_all[:, head_start:head_stop],
                preferred_element_type=jnp.float32,
            )
        )
        totals.append((maximum + jnp.log(denominator))[..., 0])
    mixture = jnp.concatenate(outputs, axis=1).reshape(packed.shape[0], -1)
    return (mixture, jnp.concatenate(totals, axis=0))


def attend_back(pos_grid, head_count, image_tokens, packed, slot_ids, places, log_totals, upstream):
    queries, keys_all, values_all = split_heads(packed, head_count)
    head_width = queries.shape[2]
    score_scale = head_width ** (-0.5)
    place_onehot_float = place_table(places, image_tokens)
    place_onehot = place_onehot_float.astype(jnp.bfloat16)
    same_image = slot_ids[:, None] == slot_ids[None, :]
    incoming = upstream.reshape(upstream.shape[0], head_count, head_width)
    query_grads = []
    key_grads = []
    value_grads = []
    table_grads = []
    for head_start in range(0, head_count, head_group_size):
        head_stop = head_start + head_group_size
        scores = group_scores(
            queries[:, head_start:head_stop],
            keys_all[:, head_start:head_stop],
            pos_grid[head_start:head_stop],
            place_onehot_float,
            same_image,
            score_scale,
        )
        weights = jnp.exp(scores - log_totals[head_start:head_stop][:, :, None])
        incoming_part = incoming[:, head_start:head_stop]
        value_grads.append(
            jnp.einsum(
                "hqk,qhd->khd",
                weights.astype(jnp.bfloat16),
                incoming_part,
                preferred_element_type=jnp.float32,
            )
        )
        weight_grads = jnp.einsum(
            "qhd,khd->hqk",
            incoming_part,
            values_all[:, head_start:head_stop],
            preferred_element_type=jnp.float32,
        )
        inner = jnp.sum(weight_grads * weights, axis=-1, keepdims=True)
        score_grads = (weights * (weight_grads - inner)).astype(jnp.bfloat16)
        query_grads.append(
            jnp.einsum(
                "hqk,khd->qhd",
                score_grads,
                keys_all[:, head_start:head_stop],
                preferred_element_type=jnp.float32,
            )
            * score_scale
        )
        key_grads.append(
            jnp.einsum(
                "hqk,qhd->khd",
                score_grads,
                queries[:, head_start:head_stop],
                preferred_element_type=jnp.float32,
            )
            * score_scale
        )
        key_placed = jnp.einsum(
            "hqk,kb->hqb", score_grads, place_onehot, preferred_element_type=jnp.float32
        )
        pair_grid = jnp.einsum(
            "qa,hqb->hab", place_onehot_float, key_placed, precision=lax.Precision.HIGHEST
        )
        table_grads.append(pair_grid.reshape(head_group_size, image_tokens * image_tokens))
    stacked = jnp.stack(
        [
            jnp.concatenate(query_grads, axis=1),
            jnp.concatenate(key_grads, axis=1),
            jnp.concatenate(value_grads, axis=1),
        ],
        axis=1,
    )
    return (
        stacked.reshape(upstream.shape[0], -1).astype(jnp.bfloat16),
        jnp.concatenate(table_grads, axis=0),
    )


def shards(
    tokens,
    condition,
    segments,
    positions,
    buckets,
    modulator,
    modulator_bias,
    projector,
    projector_bias,
    position_table,
    output_weight,
    output_bias,
    up_weight,
    up_bias,
    down_weight,
    down_bias,
    cotangent,
):
    full_set = (
        lax.all_gather(modulator, "dp", axis=0, tiled=True),
        lax.all_gather(projector, "dp", axis=0, tiled=True),
        lax.all_gather(output_weight, "dp", axis=0, tiled=True),
        lax.all_gather(up_weight, "dp", axis=0, tiled=True),
        lax.all_gather(down_weight, "dp", axis=0, tiled=True),
        lax.all_gather(modulator_bias, "dp", axis=0, tiled=True),
        lax.all_gather(projector_bias, "dp", axis=0, tiled=True),
        lax.all_gather(output_bias, "dp", axis=0, tiled=True),
        lax.all_gather(up_bias, "dp", axis=0, tiled=True),
        lax.all_gather(down_bias, "dp", axis=0, tiled=True),
    )
    modulator_all, projector_all, output_all, up_all, down_all = (
        full_set[0],
        full_set[1],
        full_set[2],
        full_set[3],
        full_set[4],
    )
    modulator_bias_all, projector_bias_all, output_bias_all, up_bias_all, down_bias_all = (
        full_set[5],
        full_set[6],
        full_set[7],
        full_set[8],
        full_set[9],
    )
    image_tokens = buckets.shape[0]
    head_count = position_table.shape[0]
    model_width = tokens.shape[2]
    token_count = tokens.shape[1]
    pack_rows = 2 * image_tokens
    pack_count = token_count // pack_rows
    image_count = condition.shape[1]
    inputs = tokens[0].astype(jnp.float32)
    slot_ids = segments[0]
    places = positions[0]
    condition_float = condition[0].astype(jnp.float32)
    silu_value, silu_back = jax.vjp(jax.nn.silu, condition_float)
    activated = silu_value.astype(jnp.bfloat16)
    modulation = jnp.dot(
        activated, modulator_all, preferred_element_type=jnp.float32
    ) + modulator_bias_all.astype(jnp.float32)
    per_pack = modulation.reshape(pack_count, 3, 6 * model_width)
    local_slot = slot_ids.reshape(pack_count, pack_rows, 1)
    per_token = jnp.where(
        local_slot == 0,
        per_pack[:, 0:1],
        jnp.where(local_slot == 1, per_pack[:, 1:2], per_pack[:, 2:3]),
    ).reshape(token_count, 6 * model_width)
    shift_attn, scale_attn, gate_attn, shift_mlp, scale_mlp, gate_mlp = jnp.split(
        per_token, 6, axis=1
    )
    normed_one, inverse_one = normalize(inputs)
    hidden_one = (normed_one * (1.0 + scale_attn) + shift_attn).astype(jnp.bfloat16)
    projector_bias_full = jnp.concatenate(
        [
            projector_bias_all[:model_width],
            jnp.zeros((model_width,), jnp.bfloat16),
            projector_bias_all[model_width:],
        ]
    ).astype(jnp.float32)
    packed = (
        jnp.dot(hidden_one, projector_all, preferred_element_type=jnp.float32) + projector_bias_full
    ).astype(jnp.bfloat16)
    pos_grid = jnp.take(position_table.astype(jnp.float32), buckets.reshape(-1), axis=1).reshape(
        head_count, image_tokens, image_tokens
    )
    packed_blocks = packed.reshape(pack_count, pack_rows, 3 * model_width)
    slot_blocks = slot_ids.reshape(pack_count, pack_rows)
    place_blocks = places.reshape(pack_count, pack_rows)

    def forward_pack(item_set):
        return attend_pack(
            pos_grid, head_count, image_tokens, item_set[0], item_set[1], item_set[2]
        )

    mixture, log_totals = lax.map(forward_pack, (packed_blocks, slot_blocks, place_blocks))
    attended = mixture.reshape(token_count, model_width).astype(jnp.bfloat16)
    branch_attn = jnp.dot(
        attended, output_all, preferred_element_type=jnp.float32
    ) + output_bias_all.astype(jnp.float32)
    middle = inputs + gate_attn * branch_attn
    normed_two, inverse_two = normalize(middle)
    hidden_two = (normed_two * (1.0 + scale_mlp) + shift_mlp).astype(jnp.bfloat16)
    up_output = jnp.dot(
        hidden_two, up_all, preferred_element_type=jnp.float32
    ) + up_bias_all.astype(jnp.float32)
    activation, gelu_back = jax.vjp(smooth_gelu, up_output)
    activation_low = activation.astype(jnp.bfloat16)
    branch_mlp = jnp.dot(
        activation_low, down_all, preferred_element_type=jnp.float32
    ) + down_bias_all.astype(jnp.float32)
    result = (middle + gate_mlp * branch_mlp).astype(jnp.bfloat16)
    modulator_use, projector_use, output_use, up_use, down_use = (
        modulator_all,
        projector_all,
        output_all,
        up_all,
        down_all,
    )
    upstream = cotangent[0].astype(jnp.float32)
    mlp_grad = (gate_mlp * upstream).astype(jnp.bfloat16)
    gate_mlp_grad = branch_mlp * upstream
    down_grad = jnp.einsum(
        "tf,td->fd", activation_low, mlp_grad, preferred_element_type=jnp.float32
    )
    down_bias_grad = jnp.sum(mlp_grad.astype(jnp.float32), axis=0)
    activation_grad = jnp.einsum(
        "td,fd->tf", mlp_grad, down_use, preferred_element_type=jnp.float32
    )
    up_grad_low = gelu_back(activation_grad)[0].astype(jnp.bfloat16)
    up_grad = jnp.einsum("td,tf->df", hidden_two, up_grad_low, preferred_element_type=jnp.float32)
    up_bias_grad = jnp.sum(up_grad_low.astype(jnp.float32), axis=0)
    hidden_two_grad = jnp.einsum(
        "tf,df->td", up_grad_low, up_use, preferred_element_type=jnp.float32
    )
    scale_mlp_grad = hidden_two_grad * normed_two
    middle_grad = upstream + normalize_back(
        normed_two, inverse_two, hidden_two_grad * (1.0 + scale_mlp)
    )
    attn_grad = (gate_attn * middle_grad).astype(jnp.bfloat16)
    gate_attn_grad = branch_attn * middle_grad
    output_grad = jnp.einsum("td,te->de", attended, attn_grad, preferred_element_type=jnp.float32)
    output_bias_grad = jnp.sum(attn_grad.astype(jnp.float32), axis=0)
    attended_grad = jnp.einsum(
        "te,de->td", attn_grad, output_use, preferred_element_type=jnp.float32
    ).astype(jnp.bfloat16)

    def backward_pack(running, item_set):
        packed_part, table_part = attend_back(
            pos_grid,
            head_count,
            image_tokens,
            item_set[0],
            item_set[1],
            item_set[2],
            item_set[3],
            item_set[4],
        )
        return (running + table_part, packed_part)

    grid_grad, packed_grads = lax.scan(
        backward_pack,
        jnp.zeros((head_count, image_tokens * image_tokens), jnp.float32),
        (
            packed_blocks,
            slot_blocks,
            place_blocks,
            log_totals,
            attended_grad.reshape(pack_count, pack_rows, model_width),
        ),
    )
    packed_grad = packed_grads.reshape(token_count, 3 * model_width)
    projector_grad = jnp.einsum(
        "td,te->de", hidden_one, packed_grad, preferred_element_type=jnp.float32
    )
    packed_sums = jnp.sum(packed_grad.astype(jnp.float32), axis=0)
    projector_bias_grad = jnp.concatenate(
        [packed_sums[:model_width], packed_sums[2 * model_width :]]
    )
    hidden_one_grad = jnp.einsum(
        "te,de->td", packed_grad, projector_use, preferred_element_type=jnp.float32
    )
    inputs_grad = middle_grad + normalize_back(
        normed_one, inverse_one, hidden_one_grad * (1.0 + scale_attn)
    )
    token_mod_grad = jnp.concatenate(
        [
            hidden_one_grad,
            hidden_one_grad * normed_one,
            gate_attn_grad,
            hidden_two_grad,
            scale_mlp_grad,
            gate_mlp_grad,
        ],
        axis=1,
    )
    selector = (local_slot == jnp.arange(3, dtype=jnp.int32)[None, None, :]).astype(jnp.float32)
    modulation_grad = (
        jnp.einsum(
            "prk,pre->pke",
            selector,
            token_mod_grad.reshape(pack_count, pack_rows, 6 * model_width),
            precision=lax.Precision.HIGHEST,
        )
        .reshape(image_count, 6 * model_width)
        .astype(jnp.bfloat16)
    )
    activated_grad = jnp.einsum(
        "ie,de->id", modulation_grad, modulator_use, preferred_element_type=jnp.float32
    )
    condition_grad = silu_back(activated_grad)[0]
    table_grad = jax.vmap(
        lambda grid_row: jax.ops.segment_sum(
            grid_row, buckets.reshape(-1), num_segments=position_table.shape[1]
        )
    )(grid_grad)
    table_total = lax.psum(table_grad, ("stream", "dp"))
    modulator_grad = jnp.einsum(
        "id,ie->de", activated, modulation_grad, preferred_element_type=jnp.float32
    )
    modulator_bias_grad = jnp.sum(modulation_grad.astype(jnp.float32), axis=0)
    shard_set = (
        lax.psum_scatter(modulator_grad, "dp", scatter_dimension=0, tiled=True),
        lax.psum_scatter(projector_grad, "dp", scatter_dimension=0, tiled=True),
        lax.psum_scatter(output_grad, "dp", scatter_dimension=0, tiled=True),
        lax.psum_scatter(up_grad, "dp", scatter_dimension=0, tiled=True),
        lax.psum_scatter(down_grad, "dp", scatter_dimension=0, tiled=True),
        lax.psum_scatter(modulator_bias_grad, "dp", scatter_dimension=0, tiled=True),
        lax.psum_scatter(projector_bias_grad, "dp", scatter_dimension=0, tiled=True),
        lax.psum_scatter(output_bias_grad, "dp", scatter_dimension=0, tiled=True),
        lax.psum_scatter(up_bias_grad, "dp", scatter_dimension=0, tiled=True),
        lax.psum_scatter(down_bias_grad, "dp", scatter_dimension=0, tiled=True),
    )
    final_set = (
        lax.psum(shard_set[0].astype(jnp.bfloat16), "stream").astype(jnp.float32),
        lax.psum(shard_set[1].astype(jnp.bfloat16), "stream").astype(jnp.float32),
        lax.psum(shard_set[2].astype(jnp.bfloat16), "stream").astype(jnp.float32),
        lax.psum(shard_set[3].astype(jnp.bfloat16), "stream").astype(jnp.float32),
        lax.psum(shard_set[4].astype(jnp.bfloat16), "stream").astype(jnp.float32),
        lax.psum(shard_set[5].astype(jnp.bfloat16), "stream").astype(jnp.float32),
        lax.psum(shard_set[6].astype(jnp.bfloat16), "stream").astype(jnp.float32),
        lax.psum(shard_set[7].astype(jnp.bfloat16), "stream").astype(jnp.float32),
        lax.psum(shard_set[8].astype(jnp.bfloat16), "stream").astype(jnp.float32),
        lax.psum(shard_set[9].astype(jnp.bfloat16), "stream").astype(jnp.float32),
    )
    return (
        result[None],
        inputs_grad[None],
        condition_grad[None],
        final_set[0],
        final_set[5],
        final_set[1],
        final_set[6],
        table_total,
        final_set[2],
        final_set[7],
        final_set[3],
        final_set[8],
        final_set[4],
        final_set[9],
    )


def solution(mesh):
    in_specs = (
        P("stream", "dp", None),
        P("stream", "dp", None),
        P("stream", "dp"),
        P("stream", "dp"),
        P(),
        P("dp", None),
        P("dp"),
        P("dp", None),
        P("dp"),
        P(),
        P("dp", None),
        P("dp"),
        P("dp", None),
        P("dp"),
        P("dp", None),
        P("dp"),
        P("stream", "dp", None),
    )
    out_specs = (
        P("stream", "dp", None),
        P("stream", "dp", None),
        P("stream", "dp", None),
        P("dp", None),
        P("dp"),
        P("dp", None),
        P("dp"),
        P(),
        P("dp", None),
        P("dp"),
        P("dp", None),
        P("dp"),
        P("dp", None),
        P("dp"),
    )
    return jax.shard_map(shards, mesh=mesh, in_specs=in_specs, out_specs=out_specs, check_vma=False)
```

profile of v0, /device:TPU:9, one launch (start us, length us, event | category | flops | bytes accessed | tf_op | source)
XLA Modules:
  0.0 2197.6 jit_solution(9128455956056867481)
XLA Ops:
  15.2 50.7 %all-reduce.13 = (bf16[6912]{0:T(1024)(128)(2,1)S(1)}, bf16[2304]{0:T(1024)(128)(2,1)S(1)}, bf16[1152]{0:T(1024)(128)(2,1)S(1)}, bf16[1152]{0:T(1024)(128)(2,1)S(1)}, bf16[4608]{0:T(1024)(128)(2,1)S(1)}) all-reduce(bf16[6912]{0:T(1024)(128)(2,1)S(1)} %dynamic-update-slice, ...), channel_id=1, replica_groups=mesh['stream'=2,'dp'=16] {'dp'}, use_global_device_ids=true, to_apply=%add | all-reduce | flops 16128 | bytes 64512
  68.2 215.9 %gather_fusion = f32[65536,16]{1,0:T(8,128)} fusion(f32[16,961]{0,1:T(8,128)S(1)} %copy.122, s32[65536]{0:T(1024)S(1)} %broadcast_clamp_fusion), kind=kCustom, calls=%fused_computation | custom fusion | bytes 8650752 | tf_op jit(solution)/shard_map/jit(_take)/gather | solution.py:248
  284.2 35.6 %select_bitcast_fusion = f32[16,65536]{0,1:T(8,128)} fusion(f32[65536,16]{1,0:T(8,128)} %gather_fusion, pred[65536]{0:T(1024)(128)(4,1)S(1)} %compare_and_fusion), kind=kLoop, calls=%fused_computation.2 | loop fusion | flops 1048576 | bytes 8454144 | tf_op jit(solution)/shard_map/jit(_take)/select_n | solution.py:248
  319.8 94.1 %fusion.176 = (f32[4,65536]{0,1:T(8,128)}, f32[4,65536]{0,1:T(8,128)}, f32[4,65536]{0,1:T(8,128)}, f32[4,65536]{0,1:T(8,128)}) fusion(f32[16,65536]{0,1:T(8,128)} %select_bitcast_fusion), kind=kLoop, calls=%fused_computation.258 | loop fusion | bytes 8388608 | tf_op jit(solution)/shard_map/while/body/eval_jaxpr/slice | solution.py:64
  413.9 19.2 copy.176
  433.1 18.9 copy.173
  452.0 19.6 copy.170
  471.6 20.2 copy.167
  583.8 11.7 fusion.184
  595.5 16.5 convert_reduce_fusion
  612.0 13.0 fusion.169
  625.1 14.1 convolution_add_fusion.1
  702.5 12.3 fusion.187
  716.0 14.2 fusion.171
  731.6 12.0 fusion.170
  764.5 17.6 fusion.162
  810.8 120.0 %reduce-scatter.16.cloned.1.call-done = f32[72,3456]{1,0:T(8,128)} async-done(((f32[1152,3456]{1,0:T(8,128)}), f32[72,3456]{1,0:T(8,128)}) %reduce-scatter.16.cloned.1.call-update) | async-done | bytes 995344
  932.8 214.1 %reduce-scatter.12.cloned.1.call-done = f32[72,4608]{1,0:T(8,128)} async-done(((f32[1152,4608]{1,0:T(8,128)}), f32[72,4608]{1,0:T(8,128)}) %reduce-scatter.12.cloned.1.call-update) | async-done | bytes 1327120 | tf_op jit(solution)/shard_map/reduce_scatter | solution.py:390
  1149.2 214.4 %reduce-scatter.14.cloned.1.call-done = f32[288,1152]{1,0:T(8,128)} async-done(((f32[4608,1152]{1,0:T(8,128)}), f32[288,1152]{1,0:T(8,128)}) %reduce-scatter.14.cloned.1.call-update) | async-done | bytes 1327120 | tf_op jit(solution)/shard_map/reduce_scatter | solution.py:391
  1365.7 321.6 %reduce-scatter.10.cloned.1.call-done = f32[72,6912]{1,0:T(8,128)} async-done(((f32[1152,6912]{1,0:T(8,128)}), f32[72,6912]{1,0:T(8,128)}) %reduce-scatter.10.cloned.1.call-update) | async-done | bytes 1990672 | tf_op jit(solution)/shard_map/reduce_scatter | solution.py:387
  1706.0 49.8 %all-reduce.12 = (bf16[6912]{0:T(1024)(128)(2,1)S(1)}, bf16[2304]{0:T(1024)(128)(2,1)S(1)}, bf16[1152]{0:T(1024)(128)(2,1)S(1)}, bf16[4608]{0:T(1024)(128)(2,1)S(1)}, bf16[1152]{0:T(1024)(128)(2,1)S(1)}) all-reduce(f32[6912]{0:T(1024)S(1)} %get-tuple-element.194, ...), channel_id=3, replica_groups=mesh['stream'=2,'dp'=16] {'dp'}, use_global_device_ids=true, to_apply=%region_23.24.clone | all-reduce | flops 16128 | bytes 96768
  1761.6 16.8 copy.164
  1778.4 347.5 %scatter_custom_fusion = f32[16,961]{0,1:T(8,128)S(1)} fusion(s32[65536]{0:T(1024)} %bitcast.328, f32[65536,16]{1,0:T(8,128)} %copy.164, f32[]{:T(128)} %constant.59.clone.1), kind=kCustom, calls=%fused_computation.201 | custom fusion | flops 1048576 | bytes 62016 | tf_op jit(solution)/shard_map/vmap()/scatter-add | solution.py:377
  2125.9 55.7 %psum.81 = f32[16,961]{0,1:T(8,128)S(1)} all-reduce(f32[16,961]{0,1:T(8,128)S(1)} %scatter_custom_fusion), channel_id=1, replica_groups=mesh['stream'=2,'dp'=16] {'stream','dp'}, use_global_device_ids=true, to_apply=%region_31.32 | all-reduce | flops 15376 | bytes 123008 | tf_op jit(solution)/shard_map/psum | solution.py:381
  (402 shorter events, 250.9 us)
Async XLA Ops:
  7.2 59.3 %copy-start.89 = (bf16[16,961]{1,0:T(8,128)(2,1)S(1)}, bf16[16,961]{1,0:T(8,128)(2,1)}, u32[]{:S(2)}) copy-start(bf16[16,961]{1,0:T(8,128)(2,1)} %param.26) | copy-start | bytes 92260
  7.3 59.4 %copy-start.54 = (s32[256,256]{1,0:T(8,128)S(1)}, s32[256,256]{1,0:T(8,128)}, u32[]{:S(2)}) copy-start(s32[256,256]{1,0:T(8,128)} %param.21) | copy-start | bytes 786436
  7.3 500.3 %all-gather.6.cloned.1.call-start = ((), (), s32[]{:S(2)}) async-start(), calls=%async_computation.5 | async-start | bytes 16920576 | tf_op jit(solution)/shard_map/all_gather | solution.py:185
  8.0 516.5 %all-gather.8.cloned.1.call-start = ((), (), s32[]{:S(2)}) async-start(), calls=%async_computation.6 | async-start | bytes 8460288 | tf_op jit(solution)/shard_map/all_gather | solution.py:186
  8.7 560.7 %all-gather.10.cloned.1.call-start = ((), (), s32[]{:S(2)}) async-start(), calls=%async_computation.7 | async-start | bytes 2820096 | tf_op jit(solution)/shard_map/all_gather | solution.py:187
  9.5 574.3 %all-gather.12.cloned.1.call-start = ((), (), s32[]{:S(2)}) async-start(), calls=%async_computation.8 | async-start | bytes 11280384 | tf_op jit(solution)/shard_map/all_gather | solution.py:188
  10.1 585.5 %all-gather.14.cloned.1.call-start = ((), (), s32[]{:S(2)}) async-start(), calls=%async_computation.9 | async-start | bytes 11280384 | tf_op jit(solution)/shard_map/all_gather | solution.py:189
  10.6 798.5 %reduce-scatter.18.cloned.1.call-start = ((), (), s32[]{:S(2)}) async-start(), calls=%async_computation.14 | async-start | bytes 5640192
  471.6 21.4 copy-start.14
  471.6 22.1 %copy-start.78 = (s32[1,512]{1,0:T(1,128)S(1)}, s32[1,512]{1,0:T(1,128)}, u32[]{:S(2)}) copy-start(s32[1,512]{1,0:T(1,128)} %param.19) | copy-start | bytes 6148
  493.3 25.6 %copy-start.91 = (f32[512]{0:T(512)}, f32[512]{0:T(512)S(1)}, u32[]{:S(2)}) copy-start(f32[512]{0:T(512)S(1)} %broadcast_multiply_fusion.5) | copy-start | bytes 6148
  493.8 25.1 %copy-start.98 = (f32[512]{0:T(512)}, f32[512]{0:T(512)S(1)}, u32[]{:S(2)}) copy-start(f32[512]{0:T(512)S(1)} %add_rsqrt_fusion.1) | copy-start | bytes 6148
  539.4 28.0 %copy-start.12 = (bf16[512,3456]{0,1:T(8,128)(2,1)}, bf16[512,3456]{0,1:T(8,128)(2,1)S(1)}, u32[]{:S(2)}) copy-start(bf16[512,3456]{0,1:T(8,128)(2,1)S(1)} %copy.121) | copy-start | bytes 10616836
  545.7 19.1 copy-start.9
  546.3 18.5 copy-start.81
  595.5 16.5 copy-start.94
  667.5 263.2 %reduce-scatter.16.cloned.1.call-start = ((), (), s32[]{:S(2)}) async-start(), calls=%async_computation.13 | async-start | bytes 16920576
  701.2 445.6 %reduce-scatter.12.cloned.1.call-start = ((), (), s32[]{:S(2)}) async-start(), calls=%async_computation.11 | async-start | bytes 22560768 | tf_op jit(solution)/shard_map/reduce_scatter | solution.py:390
  714.8 648.7 %reduce-scatter.14.cloned.1.call-start = ((), (), s32[]{:S(2)}) async-start(), calls=%async_computation.12 | async-start | bytes 22560768 | tf_op jit(solution)/shard_map/reduce_scatter | solution.py:391
  730.3 957.0 %reduce-scatter.10.cloned.1.call-start = ((), (), s32[]{:S(2)}) async-start(), calls=%async_computation.10 | async-start | bytes 33841152 | tf_op jit(solution)/shard_map/reduce_scatter | solution.py:387
  782.1 1402.0 %all-reduce.18.cloned.1.call-start = ((), (), s32[]{:S(2)}) async-start(), calls=%async_computation.15 | async-start | bytes 5971968 | tf_op jit(solution)/shard_map/psum | solution.py:399
  1365.7 324.4 %copy-start.45 = (f32[1,4,256,256]{3,1,2,0:T(4,128)S(1)}, f32[1,4,256,256]{3,1,2,0:T(4,128)}, u32[]{:S(2)}) copy-start(f32[1,4,256,256]{3,1,2,0:T(4,128)} %copy.216) | copy-start | bytes 3145732
  1365.7 324.4 %copy-start.46 = (f32[1,4,256,256]{3,1,2,0:T(4,128)S(1)}, f32[1,4,256,256]{3,1,2,0:T(4,128)}, u32[]{:S(2)}) copy-start(f32[1,4,256,256]{3,1,2,0:T(4,128)} %copy.215) | copy-start | bytes 3145732
  1365.7 324.4 %copy-start.47 = (f32[1,4,256,256]{3,1,2,0:T(4,128)S(1)}, f32[1,4,256,256]{3,1,2,0:T(4,128)}, u32[]{:S(2)}) copy-start(f32[1,4,256,256]{3,1,2,0:T(4,128)} %copy.214) | copy-start | bytes 3145732
  (98 other events, 555.0 us)
Sparse Core Ops, SparseCore 0:
  10.3 122.0 all-gather.5
  134.5 71.7 all-gather.7
  208.4 41.9 all-gather.9
  252.5 86.4 all-gather.11
  341.2 86.8 all-gather.13
  667.6 88.0 reduce-scatter.17
  759.8 170.8 reduce-scatter.15
  934.9 211.9 reduce-scatter.11
  1151.5 211.9 reduce-scatter.13
  1367.6 319.6 reduce-scatter.9
  1691.1 83.9 all-reduce.17
where the time goes:
time: 2210 us; the launch traced here: 2200 us
  waiting for transfers between devices  873 us (40%)
  local copies, waits for them, and re-layouts  456 us (21%)
  other arithmetic  448 us (20%)
  matrix products  237 us (11%)
  blocking collectives  160 us (7%)
    scatter-add x1, other arithmetic, shards(): jax.ops.segment_sum(grid_row, buckets.reshape(-1), num_segments=position_...  347 us
    reduce_scatter x1, waiting for transfers between devices, shards(): lax.psum_scatter(modulator_grad, 'dp', scatter_dimension=0, tiled=True)  322 us
    gather x1, local copies, waits for them, and re-layouts, shards(): jnp.take(position_table.astype(jnp.float32), buckets.reshape(-1), axis=1)  216 us
    reduce_scatter x1, waiting for transfers between devices, shards(): lax.psum_scatter(down_grad, 'dp', scatter_dimension=0, tiled=True)  214 us
    reduce_scatter x1, waiting for transfers between devices, shards(): lax.psum_scatter(up_grad, 'dp', scatter_dimension=0, tiled=True)  214 us
    slice x5, local copies, waits for them, and re-layouts, attend_pack(): pos_grid[head_start:head_stop]  172 us
    unnamed x13, waiting for transfers between devices  123 us
    unnamed x2, blocking collectives  101 us
  transfers between devices with their start and end apart: 11, of which 4 were waited for; matrix products, arithmetic and copies ran while one was open for 47% of the time, Pallas kernels for 0%

commit v1 on v0

v1 whole, which is shorter than its diff:
```python
import functools

import jax
import jax.numpy as jnp
from jax import lax
from jax.experimental import pallas as pl
from jax.experimental.pallas import tpu as pltpu
from jax.sharding import PartitionSpec as P

norm_epsilon = 1e-06
masked_score=-1000000000.0

def grid_kernel(table_ref, buckets_ref, grid_ref):
    chunks = table_ref.shape[1]
    for half in range(buckets_ref.shape[1] // 128):
        span = slice(128 * half, 128 * half + 128)
        index = buckets_ref[:, span]
        low, high = index & 127, index >> 7
        total = jnp.zeros(index.shape, jnp.float32)
        for chunk in range(chunks):
            row = jnp.broadcast_to(table_ref[0, chunk : chunk + 1], index.shape)
            found = jnp.take_along_axis(row, low, axis=1)
            total = jnp.where(high == chunk, found, total)
        grid_ref[0, :, span] = total.astype(jnp.bfloat16)

def bias_grid(table, buckets):
    heads, count = table.shape
    chunks = -(-count // 128)
    wide = jnp.pad(table.astype(jnp.float32), ((0, 0), (0, chunks * 128 - count)))
    return pl.pallas_call(
        grid_kernel,
        grid=(heads,),
        in_specs=[pl.BlockSpec((1, chunks, 128), lambda h: (h, 0, 0)),
                  pl.BlockSpec(buckets.shape, lambda h: (0, 0))],
        out_specs=pl.BlockSpec((1,) + buckets.shape, lambda h: (h, 0, 0)),
        out_shape=jax.ShapeDtypeStruct((heads,) + buckets.shape, jnp.bfloat16),
    )(wide.reshape(heads, chunks, 128), buckets)

def hist_kernel(grad_ref, buckets_ref, out_ref):
    rows, heads, width = grad_ref.shape
    chunks = out_ref.shape[0] // heads
    @pl.when(pl.program_id(0) == 0)
    def _():
        out_ref[...] = jnp.zeros_like(out_ref)
    total = out_ref[...]
    for row in range(rows):
        index = buckets_ref[row : row + 1, :]
        low, high = index & 127, index >> 7
        mask = lax.broadcasted_iota(jnp.int32, (chunks, width), 0) == high
        values = jnp.where(mask[None], grad_ref[row][:, None, :], 0.0)
        left = values.reshape(heads * chunks, width).astype(jnp.bfloat16)
        right = (lax.broadcasted_iota(jnp.int32, (128, width), 0) == low).astype(jnp.float32).astype(jnp.bfloat16)
        total += lax.dot_general(left, right, (((1,), (1,)), ((), ())), preferred_element_type=jnp.float32)
    out_ref[...] = total

def table_histogram(grad, buckets, count):
    places, heads, width = grad.shape
    chunks = -(-count // 128)
    step = 16
    out = pl.pallas_call(
        hist_kernel,
        grid=(places // step,),
        in_specs=[pl.BlockSpec((step, heads, width), lambda a: (a, 0, 0)),
                  pl.BlockSpec((step, width), lambda a: (a, 0))],
        out_specs=pl.BlockSpec((heads * chunks, 128), lambda a: (0, 0)),
        out_shape=jax.ShapeDtypeStruct((heads * chunks, 128), jnp.float32),
    )(grad, buckets)
    return out.reshape(heads, chunks * 128)[:, :count]

def head_windows(heads, head_width):
    found = []
    for head in range(heads):
        start = head * head_width
        base = start // 128 * 128
        stop = -(-(start + head_width) // 128) * 128
        found.append((base, stop - base, start - base))
    return found

def lane_mask(rows, width, offset, head_width):
    lane = lax.broadcasted_iota(jnp.int32, (rows, width), 1)
    return (lane >= offset) & (lane < offset + head_width)

def nt(left, right):
    return lax.dot_general(left, right, (((1,), (1,)), ((), ())), preferred_element_type=jnp.float32)
def tn(left, right):
    return lax.dot_general(left, right, (((0,), (0,)), ((), ())), preferred_element_type=jnp.float32)
def nn(left, right):
    return lax.dot_general(left, right, (((1,), (0,)), ((), ())), preferred_element_type=jnp.float32)

def attend_forward_kernel(heads, packed_ref, frame_row_ref, frame_column_ref, grid_ref, attended_ref, placed_ref, weights_ref, mixed_ref):
    rows, width3 = packed_ref.shape
    frames = placed_ref.shape[0]
    places = grid_ref.shape[1]
    width = width3 // 3
    head_width = width // heads
    scale = head_width ** (-0.5)
    place = (lax.broadcasted_iota(jnp.int32, (frames, rows), 0) == frame_row_ref[...]).astype(jnp.float32).astype(jnp.bfloat16)
    for part in range(3):
        span = slice(part * width, part * width + width)
        placed_ref[:, span] = nn(place, packed_ref[:, span]).astype(jnp.bfloat16)
    filled = nt(jnp.ones((8, rows), jnp.bfloat16), place)[0:1] > 0.5
    filled_f = jnp.where(filled, 0.0, masked_score)
    mixed_ref[...] = jnp.zeros_like(mixed_ref)
    for image in range(frames // places):
        span_rows = slice(image * places, image * places + places)
        offset_row = filled_f[:, span_rows]
        for head, (base, wide, offset) in enumerate(head_windows(heads, head_width)):
            mask = lane_mask(places, wide, offset, head_width)
            query = placed_ref[span_rows, base : base + wide]
            key = placed_ref[span_rows, width + base : width + base + wide]
            value = placed_ref[span_rows, 2 * width + base : 2 * width + base + wide]
            query = jnp.where(mask, query, jnp.zeros_like(query))
            scores = nt(query, key) * scale + grid_ref[head].astype(jnp.float32)
            scores = jnp.where(offset_row < 0.0, masked_score, scores)
            exponent = jnp.exp(scores - jnp.max(scores, axis=-1, keepdims=True))
            weights = (exponent / jnp.sum(exponent, axis=-1, keepdims=True)).astype(jnp.bfloat16)
            weights_ref[image, head] = weights
            mixture = nn(weights, value).astype(jnp.bfloat16)
            before = mixed_ref[span_rows, base : base + wide]
            mixed_ref[span_rows, base : base + wide] = jnp.where(mask, mixture, before)
    back = (lax.broadcasted_iota(jnp.int32, (rows, frames), 1) == frame_column_ref[...]).astype(jnp.float32).astype(jnp.bfloat16)
    attended_ref[...] = nn(back, mixed_ref[...]).astype(jnp.bfloat16)

def attend_forward(packed, slots, places, grid):
    rows = packed.shape[0]
    heads, image, _ = grid.shape
    frame = slots * image + places
    frames = 3 * image
    width = packed.shape[1] // 3
    return pl.pallas_call(
        functools.partial(attend_forward_kernel, heads),
        out_shape=(jax.ShapeDtypeStruct((rows, width), jnp.bfloat16),
                   jax.ShapeDtypeStruct((frames, 3 * width), jnp.bfloat16),
                   jax.ShapeDtypeStruct((3, heads, image, image), jnp.bfloat16)),
        scratch_shapes=[pltpu.VMEM((frames, width), jnp.bfloat16)],
        compiler_params=pltpu.CompilerParams(vmem_limit_bytes=48 * 2**20),
    )(packed, frame[None, :], frame[:, None], grid)

def attend_backward_kernel(heads, placed_ref, weights_ref, upstream_ref, frame_row_ref, frame_column_ref, packed_grad_ref, grid_grad_ref, up_ref, grad_ref, bias_ref):
    frames, width3 = placed_ref.shape
    rows = upstream_ref.shape[0]
    places = weights_ref.shape[2]
    width = width3 // 3
    head_width = width // heads
    scale = head_width ** (-0.5)
    place = (lax.broadcasted_iota(jnp.int32, (frames, rows), 0) == frame_row_ref[...]).astype(jnp.float32).astype(jnp.bfloat16)
    up_ref[...] = nn(place, upstream_ref[...]).astype(jnp.bfloat16)
    grad_ref[...] = jnp.zeros_like(grad_ref)
    for head, (base, wide, offset) in enumerate(head_windows(heads, head_width)):
        mask = lane_mask(places, wide, offset, head_width)
        for image in range(frames // places):
            span_rows = slice(image * places, image * places + places)
            spans = [slice(part * width + base, part * width + base + wide) for part in range(3)]
            query, key = [jnp.where(mask, t, jnp.zeros_like(t)) for t in (placed_ref[span_rows, spans[0]], placed_ref[span_rows, spans[1]])]
            value = placed_ref[span_rows, spans[2]]
            upstream = up_ref[span_rows, spans[0]]
            upstream = jnp.where(mask, upstream, jnp.zeros_like(upstream))
            weights = weights_ref[image, head]
            weights_f = weights.astype(jnp.float32)
            weight_grads = nt(upstream, value)
            inner = jnp.sum(weight_grads * weights_f, axis=-1, keepdims=True)
            score_grads_f = weights_f * (weight_grads - inner)
            score_grads = score_grads_f.astype(jnp.bfloat16)
            if image == 0:
                bias_ref[...] = score_grads_f
            else:
                bias_ref[...] += score_grads_f
            grad_ref[span_rows, spans[0]] += (nn(score_grads, key) * scale).astype(jnp.bfloat16)
            grad_ref[span_rows, spans[1]] += (tn(score_grads, query) * scale).astype(jnp.bfloat16)
            grad_ref[span_rows, spans[2]] += tn(weights, upstream).astype(jnp.bfloat16)
        grid_grad_ref[:, head, :] = bias_ref[...]
    back = (lax.broadcasted_iota(jnp.int32, (rows, frames), 1) == frame_column_ref[...]).astype(jnp.float32).astype(jnp.bfloat16)
    for part in range(3):
        span = slice(part * width, part * width + width)
        packed_grad_ref[:, span] = nn(back, grad_ref[:, span]).astype(jnp.bfloat16)

def attend_backward(placed, weights, upstream, slots, places):
    rows, width = upstream.shape
    _, heads, image, _ = weights.shape
    frame = slots * image + places
    frames = 3 * image
    return pl.pallas_call(
        functools.partial(attend_backward_kernel, heads),
        out_shape=(jax.ShapeDtypeStruct((rows, 3 * width), jnp.bfloat16),
                   jax.ShapeDtypeStruct((image, heads, image), jnp.float32)),
        scratch_shapes=[pltpu.VMEM((frames, width), jnp.bfloat16),
                        pltpu.VMEM((frames, 3 * width), jnp.bfloat16),
                        pltpu.VMEM((image, image), jnp.float32)],
        compiler_params=pltpu.CompilerParams(vmem_limit_bytes=56 * 2**20),
    )(placed, weights, upstream, frame[None, :], frame[:, None])

def normalize(values):
    center = values - jnp.mean(values, axis=-1, keepdims=True)
    inverse = lax.rsqrt(jnp.mean(center * center, axis=-1, keepdims=True) + norm_epsilon)
    return (center * inverse, inverse)


def normalize_back(normed, inverse, upstream):
    return inverse * (
        upstream
        - jnp.mean(upstream, axis=-1, keepdims=True)
        - normed * jnp.mean(upstream * normed, axis=-1, keepdims=True)
    )


def smooth_gelu(values):
    return jax.nn.gelu(values, approximate=True)


def shards(
    tokens,
    condition,
    segments,
    positions,
    buckets,
    modulator,
    modulator_bias,
    projector,
    projector_bias,
    position_table,
    output_weight,
    output_bias,
    up_weight,
    up_bias,
    down_weight,
    down_bias,
    cotangent,
):
    heads, bucket_count = position_table.shape
    image_tokens = buckets.shape[0]
    rows, model_width = tokens.shape[1], tokens.shape[2]
    images = condition.shape[1]
    shard = modulator.shape[0]
    feed_width = up_weight.shape[1]
    dp_index = lax.axis_index("dp")
    stream_index = lax.axis_index("stream")
    low = jnp.bfloat16
    full = jnp.float32

    def gather(part):
        return lax.all_gather(part, "dp", axis=0, tiled=True)

    inputs = tokens[0].astype(full)
    slot_ids, places = segments[0], positions[0]
    silu_value, silu_back = jax.vjp(jax.nn.silu, condition[0].astype(full))
    activated = silu_value.astype(low)
    activated_both = lax.all_gather(activated, ("stream", "dp"), axis=0, tiled=True)
    slots = activated_both.shape[0]
    activated_own = lax.dynamic_slice(activated_both, (0, dp_index * shard), (slots, shard))
    stream_slots = slots // 2
    partial = jnp.dot(
        lax.dynamic_slice(activated_own, (stream_index * stream_slots, 0), (stream_slots, shard)),
        modulator,
        preferred_element_type=full,
    )
    bias_parts = (modulator_bias, projector_bias, output_bias, up_bias, down_bias)
    bias_all = lax.all_gather(jnp.concatenate(bias_parts), "dp", axis=0)
    bias_full = []
    start = 0
    for part in bias_parts:
        bias_full.append(bias_all[:, start : start + part.shape[0]].reshape(-1).astype(full))
        start += part.shape[0]
    modulation = (
        lax.psum_scatter(partial, "dp", scatter_dimension=0, tiled=True) + bias_full[0]
    )
    projector_all = gather(projector)
    output_all = gather(output_weight)
    up_all = gather(up_weight)
    down_all = gather(down_weight)
    grid = bias_grid(position_table, buckets)
    local = slot_ids[:, None]
    per_token = jnp.where(
        local == 0, modulation[0:1], jnp.where(local == 1, modulation[1:2], modulation[2:3])
    )
    shift_attn, scale_attn, gate_attn, shift_mlp, scale_mlp, gate_mlp = jnp.split(
        per_token, 6, axis=1
    )
    normed_one, inverse_one = normalize(inputs)
    hidden_one = (normed_one * (1.0 + scale_attn) + shift_attn).astype(low)
    packed_bias = jnp.concatenate(
        [bias_full[1][:model_width], jnp.zeros((model_width,), full), bias_full[1][model_width:]]
    )
    packed = (
        jnp.dot(hidden_one, projector_all, preferred_element_type=full) + packed_bias
    ).astype(low)
    attended, placed, weights = attend_forward(packed, slot_ids, places, grid)
    branch_attn = jnp.dot(attended, output_all, preferred_element_type=full) + bias_full[2]
    middle = inputs + gate_attn * branch_attn
    normed_two, inverse_two = normalize(middle)
    hidden_two = (normed_two * (1.0 + scale_mlp) + shift_mlp).astype(low)
    up_output = jnp.dot(hidden_two, up_all, preferred_element_type=full) + bias_full[3]
    activation, gelu_back = jax.vjp(lambda v: jax.nn.gelu(v, approximate=True), up_output)
    activation_low = activation.astype(low)
    branch_mlp = jnp.dot(activation_low, down_all, preferred_element_type=full) + bias_full[4]
    result = (middle + gate_mlp * branch_mlp).astype(low)

    upstream = cotangent[0].astype(full)
    mlp_grad = (gate_mlp * upstream).astype(low)
    gate_mlp_grad = branch_mlp * upstream

    def scatter(grad):
        part = lax.psum_scatter(grad.astype(low), "dp", scatter_dimension=0, tiled=True)
        return lax.psum(part, "stream").astype(full)

    down_grad = scatter(
        jnp.einsum("tf,td->fd", activation_low, mlp_grad, preferred_element_type=full)
    )
    activation_grad = jnp.einsum("td,fd->tf", mlp_grad, down_all, preferred_element_type=full)
    up_grad_low = gelu_back(activation_grad)[0].astype(low)
    up_grad = scatter(
        jnp.einsum("td,tf->df", hidden_two, up_grad_low, preferred_element_type=full)
    )
    hidden_two_grad = jnp.einsum(
        "tf,df->td", up_grad_low, up_all, preferred_element_type=full
    )
    middle_grad = upstream + normalize_back(
        normed_two, inverse_two, hidden_two_grad * (1.0 + scale_mlp)
    )
    attn_grad = (gate_attn * middle_grad).astype(low)
    gate_attn_grad = branch_attn * middle_grad
    output_grad = scatter(
        jnp.einsum("td,te->de", attended, attn_grad, preferred_element_type=full)
    )
    attended_grad = jnp.einsum(
        "te,de->td", attn_grad, output_all, preferred_element_type=full
    ).astype(low)
    packed_grad, grid_grad = attend_backward(placed, weights, attended_grad, slot_ids, places)
    projector_grad = scatter(
        jnp.einsum("td,te->de", hidden_one, packed_grad, preferred_element_type=full)
    )
    table_grad = table_histogram(grid_grad, buckets, bucket_count)
    packed_sums = jnp.sum(packed_grad.astype(full), axis=0)
    sums = (
        table_grad.reshape(-1),
        packed_sums[:model_width],
        packed_sums[2 * model_width :],
        jnp.sum(attn_grad.astype(full), axis=0),
        jnp.sum(up_grad_low.astype(full), axis=0),
        jnp.sum(mlp_grad.astype(full), axis=0),
    )
    small = lax.psum(jnp.concatenate(sums), ("stream", "dp"))
    table_count = heads * bucket_count
    table_total = small[:table_count].reshape(heads, bucket_count)
    bias_grads = []
    start = table_count
    for part in bias_parts[1:]:
        size = part.shape[0]
        bias_grads.append(lax.dynamic_slice(small, (start + dp_index * size,), (size,)))
        start += size * (model_width // shard)
    hidden_one_grad = jnp.einsum(
        "te,de->td", packed_grad, projector_all, preferred_element_type=full
    )
    inputs_grad = middle_grad + normalize_back(
        normed_one, inverse_one, hidden_one_grad * (1.0 + scale_attn)
    )
    token_mod_grad = jnp.concatenate(
        [
            hidden_one_grad,
            hidden_one_grad * normed_one,
            gate_attn_grad,
            hidden_two_grad,
            hidden_two_grad * normed_two,
            gate_mlp_grad,
        ],
        axis=1,
    )
    modulation_grad = jnp.stack(
        [jnp.sum(jnp.where(local == slot, token_mod_grad, 0.0), axis=0) for slot in range(images)]
    ).astype(low)
    modulation_grad_both = lax.all_gather(modulation_grad, ("stream", "dp"), axis=0, tiled=True)
    modulator_grad = jnp.einsum(
        "id,ie->de", activated_own, modulation_grad_both, preferred_element_type=full
    )
    bias_width = modulator_bias.shape[0]
    modulator_bias_grad = jnp.sum(
        lax.dynamic_slice(
            modulation_grad_both, (0, dp_index * bias_width), (slots, bias_width)
        ).astype(full),
        axis=0,
    )
    activated_part = jnp.einsum(
        "ie,de->id",
        lax.dynamic_slice(
            modulation_grad_both, (stream_index * stream_slots, 0), (stream_slots, 6 * model_width)
        ),
        modulator,
        preferred_element_type=full,
    )
    activated_grad = (
        lax.all_to_all(
            activated_part.reshape(-1, images, shard), "dp", split_axis=0, concat_axis=0, tiled=True
        )
        .transpose(1, 0, 2)
        .reshape(images, model_width)
    )
    condition_grad = silu_back(activated_grad)[0]
    return (
        result[None],
        inputs_grad[None],
        condition_grad[None],
        modulator_grad,
        modulator_bias_grad,
        projector_grad,
        bias_grads[0],
        table_total,
        output_grad,
        bias_grads[1],
        up_grad,
        bias_grads[2],
        down_grad,
        bias_grads[3],
    )


def solution(mesh):
    in_specs = (
        P("stream", "dp", None),
        P("stream", "dp", None),
        P("stream", "dp"),
        P("stream", "dp"),
        P(),
        P("dp", None),
        P("dp"),
        P("dp", None),
        P("dp"),
        P(),
        P("dp", None),
        P("dp"),
        P("dp", None),
        P("dp"),
        P("dp", None),
        P("dp"),
        P("stream", "dp", None),
    )
    out_specs = (
        P("stream", "dp", None),
        P("stream", "dp", None),
        P("stream", "dp", None),
        P("dp", None),
        P("dp"),
        P("dp", None),
        P("dp"),
        P(),
        P("dp", None),
        P("dp"),
        P("dp", None),
        P("dp"),
        P("dp", None),
        P("dp"),
    )
    return jax.shard_map(shards, mesh=mesh, in_specs=in_specs, out_specs=out_specs, check_vma=False)
```

time: 2210 us -> 1170 us (0.53)
  local copies, waits for them, and re-layouts: 456 us -> 27.4 us
  other arithmetic: 448 us -> 39.6 us
  matrix products: 237 us -> 129 us
  waiting for transfers between devices: 873 us -> 783 us
  Pallas kernels: 0 us -> 74.4 us
  blocking collectives: 160 us -> 88.9 us
    reduce_scatter x3 -> x2, waiting for transfers between devices: 750 us -> 248 us  [scatter(): lax.psum_scatter(grad.astype(low), 'dp', scatter_dimension=0, tiled=True)]
    scatter-add x1 -> x0, other arithmetic: 347 us -> none  [shards(): jax.ops.segment_sum(grid_row, buckets.reshape(-1), num_segments=position_...]
    all_gather x5, waiting for transfers between devices: 0.03 us -> 292 us  [the longest x4 238 us: gather(): return lax.all_gather(part, 'dp', axis=0, tiled=True)]
    gather x1 -> x0, local copies, waits for them, and re-layouts: 216 us -> none  [shards(): jnp.take(position_table.astype(jnp.float32), buckets.reshape(-1), axis=1)]
    psum x1 -> x2, waiting for transfers between devices: 0.01 us -> 172 us  [the longest x1 126 us: shards(): small = lax.psum(jnp.concatenate(sums), ('stream', 'dp'))]
    slice x9 -> x5, local copies, waits for them, and re-layouts: 172 us -> 1.24 us  [the longest x1 0.84 us: shards(): table_total = small[:table_count].reshape(heads, bucket_count)]
    dot_general x55 -> x14, matrix products: 223 us -> 115 us  [the longest x1 15.8 us: shards(): jnp.einsum('td,fd->tf', mlp_grad, down_all, preferred_element_type=full)]
    pallas_call x0 -> x4, Pallas kernels: none -> 74.4 us  [the longest x1 31.9 us: attend_backward(): pl.pallas_call(functools.partial(attend_backward_kernel, heads), out_shap...]
  transfers between devices with their start and end apart: 11 -> 13, of which waited for: 4 -> 12; matrix products, arithmetic and copies ran while one was open for 47% -> 11% of each run, Pallas kernels for 0% -> 6%
where the time goes in v1:
time: 1170 us
  waiting for transfers between devices  783 us (67%)
  matrix products  129 us (11%)
  blocking collectives  88.9 us (8%)
  Pallas kernels  74.4 us (6%)
  other arithmetic  39.6 us (3%)
  local copies, waits for them, and re-layouts  27.4 us (2%)
  between operations  16.5 us (1%)
    reduce_scatter x2, waiting for transfers between devices, scatter(): lax.psum_scatter(grad.astype(low), 'dp', scatter_dimension=0, tiled=True)  248 us
    all_gather x4, waiting for transfers between devices, gather(): return lax.all_gather(part, 'dp', axis=0, tiled=True)  238 us
    psum x1, waiting for transfers between devices, shards(): small = lax.psum(jnp.concatenate(sums), ('stream', 'dp'))  126 us
    unnamed x15, waiting for transfers between devices  69.4 us
    all_gather x1, waiting for transfers between devices, shards(): lax.all_gather(modulation_grad, ('stream', 'dp'), axis=0, tiled=True)  53.9 us
    unnamed x1, blocking collectives  49.5 us
    psum x1, waiting for transfers between devices, scatter(): return lax.psum(part, 'stream').astype(full)  46 us
    all_gather x1, blocking collectives, shards(): lax.all_gather(activated, ('stream', 'dp'), axis=0, tiled=True)  39.4 us
  transfers between devices with their start and end apart: 13, of which 12 were waited for; matrix products, arithmetic and copies ran while one was open for 11% of the time, Pallas kernels for 6%

profile of v1, /device:TPU:9, one launch (start us, length us, event | category | flops | bytes accessed | tf_op | source)
XLA Modules:
  0.0 1166.0 jit_solution(4759058596716641940)
XLA Ops:
  8.1 39.4 %all-gather.1 = bf16[32,3,1152]{2,1,0:T(4,128)(2,1)S(1)} all-gather(bf16[1,3,1152]{2,1,0:T(4,128)(2,1)S(1)} %fusion.46), channel_id=1, replica_groups=mesh['stream'=2,'dp'=16] {'stream','dp'}, dimensions={0}, use_global_device_ids=true | all-gather | bytes 228096 | tf_op jit(solution)/shard_map/all_gather | solution.py:247
  53.6 49.5 %all-reduce.1 = bf16[16128]{0:T(1024)(128)(2,1)S(1)} all-reduce(bf16[16128]{0:T(1024)(128)(2,1)S(1)} %dynamic-update-slice), channel_id=2, replica_groups=mesh['stream'=2,'dp'=16] {'dp'}, use_global_device_ids=true, to_apply=%add.1 | all-reduce | flops 16128 | bytes 64512
  105.5 14.6 %shard_map.272.grid_ref = bf16[16,256,256]{2,1,0:T(8,128)(2,1)} custom-call(f32[16,8,128]{2,1,0:T(8,128)} %bitcast.104, s32[256,256]{1,0:T(8,128)} %buckets_ref.3), custom_call_target="tpu_custom_call" | custom-call | tf_op jit(solution)/shard_map/pallas_call | solution.py:30
  121.4 20.0 %all-reduce.12.cloned.1.call-done = f32[48,6912]{1,0:T(8,128)} async-done(((f32[48,6912]{1,0:T(8,128)}), f32[48,6912]{1,0:T(8,128)}) %all-reduce.12.cloned.1.call-update) | async-done | bytes 1327120
  152.5 64.3 %all-gather.9.cloned.1.call-done = bf16[1152,3456]{1,0:T(8,128)(2,1)} async-done(((bf16[72,3456]{1,0:T(8,128)(2,1)}), bf16[1152,3456]{1,0:T(8,128)(2,1)}) %all-gather.9.cloned.1.call-update) | async-done | bytes 7962640 | tf_op jit(solution)/shard_map/all_gather | solution.py:241
  227.1 15.1 %shard_map.273 = (bf16[512,1152]{1,0:T(8,128)(2,1)S(1)}, bf16[768,3456]{1,0:T(8,128)(2,1)}, bf16[3,16,256,256]{3,2,1,0:T(8,128)(2,1)}) custom-call(bf16[512,3456]{1,0:T(8,128)(2,1)} %add_convert_fusion.packed_ref, s32[1,512]{1,0:T(1,128)S(1)} %multiply_add_fusion.frame_row_ref, s32[512,1]{1,0:T(8,128)S(1)} %copy.40.frame_column_ref, ...), custom_call_target="tpu_custom_call" | custom-call | tf_op jit(solution)/shard_map/pallas_call | solution.py:130
  243.2 17.7 %all-gather.11.cloned.1.call-done = bf16[1152,1152]{1,0:T(8,128)(2,1)} async-done(((bf16[72,1152]{1,0:T(8,128)(2,1)}), bf16[1152,1152]{1,0:T(8,128)(2,1)}) %all-gather.11.cloned.1.call-update) | async-done | bytes 2654224 | tf_op jit(solution)/shard_map/all_gather | solution.py:241
  271.4 78.1 %all-gather.13.cloned.1.call-done = bf16[1152,4608]{1,0:T(8,128)(2,1)} async-done(((bf16[72,4608]{1,0:T(8,128)(2,1)}), bf16[1152,4608]{1,0:T(8,128)(2,1)}) %all-gather.13.cloned.1.call-update) | async-done | bytes 10616848 | tf_op jit(solution)/shard_map/all_gather | solution.py:241
  349.6 11.5 fusion.59
  361.1 77.5 %all-gather.15.cloned.1.call-done = bf16[4608,1152]{1,0:T(8,128)(2,1)} async-done(((bf16[288,1152]{1,0:T(8,128)(2,1)}), bf16[4608,1152]{1,0:T(8,128)(2,1)}) %all-gather.15.cloned.1.call-update) | async-done | bytes 10616848 | tf_op jit(solution)/shard_map/all_gather | solution.py:241
  438.6 15.8 %convert_reduce_fusion = (f32[4608]{0:T(1024)S(1)}, bf16[512,4608]{1,0:T(8,128)(2,1)S(1)}) fusion(f32[512,4608]{1,0:T(8,128)} %fusion.59, f32[4608]{0:T(1024)S(1)} %reshape.193, bf16[512,1152]{1,0:T(8,128)(2,1)} %get-tuple-element.70, bf16[4608,1152]{1,0:T(8,128)(2,1)} %all-gather.15.cloned.1.call-done), kind=kOutput, calls=%fused_computation.16 | convolution fusion | flops 5490077184 | bytes 25989120 | tf_op jit(solution)/shard_map/td,fd->tf/dot_general | solution.py:308
  454.4 13.1 %fusion.49 = (f32[512]{0:T(512)S(1)}, f32[512]{0:T(512)S(1)}, f32[512,1152]{1,0:T(8,128)S(1)}) fusion(f32[512,6912]{1,0:T(8,128)} %copy-done.6, f32[512]{0:T(512)S(1)} %add_rsqrt_fusion, f32[512,1152]{1,0:T(8,128)S(1)} %get-tuple-element.77, f32[512]{0:T(512)S(1)} %broadcast_multiply_fusion.4, bf16[512,4608]{1,0:T(8,128)(2,1)S(1)} %get-tuple-element.72, ...), kind=kOutput, calls=%fused_computation.114 | convolution fusion | flops 5439945728 | bytes 22421504 | tf_op jit(solution)/shard_map/tf,df->td/dot_general | solution.py:313
  467.5 13.7 %convolution_add_fusion = f32[512,1152]{1,0:T(8,128)S(1)} fusion(bf16[4608,1152]{1,0:T(8,128)(2,1)} %all-gather.15.cloned.1.call-done, f32[1152]{0:T(1024)S(1)} %reshape.194, f32[512,4608]{1,0:T(8,128)} %fusion.59, f32[4608]{0:T(1024)S(1)} %reshape.193), kind=kOutput, calls=%fused_computation.24 | convolution fusion | flops 5460000768 | bytes 22436352 | tf_op jit(solution)/shard_map/dot_general | solution.py:294
  494.0 31.9 %shard_map.274 = (bf16[512,3456]{1,0:T(8,128)(2,1)}, f32[256,16,256]{2,1,0:T(8,128)}) custom-call(bf16[768,3456]{1,0:T(8,128)(2,1)} %get-tuple-element.20.placed_ref, bf16[3,16,256,256]{3,2,1,0:T(8,128)(2,1)} %get-tuple-element.21.weights_ref, bf16[512,1152]{1,0:T(8,128)(2,1)} %convolution_convert_fusion.4.upstream_ref, s32[1,512]{1,0:T(1,128)} %copy-done.5, ...), custom_call_target="tpu_custom_call" | custom-call | tf_op jit(solution)/shard_map/pallas_call | solution.py:182
  534.8 13.2 %convolution_convert_fusion = bf16[4608,1152]{1,0:T(8,128)(2,1)} fusion(bf16[512,1152]{1,0:T(8,128)(2,1)} %get-tuple-element.70, f32[512,4608]{1,0:T(8,128)} %fusion.59, f32[4608]{0:T(1024)S(1)} %reshape.193), kind=kOutput, calls=%fused_computation | convolution fusion | flops 5464719360 | bytes 21252096 | tf_op jit(solution)/shard_map/tf,td->fd/dot_general | solution.py:306
  548.1 10.4 convolution_convert_fusion.1
  558.8 12.8 %shard_map.275 = f32[128,128]{1,0:T(8,128)} custom-call(f32[256,16,256]{2,1,0:T(8,128)} %get-tuple-element.23.grad_ref, s32[256,256]{1,0:T(8,128)} %buckets_ref.3), custom_call_target="tpu_custom_call" | custom-call | tf_op jit(solution)/shard_map/pallas_call | solution.py:60
  572.5 12.9 %fusion.50 = (f32[512]{0:T(512)S(1)}, f32[512]{0:T(512)S(1)}, f32[512,6912]{1,0:T(8,128)}, f32[512,1152]{1,0:T(8,128)S(1)}) fusion(f32[512,6912]{1,0:T(8,128)} %copy-done.6, f32[512]{0:T(512)S(1)} %add_rsqrt_fusion.1, f32[512]{0:T(512)S(1)} %broadcast_multiply_fusion.5, bf16[1,512,1152]{2,1,0:T(8,128)(2,1)} %param.17, ...), kind=kOutput, calls=%fused_computation.115 | convolution fusion | flops 4081581056 | bytes 19767296 | tf_op jit(solution)/shard_map/te,de->td/dot_general | solution.py:350
  608.7 46.9 %reduce-scatter.13.cloned.1.call-done = bf16[72,3456]{1,0:T(8,128)(2,1)} async-done(((bf16[1152,3456]{1,0:T(8,128)(2,1)}), bf16[72,3456]{1,0:T(8,128)(2,1)}) %reduce-scatter.13.cloned.1.call-update) | async-done | bytes 497680
  655.6 124.2 %reduce-scatter.11.cloned.1.call-done = bf16[288,1152]{1,0:T(8,128)(2,1)} async-done(((bf16[4608,1152]{1,0:T(8,128)(2,1)}), bf16[288,1152]{1,0:T(8,128)(2,1)}) %reduce-scatter.11.cloned.1.call-update) | async-done | bytes 663568 | tf_op jit(solution)/shard_map/reduce_scatter | solution.py:302
  779.8 124.1 %reduce-scatter.9.cloned.1.call-done = bf16[72,4608]{1,0:T(8,128)(2,1)} async-done(((bf16[1152,4608]{1,0:T(8,128)(2,1)}), bf16[72,4608]{1,0:T(8,128)(2,1)}) %reduce-scatter.9.cloned.1.call-update) | async-done | bytes 663568 | tf_op jit(solution)/shard_map/reduce_scatter | solution.py:302
  903.9 126.4 %all-reduce.10.cloned.1.call-done = f32[24592]{0:T(1024)} async-done(((f32[24592]{0:T(1024)}), f32[24592]{0:T(1024)}) %all-reduce.10.cloned.1.call-update) | async-done | bytes 98384 | tf_op jit(solution)/shard_map/psum | solution.py:341
  1035.9 53.9 %all-gather.17.cloned.1.call-done = bf16[32,3,6912]{2,1,0:T(4,128)(2,1)} async-done(((bf16[1,3,6912]{2,1,0:T(4,128)(2,1)}), bf16[32,3,6912]{2,1,0:T(4,128)(2,1)}) %all-gather.17.cloned.1.call-update) | async-done | bytes 1327120 | tf_op jit(solution)/shard_map/all_gather | solution.py:370
  1106.7 46.0 %all-reduce.14.cloned.1.call-done = (bf16[72,3456]{1,0:T(8,128)(2,1)}, bf16[72,1152]{1,0:T(8,128)(2,1)}, bf16[72,4608]{1,0:T(8,128)(2,1)}, bf16[288,1152]{1,0:T(8,128)(2,1)}) async-done(((bf16[72,3456]{1,0:T(8,128)(2,1)}, bf16[72,1152]{1,0:T(8,128)(2,1)}, bf16[72,4608]{1,0:T(8,128)(2,1)}, bf16[288,1152]{1,0:T(8,128)(2,1)}), (bf16[72,3456]{1,0:T(8,128)(2,1)}, bf16[72,1152]{1,0:T(8,128)(2,1)}, ...) | async-done | bytes 1990672 | tf_op jit(solution)/shard_map/psum | solution.py:303
  (202 shorter events, 116.6 us)
Async XLA Ops:
  7.2 40.5 %copy-start = (bf16[72,6912]{1,0:T(8,128)(2,1)S(1)}, bf16[72,6912]{1,0:T(8,128)(2,1)}, u32[]{:S(2)}) copy-start(bf16[72,6912]{1,0:T(8,128)(2,1)} %param.22) | copy-start | bytes 2985988
  7.2 134.2 %all-reduce.12.cloned.1.call-start = ((), (), s32[]{:S(2)}) async-start(), calls=%async_computation.13 | async-start | bytes 2654208
  49.2 54.8 %copy-start.26 = (bf16[16,961]{1,0:T(8,128)(2,1)S(1)}, bf16[16,961]{1,0:T(8,128)(2,1)}, u32[]{:S(2)}) copy-start(bf16[16,961]{1,0:T(8,128)(2,1)} %param.26) | copy-start | bytes 92260
  49.2 55.5 %copy-start.27 = (s32[1,512]{1,0:T(1,128)S(1)}, s32[1,512]{1,0:T(1,128)}, u32[]{:S(2)}) copy-start(s32[1,512]{1,0:T(1,128)} %param.19) | copy-start | bytes 6148
  49.2 55.5 %copy-start.33 = (s32[1,512]{1,0:T(1,128)S(1)}, s32[1,512]{1,0:T(1,128)}, u32[]{:S(2)}) copy-start(s32[1,512]{1,0:T(1,128)} %param.20) | copy-start | bytes 6148
  49.2 167.5 %all-gather.9.cloned.1.call-start = ((), (), s32[]{:S(2)}) async-start(), calls=%async_computation.5 | async-start | bytes 8460288 | tf_op jit(solution)/shard_map/all_gather | solution.py:241
  50.0 210.9 %all-gather.11.cloned.1.call-start = ((), (), s32[]{:S(2)}) async-start(), calls=%async_computation.6 | async-start | bytes 2820096 | tf_op jit(solution)/shard_map/all_gather | solution.py:241
  50.7 70.0 %copy-start.8 = (bf16[1,512,1152]{2,1,0:T(8,128)(2,1)S(1)}, bf16[1,512,1152]{2,1,0:T(8,128)(2,1)}, u32[]{:S(2)}) copy-start(bf16[1,512,1152]{2,1,0:T(8,128)(2,1)} %param.17) | copy-start | bytes 3538948
  50.7 298.8 %all-gather.13.cloned.1.call-start = ((), (), s32[]{:S(2)}) async-start(), calls=%async_computation.7 | async-start | bytes 11280384 | tf_op jit(solution)/shard_map/all_gather | solution.py:241
  51.3 387.3 %all-gather.15.cloned.1.call-start = ((), (), s32[]{:S(2)}) async-start(), calls=%async_computation.8 | async-start | bytes 11280384 | tf_op jit(solution)/shard_map/all_gather | solution.py:241
  51.9 556.8 %reduce-scatter.15.cloned.1.call-start = ((), (), s32[]{:S(2)}) async-start(), calls=%async_computation.15 | async-start | bytes 2820096
  104.7 122.4 %copy-start.5 = (s32[1,512]{1,0:T(1,128)}, s32[1,512]{1,0:T(1,128)S(1)}, u32[]{:S(2)}) copy-start(s32[1,512]{1,0:T(1,128)S(1)} %multiply_add_fusion.frame_row_ref) | copy-start | bytes 6148
  104.8 122.2 %copy-start.4 = (s32[512,1]{1,0:T(8,128)}, s32[512,1]{1,0:T(8,128)S(1)}, u32[]{:S(2)}) copy-start(s32[512,1]{1,0:T(8,128)S(1)} %copy.40.frame_column_ref) | copy-start | bytes 6148
  120.7 25.1 %copy-start.28 = (pred[512]{0:T(512)(128)(4,1)}, pred[512]{0:T(512)(128)(4,1)S(1)}, u32[]{:S(2)}) copy-start(pred[512]{0:T(512)(128)(4,1)S(1)} %get-tuple-element.63) | copy-start | bytes 1540
  120.7 25.1 %copy-start.30 = (pred[512]{0:T(512)(128)(4,1)}, pred[512]{0:T(512)(128)(4,1)S(1)}, u32[]{:S(2)}) copy-start(pred[512]{0:T(512)(128)(4,1)S(1)} %get-tuple-element.64) | copy-start | bytes 1540
  152.5 74.6 %copy-start.1 = (bf16[16,256,256]{2,1,0:T(8,128)(2,1)S(1)}, bf16[16,256,256]{2,1,0:T(8,128)(2,1)}, u32[]{:S(2)}) copy-start(bf16[16,256,256]{2,1,0:T(8,128)(2,1)} %shard_map.272.grid_ref) | copy-start | bytes 6291460
  488.6 167.0 %reduce-scatter.13.cloned.1.call-start = ((), (), s32[]{:S(2)}) async-start(), calls=%async_computation.14 | async-start | bytes 8460288
  494.0 31.9 %copy-start.21 = (bf16[512,1152]{1,0:T(8,128)(2,1)S(1)}, bf16[512,1152]{1,0:T(8,128)(2,1)}, u32[]{:S(2)}) copy-start(bf16[512,1152]{1,0:T(8,128)(2,1)} %fusion.16) | copy-start | bytes 3538948
  534.5 245.2 %reduce-scatter.11.cloned.1.call-start = ((), (), s32[]{:S(2)}) async-start(), calls=%async_computation.11 | async-start | bytes 11280384 | tf_op jit(solution)/shard_map/reduce_scatter | solution.py:302
  548.0 355.8 %reduce-scatter.9.cloned.1.call-start = ((), (), s32[]{:S(2)}) async-start(), calls=%async_computation.10 | async-start | bytes 11280384 | tf_op jit(solution)/shard_map/reduce_scatter | solution.py:302
  558.5 471.9 %all-reduce.10.cloned.1.call-start = ((), (), s32[]{:S(2)}) async-start(), calls=%async_computation.9 | async-start | bytes 204800 | tf_op jit(solution)/shard_map/psum | solution.py:341
  607.9 481.9 %all-gather.17.cloned.1.call-start = ((), (), s32[]{:S(2)}) async-start(), calls=%async_computation.12 | async-start | bytes 1824768 | tf_op jit(solution)/shard_map/all_gather | solution.py:370
  608.7 544.0 %all-reduce.14.cloned.1.call-start = ((), (), s32[]{:S(2)}) async-start(), calls=%async_computation.16 | async-start | bytes 3981312 | tf_op jit(solution)/shard_map/psum | solution.py:303
  1093.8 10.8 all-to-all-start
  (34 other events, 227.0 us)
Sparse Core Ops, SparseCore 0:
  49.4 91.9 all-reduce.11
  143.5 73.1 all-gather.8
  218.9 41.9 all-gather.10
  263.0 86.4 all-gather.12
  351.7 86.8 all-gather.14
  488.7 60.4 reduce-scatter.14
  553.9 101.7 reduce-scatter.12
  659.7 120.0 reduce-scatter.10
  783.8 119.9 reduce-scatter.8
  909.9 120.4 all-reduce.9
  1033.7 55.9 all-gather.16
  1092.1 60.5 all-reduce.13

commit v2 on v1

--- a/solution.py
+++ b/solution.py
@@ -207,6 +207,553 @@
     return jax.nn.gelu(values, approximate=True)
 
 
+MESH = pl.DeviceIdType.MESH
+low = jnp.bfloat16
+full = jnp.float32
+
+
+class Place:
+    def __init__(self):
+        self.x = lax.axis_index("stream")
+        self.d = lax.axis_index("dp")
+        self.z = self.d // 4
+        self.y = (self.d // 2) % 2
+        self.c = self.d % 2
+    def zz(self, j):
+        return (self.z, self.z + 1 - 2 * (self.z % 2), self.z + 2 - 4 * (self.z // 2), 3 - self.z)[j]
+    def chip(self, j=0, yy=0):
+        return self.zz(j) * 2 + (self.y if yy == 0 else 1 - self.y)
+    def at(self, x=0, y=0, j=0, core=0):
+        xx = self.x if x == 0 else 1 - self.x
+        cc = self.c if core == 0 else 1 - self.c
+        return (xx, self.chip(j, y) * 2 + cc)
+
+def gather_region(place, full_ref, w, chip, part):
+    c, x = place.c, place.x
+    if w < 2:
+        off, size = {"all": (0, 2304), "ad": (1024 * x, 1280), "a": (1280 * x, 1024)}[part]
+        col = pl.multiple_of(4608 * w + 2304 * c + off, 128)
+        return full_ref[0].at[pl.ds(pl.multiple_of(chip * 144, 16), 144), pl.ds(col, size)]
+    off, size = {"all": (0, 288), "ad": (128 * x, 160), "a": (160 * x, 128)}[part]
+    row = pl.multiple_of(c * 2304 + chip * 288 + off, 16)
+    return full_ref[1].at[pl.ds(row, size), :]
+
+class Gather:
+    def __init__(self, place, full_ref, send, recv):
+        self.place, self.full, self.send, self.recv = place, full_ref, send, recv
+    def copy(self, w, slot, region_src, device):
+        return pltpu.make_async_remote_copy(src_ref=region_src, dst_ref=region_src, send_sem=self.send.at[w, slot],
+            recv_sem=self.recv.at[w, slot], device_id=device, device_id_type=MESH)
+    def region(self, w, chip, part):
+        return gather_region(self.place, self.full, w, chip, part)
+    def desc(self, w, kind, j=0, yy=0, recv=False):
+        p = self.place
+        if kind == "z":
+            return self.copy(w, j - 1, self.region(w, p.chip(j if recv else 0), "ad"), p.at(j=j))
+        if kind == "y":
+            part = "all" if j == 0 else "ad"
+            return self.copy(w, 3 + j, self.region(w, p.chip(j, 1 if recv else 0), part), p.at(y=1))
+        if kind == "x":
+            if recv:
+                return self.copy(w, 7 + 2 * (j - 1) + yy, self.other_a(w, p.chip(j, yy)), p.at(x=1))
+            return self.copy(w, 7 + 2 * (j - 1) + yy, self.region(w, p.chip(j, yy), "a"), p.at(x=1))
+        if kind == "s":
+            slot = 13 + 2 * j + yy - 1
+            if recv:
+                return self.copy(w, slot, self.other_half(w, p.chip(j, yy)), p.at(core=1))
+            return self.copy(w, slot, self.region(w, p.chip(j, yy), "all"), p.at(core=1))
+    def other_a(self, w, chip):
+        q = type("Q", (), {})(); q.c, q.x = self.place.c, 1 - self.place.x
+        return gather_region(q, self.full, w, chip, "a")
+    def other_half(self, w, chip):
+        q = type("Q", (), {})(); q.c, q.x = 1 - self.place.c, self.place.x
+        return gather_region(q, self.full, w, chip, "all")
+    def start(self, w):
+        for j in (1, 2, 3):
+            self.desc(w, "z", j).start()
+        self.desc(w, "y", 0).start()
+    def on_z(self, w, j):
+        self.desc(w, "z", j, recv=True).wait_recv()
+        self.desc(w, "x", j, 0).start()
+        self.desc(w, "y", j).start()
+    def on_y(self, w, j):
+        self.desc(w, "y", j, recv=True).wait_recv()
+        if j == 0:
+            self.desc(w, "s", 0, 1).start()
+        else:
+            self.desc(w, "x", j, 1).start()
+    def on_x(self, w, j, yy):
+        self.desc(w, "x", j, yy, recv=True).wait_recv()
+        self.desc(w, "s", j, yy).start()
+    def on_s(self, w, j, yy):
+        self.desc(w, "s", j, yy, recv=True).wait_recv()
+    def finish(self, w):
+        for j in (1, 2, 3):
+            self.desc(w, "z", j).wait_send()
+            self.desc(w, "y", j).wait_send()
+            for yy in (0, 1):
+                self.desc(w, "x", j, yy).wait_send()
+                self.desc(w, "s", j, yy).wait_send()
+        self.desc(w, "y", 0).wait_send()
+        self.desc(w, "s", 0, 1).wait_send()
+
+def gather_kernel(note_ref, mod_ref, shard_ref, down_ref, full12_ref, full3_ref, inbox_ref, modulation_ref,
+                  sib, chip, msend, mrecv, csem, csend, crecv, send, recv, part, got0, got1, psend, precv):
+    place = Place()
+    x, d, c = place.x, place.d, place.c
+    barrier = pltpu.get_barrier_semaphore()
+    def peer(t, k):
+        return (x if t == 0 else 1 - x, (d + k) % 16)
+    for t in (0, 1):
+        for k in range(16):
+            if (t, k) != (0, 0):
+                pl.semaphore_signal(barrier, inc=1, device_id=peer(t, k), device_id_type=MESH)
+    pl.semaphore_wait(barrier, 31)
+    sib_copy = pltpu.make_async_remote_copy(src_ref=shard_ref, dst_ref=sib, send_sem=csend.at[0], recv_sem=crecv.at[0],
+        device_id=place.at(core=1), device_id_type=MESH)
+    sib_copy.start()
+    mine = full3_ref.at[pl.ds(pl.multiple_of(c * 2304 + place.chip() * 288, 16), 288), :]
+    own3 = pltpu.make_async_copy(down_ref, mine, csem.at[0])
+    own3.start()
+    theirs = full3_ref.at[pl.ds(pl.multiple_of((1 - c) * 2304 + place.chip() * 288, 16), 288), :]
+    def note(t, k, recv=False):
+        if recv:
+            src = (x if t == 0 else 1 - x) * 16 + (d + 16 - k) % 16
+        else:
+            src = x * 16 + d
+        return pltpu.make_async_remote_copy(src_ref=note_ref.at[(d + k) % 16], dst_ref=inbox_ref.at[src],
+            send_sem=msend.at[t, k], recv_sem=mrecv.at[t, k], device_id=peer(t, k), device_id_type=MESH)
+    for t in (0, 1):
+        for k in range(16):
+            if (t, k) != (0, 0):
+                note(t, k).start()
+    inbox_ref[x * 16 + d] = note_ref[d]
+    down_copy = pltpu.make_async_remote_copy(src_ref=down_ref, dst_ref=mine, send_sem=csend.at[1], recv_sem=crecv.at[1],
+        device_id=place.at(core=1), device_id_type=MESH)
+    down_copy.start()
+    sib_copy.wait()
+    columns = 512
+    def assemble(i, _):
+        span = pl.ds(pl.multiple_of(i * columns, columns), columns)
+        own, other = shard_ref[0:72, span].astype(jnp.float32), sib[0:72, span].astype(jnp.float32)
+        top = jnp.where(c == 0, own, other)
+        bottom = jnp.where(c == 0, other, own)
+        chip[:, span] = jnp.concatenate([top, bottom], axis=0).astype(jnp.bfloat16)
+        return 0
+    lax.fori_loop(0, shard_ref.shape[1] // columns, assemble, 0)
+    own12 = pltpu.make_async_copy(chip, full12_ref.at[pl.ds(pl.multiple_of(place.chip() * 144, 16), 144), :], csem.at[1])
+    own12.start()
+    own12.wait()
+    own3.wait()
+    g = Gather(place, (full12_ref, full3_ref), send, recv)
+    g.start(0)
+    for t in (0, 1):
+        for k in range(16):
+            if (t, k) != (0, 0):
+                note(t, k, recv=True).wait_recv()
+    lhs = inbox_ref[pl.ds(x * 16, 16), 0:8, :].reshape(128, 128).astype(jnp.bfloat16)
+    cols = 768
+    def project(i, _):
+        span = pl.ds(pl.multiple_of(i * cols, cols), cols)
+        out = jnp.dot(lhs, mod_ref[:, span], preferred_element_type=jnp.float32)
+        for chip_at in range(8):
+            for core in range(2):
+                dest = (chip_at * 2 + core) * 8
+                part[core, chip_at, :, span] = out[dest : dest + 4]
+        return 0
+    lax.fori_loop(0, mod_ref.shape[1] // cols, project, 0)
+    half = pltpu.make_async_remote_copy(src_ref=part.at[1 - c], dst_ref=got0, send_sem=psend.at[0], recv_sem=precv.at[0],
+        device_id=place.at(core=1), device_id_type=MESH)
+    half.start()
+    half.wait()
+    for chip_at in range(8):
+        part[c, chip_at] += got0[chip_at]
+    def share(k):
+        dest = (place.chip() + k) % 8
+        return pltpu.make_async_remote_copy(src_ref=part.at[c, dest], dst_ref=got1.at[k - 1], send_sem=psend.at[k], recv_sem=precv.at[k],
+            device_id=(x, dest * 2 + c), device_id_type=MESH)
+    for k in range(1, 8):
+        share(k).start()
+    for j in (1, 2, 3):
+        g.on_z(0, j)
+    g.start(1)
+    for k in range(1, 8):
+        share(k).wait_recv()
+    total = part[c, place.chip()]
+    for k in range(1, 8):
+        total += got1[k - 1]
+    modulation_ref[...] = total
+    g.on_y(0, 0)
+    for j in (1, 2, 3):
+        g.on_y(0, j)
+    for j in (1, 2, 3):
+        g.on_z(1, j)
+    for j in (1, 2, 3):
+        g.on_x(0, j, 0)
+    down_copy.wait()
+    g.start(2)
+    for j in (1, 2, 3):
+        g.on_x(0, j, 1)
+    g.on_y(1, 0)
+    for j in (1, 2, 3):
+        g.on_y(1, j)
+    for j in (1, 2, 3):
+        g.on_z(2, j)
+    for yy in (0, 1):
+        for j in (1, 2, 3):
+            g.on_x(1, j, yy)
+    g.on_y(2, 0)
+    for j in (1, 2, 3):
+        g.on_y(2, j)
+    for yy in (0, 1):
+        for j in (1, 2, 3):
+            g.on_x(2, j, yy)
+    for w in range(3):
+        for j in range(4):
+            for yy in (0, 1):
+                if (j, yy) != (0, 0):
+                    g.on_s(w, j, yy)
+        g.finish(w)
+    for t in (0, 1):
+        for k in range(16):
+            if (t, k) != (0, 0):
+                note(t, k).wait_send()
+    for k in range(1, 8):
+        share(k).wait_send()
+
+def gather_weights(notes, modulator, shard12, down):
+    any_, vm = pl.BlockSpec(memory_space=pl.ANY), pl.BlockSpec(memory_space=pltpu.VMEM)
+    width = modulator.shape[1]
+    return pl.pallas_call(
+        gather_kernel,
+        out_shape=(jax.ShapeDtypeStruct((1152, 9216), low), jax.ShapeDtypeStruct((4608, 1152), low),
+                   jax.ShapeDtypeStruct((32, 16, 128), full), jax.ShapeDtypeStruct((4, width), full)),
+        in_specs=[vm, vm, vm, any_],
+        out_specs=(any_, any_, vm, vm),
+        scratch_shapes=[
+            pltpu.VMEM(shard12.shape, low), pltpu.VMEM((144, shard12.shape[1]), low),
+            pltpu.SemaphoreType.DMA((2, 16)), pltpu.SemaphoreType.DMA((2, 16)),
+            pltpu.SemaphoreType.DMA((2,)), pltpu.SemaphoreType.DMA((2,)), pltpu.SemaphoreType.DMA((2,)),
+            pltpu.SemaphoreType.DMA((3, 20)), pltpu.SemaphoreType.DMA((3, 20)),
+            pltpu.VMEM((2, 8, 4, width), full), pltpu.VMEM((8, 4, width), full), pltpu.VMEM((7, 4, width), full),
+            pltpu.SemaphoreType.DMA((8,)), pltpu.SemaphoreType.DMA((8,)),
+        ],
+        compiler_params=pltpu.CompilerParams(collective_id=0, has_side_effects=True, vmem_limit_bytes=40 * 2**20),
+    )(notes, modulator, shard12, down)
+
+def feed_order(values, axis, chips):
+    shape = values.shape
+    part = shape[axis] // (2 * chips)
+    split = shape[:axis] + (chips, 2, part) + shape[axis + 1 :]
+    return jnp.swapaxes(values.reshape(split), axis, axis + 1).reshape(shape)
+def feed_restore(values, axis, chips):
+    shape = values.shape
+    part = shape[axis] // (2 * chips)
+    split = shape[:axis] + (2, chips, part) + shape[axis + 1 :]
+    return jnp.swapaxes(values.reshape(split), axis, axis + 1).reshape(shape)
+
+
+def rs_part(place, w, part):
+    x = place.x
+    unit = 768 if w < 2 else 96
+    off, size = {"all": (0, 3), "ad": (x, 2), "a": (2 * x, 1), "o": (2 - 2 * x, 1), "od": (1 - x, 2)}[part]
+    return pl.multiple_of(unit * off, 128 if w < 2 else 16), unit * size
+
+class Scatter:
+    def __init__(self, place, acc12, acc3, rx, ry, rz, rf, send, recv):
+        self.p, self.acc12, self.acc3, self.rx, self.ry, self.rz, self.rf, self.send, self.recv = place, acc12, acc3, rx, ry, rz, rf, send, recv
+    def acc(self, w, chip, part):
+        off, size = rs_part(self.p, w, part)
+        if w < 2:
+            return self.acc12.at[chip, :, pl.ds(2304 * w + off, size)]
+        return self.acc3.at[chip, pl.ds(off, size), :]
+    def land(self, w, kind, i, size=None):
+        b = {"x": self.rx, "y": self.ry, "z": self.rz, "f": self.rf, "Y": self.rf}[kind]
+        if kind == "f":
+            return self.rf[w].at[0]
+        if kind == "Y":
+            return self.rf[w].at[1]
+        return b[w].at[i]
+    def copy(self, w, slot, src, dst, device):
+        return pltpu.make_async_remote_copy(src_ref=src, dst_ref=dst, send_sem=self.send.at[w, slot], recv_sem=self.recv.at[w, slot], device_id=device, device_id_type=MESH)
+    def x(self, w, j, yy):
+        return self.copy(w, 2 * (j - 1) + yy, self.acc(w, self.p.chip(j, yy), "o"), self.land(w, "x", 2 * (j - 1) + yy), self.p.at(x=1))
+    def y(self, w, j):
+        return self.copy(w, 5 + j, self.acc(w, self.p.chip(j, 1), "ad"), self.land(w, "y", j - 1), self.p.at(y=1))
+    def Y(self, w):
+        return self.copy(w, 9, self.acc(w, self.p.chip(0, 1), "all"), self.land(w, "Y", 0), self.p.at(y=1))
+    def z(self, w, j):
+        return self.copy(w, 9 + j, self.acc(w, self.p.chip(j, 0), "ad"), self.land(w, "z", j - 1), self.p.at(j=j))
+    def f(self, w):
+        return self.copy(w, 13, self.acc(w, self.p.chip(0, 0), "all"), self.land(w, "f", 0), self.p.at(x=1))
+    def add(self, w, chip, part, land):
+        dst = self.acc(w, chip, part)
+        rows = dst.shape[0]
+        step = 48
+        def body(i, _):
+            span = pl.ds(pl.multiple_of(i * step, 16), step)
+            dst[span, :] = dst[span, :] + land[span, :]
+            return 0
+        lax.fori_loop(0, rows // step, body, 0)
+    def ready(self, w, j, yy):
+        if j > 0:
+            self.x(w, j, yy).start()
+        elif yy == 1:
+            self.Y(w).start()
+    def on_x(self, w, j, yy):
+        self.x(w, j, yy).wait_recv()
+        self.add(w, self.p.chip(j, yy), "a", self.land(w, "x", 2 * (j - 1) + yy))
+        if yy == 1:
+            self.y(w, j).start()
+    def on_y(self, w, j):
+        self.y(w, j).wait_recv()
+        self.add(w, self.p.chip(j, 0), "ad", self.land(w, "y", j - 1))
+        self.z(w, j).start()
+    def on_Y(self, w):
+        self.Y(w).wait_recv()
+        self.add(w, self.p.chip(0, 0), "all", self.land(w, "Y", 0))
+    def on_z(self, w, j):
+        self.z(w, j).wait_recv()
+        self.add(w, self.p.chip(0, 0), "ad", self.land(w, "z", j - 1))
+    def last(self, w):
+        self.f(w).start()
+    def finish(self, w):
+        for j in (1, 2, 3):
+            for yy in (0, 1):
+                self.x(w, j, yy).wait_send()
+            self.y(w, j).wait_send()
+            self.z(w, j).wait_send()
+        self.Y(w).wait_send()
+
+def rs_shapes():
+    V, D = pltpu.VMEM, pltpu.SemaphoreType.DMA
+    a = [V((8, 144, 4608), low), V((8, 288, 1152), low)]
+    rx = [V((6, 144, 768), low), V((6, 144, 768), low), V((6, 96, 1152), low)]
+    ry = [V((3, 144, 1536), low), V((3, 144, 1536), low), V((3, 192, 1152), low)]
+    rz = [V((3, 144, 1536), low), V((3, 144, 1536), low), V((3, 192, 1152), low)]
+    rf = [V((2, 144, 2304), low), V((2, 144, 2304), low), V((2, 288, 1152), low)]
+    return a, rx, ry, rz, rf
+
+def scatter_kernel(sizes, mg_ref, vec_ref, inbox_ref, mod_ref, g12_ref, g3_ref,
+                   out12_ref, out3_ref, vec_out_ref, gmod_ref, gmodsum_ref, cond_ref, *rest):
+    it = iter(rest)
+    take = lambda n: [next(it) for _ in range(n)]
+    acc12, acc3 = take(2)
+    rx, ry, rz, rf = take(3), take(3), take(3), take(3)
+    own12, own3, fin, sibfin = take(4)
+    vbuf, vsum, mgall, cpart = take(4)
+    send, recv, ssend, srecv, lsem, vsend, vrecv, msend, mrecv, csend, crecv, fsend, frecv = take(13)
+    place = Place()
+    x, d, c, z = place.x, place.d, place.c, place.z
+    barrier = pltpu.get_barrier_semaphore()
+    for k in range(1, 16):
+        pl.semaphore_signal(barrier, inc=1, device_id=(x, (d + k) % 16), device_id_type=MESH)
+    pl.semaphore_signal(barrier, inc=1, device_id=place.at(x=1), device_id_type=MESH)
+    pl.semaphore_wait(barrier, 16)
+    s = Scatter(place, acc12, acc3, rx, ry, rz, rf, send, recv)
+    order = [(1, 1), (1, 0), (2, 1), (2, 0), (3, 1), (3, 0), (0, 1), (0, 0)]
+    def sib(w, n, recv_side=False):
+        j, yy = order[n]
+        chip = place.chip(j, yy)
+        cc = 1 - c
+        if w < 2:
+            src = g12_ref.at[pl.ds(pl.multiple_of(chip * 144, 16), 144), pl.ds(pl.multiple_of(4608 * w + 2304 * cc, 128), 2304)]
+            dst = acc12.at[chip, :, pl.ds(2304 * w, 2304)]
+        else:
+            src = g3_ref.at[pl.ds(pl.multiple_of(cc * 2304 + chip * 288, 16), 288), :]
+            dst = acc3.at[chip]
+        return pltpu.make_async_remote_copy(src_ref=src, dst_ref=dst, send_sem=ssend.at[w, n], recv_sem=srecv.at[w, n], device_id=place.at(core=1), device_id_type=MESH)
+    def own(w, n):
+        j, yy = order[n]
+        chip = place.chip(j, yy)
+        if w < 2:
+            src = g12_ref.at[pl.ds(pl.multiple_of(chip * 144, 16), 144), pl.ds(pl.multiple_of(4608 * w + 2304 * c, 128), 2304)]
+            dst = own12.at[n % 2]
+        else:
+            src = g3_ref.at[pl.ds(pl.multiple_of(c * 2304 + chip * 288, 16), 288), :]
+            dst = own3.at[n % 2]
+        return pltpu.make_async_copy(src, dst, lsem.at[w, n])
+    def stage0(w):
+        for n in range(8):
+            sib(w, n).start()
+        own(w, 0).start()
+        for n in range(8):
+            if n < 7:
+                own(w, n + 1).start()
+            own(w, n).wait()
+            sib(w, n).wait_recv()
+            j, yy = order[n]
+            s.add(w, place.chip(j, yy), "all", (own12 if w < 2 else own3).at[n % 2])
+            s.ready(w, j, yy)
+    def mids(w):
+        for j in (1, 2, 3):
+            s.on_x(w, j, 1)
+            s.on_x(w, j, 0)
+    def ys(w):
+        for j in (1, 2, 3):
+            s.on_y(w, j)
+        s.on_Y(w)
+    def zs(w):
+        for j in (1, 2, 3):
+            s.on_z(w, j)
+        s.last(w)
+    def vcopy(n):
+        if n < 3:
+            dev = (place.at(core=1), place.at(x=1), place.at(y=1))[n]
+            return pltpu.make_async_remote_copy(src_ref=vsum, dst_ref=vbuf.at[n], send_sem=vsend.at[n], recv_sem=vrecv.at[n], device_id=dev, device_id_type=MESH)
+        j = n - 2
+        return pltpu.make_async_remote_copy(src_ref=vsum, dst_ref=vbuf.at[3 + z], send_sem=vsend.at[n], recv_sem=vrecv.at[n], device_id=place.at(j=j), device_id_type=MESH)
+    def vrecv_wait(j):
+        pltpu.make_async_remote_copy(src_ref=vsum, dst_ref=vbuf.at[3 + place.zz(j)], send_sem=vsend.at[2 + j], recv_sem=vrecv.at[2 + j], device_id=place.at(j=j), device_id_type=MESH).wait_recv()
+    def mrow(xx, chip, cc):
+        return (x if xx == 0 else 1 - x) * 16 + chip * 2 + (c if cc == 0 else 1 - c)
+    def mcopy(slot, row, dev):
+        return pltpu.make_async_remote_copy(src_ref=mgall.at[row], dst_ref=mgall.at[row], send_sem=msend.at[slot], recv_sem=mrecv.at[slot], device_id=dev, device_id_type=MESH)
+    def mz(j, r=False):
+        return mcopy(j, mrow(0, place.chip(j if r else 0), 0), place.at(j=j))
+    def my(j, r=False):
+        return mcopy(4 + j, mrow(0, place.chip(j, 1 if r else 0), 0), place.at(y=1))
+    def mx(j, yy, r=False):
+        return mcopy(8 + 2 * j + yy, mrow(1 if r else 0, place.chip(j, yy), 0), place.at(x=1))
+    def ms(xx, j, yy, r=False):
+        return mcopy(16 + xx * 8 + 2 * j + yy, mrow(xx, place.chip(j, yy), 1 if r else 0), place.at(core=1))
+    stage0(2)
+    vsum[...] = vec_ref[...]
+    mgall[x * 16 + d] = mg_ref[...]
+    vcopy(0).start()
+    for j in (1, 2, 3):
+        mz(j).start()
+    my(0).start()
+    mx(0, 0).start()
+    ms(0, 0, 0).start()
+    vcopy(0).wait()
+    vsum[...] += vbuf[0]
+    vcopy(1).start()
+    for j in (1, 2, 3):
+        mz(j, True).wait_recv()
+        my(j).start()
+        mx(j, 0).start()
+        ms(0, j, 0).start()
+    mids(2)
+    vcopy(1).wait()
+    vsum[...] += vbuf[1]
+    vcopy(2).start()
+    for j in (0, 1, 2, 3):
+        my(j, True).wait_recv()
+        mx(j, 1).start()
+        ms(0, j, 1).start()
+    stage0(1)
+    ys(2)
+    vcopy(2).wait()
+    vsum[...] += vbuf[2]
+    for j in (1, 2, 3):
+        vcopy(2 + j).start()
+    vbuf[3 + z] = vsum[...]
+    for yy in (0, 1):
+        for j in range(4):
+            mx(j, yy, True).wait_recv()
+            ms(1, j, yy).start()
+    mids(1)
+    zs(2)
+    stage0(0)
+    ys(1)
+    mids(0)
+    zs(1)
+    for j in (1, 2, 3):
+        vrecv_wait(j)
+    vec_out_ref[...] = vbuf[3] + vbuf[4] + vbuf[5] + vbuf[6]
+    for xx in (0, 1):
+        for yy in (0, 1):
+            for j in range(4):
+                ms(xx, j, yy, True).wait_recv()
+    def place_rows(p, devices):
+        base = 3 * (p - 2) if p >= 2 else 3 * p
+        shape = (devices * 16, devices * 8)
+        r, q = lax.broadcasted_iota(jnp.int32, shape, 0), lax.broadcasted_iota(jnp.int32, shape, 1)
+        return ((r // 16 == q // 8) & (r % 16 - base == q % 8) & (q % 8 < 3)).astype(full).astype(low)
+    act = inbox_ref[:, 0:8, :].reshape(256, 128).astype(low)
+    cond_total = jnp.zeros((128, 128), full)
+    for p in range(6):
+        tile = 0 if p >= 2 else 1
+        span = slice(1152 * p, 1152 * p + 1152)
+        pieces = mgall[:, 16 * tile : 16 * tile + 16, :].reshape(512, 1152)
+        where = place_rows(p, 32)
+        left = jnp.dot(where, act, preferred_element_type=full).astype(low)
+        grad = lax.dot_general(left, pieces, (((0,), (0,)), ((), ())), preferred_element_type=full)
+        gmod_ref[:, span] = grad[0:72]
+        ones = jnp.broadcast_to((jnp.sum(where.astype(full), axis=1, keepdims=True)).astype(low), (512, 128))
+        gmodsum_ref[:, span] = lax.dot_general(ones, pieces, (((0,), (0,)), ((), ())), preferred_element_type=full)[0:8]
+        mine = mgall[pl.ds(x * 16, 16), 16 * tile : 16 * tile + 16, :].reshape(256, 1152)
+        rows = lax.dot_general(place_rows(p, 16), mine, (((0,), (0,)), ((), ())), preferred_element_type=full).astype(low)
+        cond_total += lax.dot_general(rows, mod_ref[:, span], (((1,), (1,)), ((), ())), preferred_element_type=full)
+    cpart[...] = cond_total.reshape(16, 8, 128)
+    def ccopy(k, r=False):
+        dest = (d + k) % 16
+        src = (d + 16 - k) % 16
+        return pltpu.make_async_remote_copy(src_ref=cpart.at[dest], dst_ref=cond_ref.at[src if r else d], send_sem=csend.at[k], recv_sem=crecv.at[k], device_id=(x, dest), device_id_type=MESH)
+    for k in range(1, 16):
+        ccopy(k).start()
+    cond_ref[d] = cpart[d]
+    ys(0)
+    zs(0)
+    def final(w):
+        s.f(w).wait()
+        chip = place.chip(0, 0)
+        if w == 2:
+            out3_ref[...] = acc3[chip].astype(full) + rf[2][0].astype(full)
+        else:
+            span = slice(2304 * w, 2304 * w + 2304)
+            fin[w] = (acc12[chip, :, span].astype(full) + rf[w][0].astype(full)).astype(low)
+            fcopy(w).start()
+    def fcopy(w):
+        return pltpu.make_async_remote_copy(src_ref=fin.at[w], dst_ref=sibfin.at[w], send_sem=fsend.at[w], recv_sem=frecv.at[w], device_id=place.at(core=1), device_id_type=MESH)
+    final(2)
+    final(1)
+    def write(w):
+        fcopy(w).wait()
+        mine, theirs = fin[w].astype(full), sibfin[w].astype(full)
+        mine = jnp.where(c == 0, mine[0:72], mine[72:144])
+        theirs = jnp.where(c == 0, theirs[0:72], theirs[72:144])
+        out12_ref[:, 4608 * w : 4608 * w + 2304] = jnp.where(c == 0, mine, theirs)
+        out12_ref[:, 4608 * w + 2304 : 4608 * w + 4608] = jnp.where(c == 0, theirs, mine)
+    write(1)
+    final(0)
+    write(0)
+    for k in range(1, 16):
+        ccopy(k, True).wait_recv()
+        ccopy(k).wait_send()
+    for j in (1, 2, 3):
+        vcopy(2 + j).wait_send()
+        mz(j).wait_send()
+    for j in range(4):
+        my(j).wait_send()
+        for yy in (0, 1):
+            mx(j, yy).wait_send()
+            for xx in (0, 1):
+                ms(xx, j, yy).wait_send()
+    for w in range(3):
+        s.finish(w)
+        for n in range(8):
+            sib(w, n).wait_send()
+
+def scatter_grads(mg, vec, inbox, mod, g12, g3):
+    any_, vm = pl.BlockSpec(memory_space=pl.ANY), pl.BlockSpec(memory_space=pltpu.VMEM)
+    a, rx, ry, rz, rf = rs_shapes()
+    V, D = pltpu.VMEM, pltpu.SemaphoreType.DMA
+    S = jax.ShapeDtypeStruct
+    return pl.pallas_call(
+        functools.partial(scatter_kernel, None),
+        out_shape=(S((72, 9216), full), S((288, 1152), full), S(vec.shape, full), S((72, 6912), full), S((8, 6912), full), S((16, 8, 128), full)),
+        in_specs=[vm, vm, vm, vm, any_, any_],
+        out_specs=(vm,) * 6,
+        scratch_shapes=a + rx + ry + rz + rf + [
+            V((2, 144, 2304), low), V((2, 288, 1152), low), V((2, 144, 2304), low), V((2, 144, 2304), low),
+            V((7,) + vec.shape, full), V(vec.shape, full), V((32, 32, 1152), low), V((16, 8, 128), full),
+            D((3, 14)), D((3, 14)), D((3, 8)), D((3, 8)), D((3, 8)), D((6,)), D((6,)), D((32,)), D((32,)), D((16,)), D((16,)), D((2,)), D((2,))],
+        compiler_params=pltpu.CompilerParams(collective_id=1, has_side_effects=True, vmem_limit_bytes=63 * 2**20),
+    )(mg, vec, inbox, mod, g12, g3)
+
+
 def shards(
     tokens,
     condition,
@@ -412,6 +959,210 @@
     )
 
 
+def own_shards(
+    tokens,
+    condition,
+    segments,
+    positions,
+    buckets,
+    modulator,
+    modulator_bias,
+    projector,
+    projector_bias,
+    position_table,
+    output_weight,
+    output_bias,
+    up_weight,
+    up_bias,
+    down_weight,
+    down_bias,
+    cotangent,
+):
+    heads, bucket_count = position_table.shape
+    image_tokens = buckets.shape[0]
+    rows, model_width = tokens.shape[1], tokens.shape[2]
+    images = condition.shape[1]
+    shard = modulator.shape[0]
+    feed_width = up_weight.shape[1]
+    dp_index = lax.axis_index("dp")
+    stream_index = lax.axis_index("stream")
+    low = jnp.bfloat16
+    full = jnp.float32
+
+    def gather(part):
+        return lax.all_gather(part, "dp", axis=0, tiled=True)
+
+    inputs = tokens[0].astype(full)
+    slot_ids, places = segments[0], positions[0]
+    silu_value, silu_back = jax.vjp(jax.nn.silu, condition[0].astype(full))
+    activated = silu_value.astype(low)
+    devices = model_width // shard
+    bias_parts = (modulator_bias, projector_bias, output_bias, up_bias, down_bias)
+    slices = jnp.pad(
+        activated.astype(full).reshape(images, devices, shard).transpose(1, 0, 2),
+        ((0, 0), (0, 8 - images), (0, 128 - shard)),
+    )
+    joined = jnp.concatenate(bias_parts).astype(full)
+    joined = jnp.pad(joined, (0, 1024 - joined.shape[0])).reshape(1, 8, 128)
+    notes = jnp.concatenate([slices, jnp.broadcast_to(joined, (devices, 8, 128))], axis=1)
+    chips = devices // 2
+    shard12 = jnp.pad(
+        jnp.concatenate([projector, output_weight, feed_order(up_weight, 1, chips)], axis=1),
+        ((0, 8), (0, 0)),
+    )
+    wide_modulator = jnp.pad(modulator, ((0, 128 - shard), (0, 0)))
+    full12, down_all, inbox, modulation = gather_weights(
+        notes, wide_modulator, shard12, down_weight
+    )
+    bias_all = lax.dynamic_slice(inbox, (stream_index * devices, 8, 0), (devices, 8, 128)).reshape(
+        devices, 1024
+    )
+    bias_full = []
+    start = 0
+    for part in bias_parts:
+        bias_full.append(bias_all[:, start : start + part.shape[0]].reshape(-1))
+        start += part.shape[0]
+    bias_full[3] = feed_order(bias_full[3], 0, chips)
+    modulation = modulation[:3] + bias_full[0]
+    packed_width = 3 * model_width
+    projector_all = full12[:, :packed_width]
+    output_all = full12[:, packed_width : 4 * model_width]
+    up_all = full12[:, 4 * model_width :]
+    grid = bias_grid(position_table, buckets)
+    local = slot_ids[:, None]
+    per_token = jnp.where(
+        local == 0, modulation[0:1], jnp.where(local == 1, modulation[1:2], modulation[2:3])
+    )
+    shift_attn, scale_attn, gate_attn, shift_mlp, scale_mlp, gate_mlp = jnp.split(
+        per_token, 6, axis=1
+    )
+    normed_one, inverse_one = normalize(inputs)
+    hidden_one = (normed_one * (1.0 + scale_attn) + shift_attn).astype(low)
+    packed_bias = jnp.concatenate(
+        [bias_full[1][:model_width], jnp.zeros((model_width,), full), bias_full[1][model_width:]]
+    )
+    packed = (
+        jnp.dot(hidden_one, projector_all, preferred_element_type=full) + packed_bias
+    ).astype(low)
+    attended, placed, weights = attend_forward(packed, slot_ids, places, grid)
+    branch_attn = jnp.dot(attended, output_all, preferred_element_type=full) + bias_full[2]
+    middle = inputs + gate_attn * branch_attn
+    normed_two, inverse_two = normalize(middle)
+    hidden_two = (normed_two * (1.0 + scale_mlp) + shift_mlp).astype(low)
+    up_output = jnp.dot(hidden_two, up_all, preferred_element_type=full) + bias_full[3]
+    activation, gelu_back = jax.vjp(lambda v: jax.nn.gelu(v, approximate=True), up_output)
+    activation_low = activation.astype(low)
+    branch_mlp = jnp.dot(activation_low, down_all, preferred_element_type=full) + bias_full[4]
+    result = (middle + gate_mlp * branch_mlp).astype(low)
+
+    upstream = cotangent[0].astype(full)
+    mlp_grad = (gate_mlp * upstream).astype(low)
+    gate_mlp_grad = branch_mlp * upstream
+
+    down_grad = jnp.einsum("tf,td->fd", activation_low, mlp_grad, preferred_element_type=full)
+    activation_grad = jnp.einsum("td,fd->tf", mlp_grad, down_all, preferred_element_type=full)
+    up_grad_low = gelu_back(activation_grad)[0].astype(low)
+    up_grad = jnp.einsum("td,tf->df", hidden_two, up_grad_low, preferred_element_type=full)
+    hidden_two_grad = jnp.einsum(
+        "tf,df->td", up_grad_low, up_all, preferred_element_type=full
+    )
+    middle_grad = upstream + normalize_back(
+        normed_two, inverse_two, hidden_two_grad * (1.0 + scale_mlp)
+    )
+    attn_grad = (gate_attn * middle_grad).astype(low)
+    gate_attn_grad = branch_attn * middle_grad
+    output_grad = jnp.einsum("td,te->de", attended, attn_grad, preferred_element_type=full)
+    attended_grad = jnp.einsum(
+        "te,de->td", attn_grad, output_all, preferred_element_type=full
+    ).astype(low)
+    packed_grad, grid_grad = attend_backward(placed, weights, attended_grad, slot_ids, places)
+    projector_grad = jnp.einsum("td,te->de", hidden_one, packed_grad, preferred_element_type=full)
+    table_grad = table_histogram(grid_grad, buckets, bucket_count)
+    packed_sums = jnp.sum(packed_grad.astype(full), axis=0)
+    sums = (
+        table_grad.reshape(-1),
+        packed_sums[:model_width],
+        packed_sums[2 * model_width :],
+        jnp.sum(attn_grad.astype(full), axis=0),
+        jnp.sum(up_grad_low.astype(full), axis=0),
+        jnp.sum(mlp_grad.astype(full), axis=0),
+    )
+    hidden_one_grad = jnp.einsum(
+        "te,de->td", packed_grad, projector_all, preferred_element_type=full
+    )
+    inputs_grad = middle_grad + normalize_back(
+        normed_one, inverse_one, hidden_one_grad * (1.0 + scale_attn)
+    )
+    token_mod_grad = jnp.concatenate(
+        [
+            hidden_one_grad,
+            hidden_one_grad * normed_one,
+            gate_attn_grad,
+            hidden_two_grad,
+            hidden_two_grad * normed_two,
+            gate_mlp_grad,
+        ],
+        axis=1,
+    )
+    modulation_grad = jnp.stack(
+        [jnp.sum(jnp.where(local == slot, token_mod_grad, 0.0), axis=0) for slot in range(images)]
+    ).astype(low)
+    mg = modulation_grad.reshape(images, 6, model_width).transpose(1, 0, 2)
+    mg = mg.reshape(6 * images, model_width)
+    late = 2 * images
+    mg = jnp.concatenate(
+        [
+            jnp.pad(mg[late:], ((0, 16 - 4 * images), (0, 0))),
+            jnp.pad(mg[:late], ((0, 16 - late), (0, 0))),
+        ]
+    )
+    vector = jnp.concatenate(sums)
+    vector = jnp.pad(vector, (0, 25600 - vector.shape[0])).reshape(200, 128)
+    grad12 = jnp.concatenate([projector_grad, output_grad, up_grad], axis=1).astype(low)
+    out12, down_grad, small, modulator_grad, modulator_sums, cond_parts = scatter_grads(
+        mg, vector, inbox, wide_modulator, grad12, down_grad.astype(low)
+    )
+    small = small.reshape(-1)
+    table_count = heads * bucket_count
+    table_total = small[:table_count].reshape(heads, bucket_count)
+    bias_grads = []
+    start = table_count
+    for part in bias_parts[1:]:
+        size = part.shape[0]
+        whole = small[start : start + size * devices]
+        if size == 4 * shard:
+            whole = feed_restore(whole, 0, chips)
+        bias_grads.append(lax.dynamic_slice(whole, (dp_index * size,), (size,)))
+        start += size * devices
+    bias_width = modulator_bias.shape[0]
+    modulator_bias_grad = lax.dynamic_slice(
+        modulator_sums[0], (dp_index * bias_width,), (bias_width,)
+    )
+    activated_grad = (
+        cond_parts[:, :images, :shard].transpose(1, 0, 2).reshape(images, model_width)
+    )
+    projector_grad = out12[:, :packed_width]
+    output_grad = out12[:, packed_width : 4 * model_width]
+    up_grad = feed_restore(out12[:, 4 * model_width :], 1, chips)
+    condition_grad = silu_back(activated_grad)[0]
+    return (
+        result[None],
+        inputs_grad[None],
+        condition_grad[None],
+        modulator_grad,
+        modulator_bias_grad,
+        projector_grad,
+        bias_grads[0],
+        table_total,
+        output_grad,
+        bias_grads[1],
+        up_grad,
+        bias_grads[2],
+        down_grad,
+        bias_grads[3],
+    )
+
+
 def solution(mesh):
     in_specs = (
         P("stream", "dp", None),
@@ -448,4 +1199,5 @@
         P("dp", None),
         P("dp"),
     )
-    return jax.shard_map(shards, mesh=mesh, in_specs=in_specs, out_specs=out_specs, check_vma=False)
+    own = dict(mesh.shape) == {'stream': 2, 'dp': 16}
+    return jax.shard_map(own_shards if own else shards, mesh=mesh, in_specs=in_specs, out_specs=out_specs, check_vma=False)

time: 1170 us -> 709 us (0.61)
  waiting for transfers between devices: 783 us -> 0 us
  Pallas kernels: 74.4 us -> 467 us
  blocking collectives: 88.9 us -> 0 us
  local copies, waits for them, and re-layouts: 27.4 us -> 52.2 us
  other arithmetic: 39.6 us -> 60.9 us
  between operations: 16.5 us -> 1.56 us
    pallas_call x0 -> x2, Pallas kernels: none -> 393 us  [the longest x1 215 us: scatter_grads(): pl.pallas_call(functools.partial(scatter_kernel, None), out_shape=(S((72,...]
    all_gather x5 -> x0, waiting for transfers between devices: 292 us -> none  [the longest x4 238 us: gather(): return lax.all_gather(part, 'dp', axis=0, tiled=True)]
    reduce_scatter x2 -> x0, waiting for transfers between devices: 248 us -> none  [scatter(): lax.psum_scatter(grad.astype(low), 'dp', scatter_dimension=0, tiled=True)]
    psum x2 -> x0, waiting for transfers between devices: 172 us -> none  [the longest x1 126 us: shards(): small = lax.psum(jnp.concatenate(sums), ('stream', 'dp'))]
    unnamed x15 -> x0, waiting for transfers between devices: 69.4 us -> none
    unnamed x1 -> x0, blocking collectives: 49.5 us -> none
    all_gather x1 -> x0, blocking collectives: 39.4 us -> none  [shards(): lax.all_gather(activated, ('stream', 'dp'), axis=0, tiled=True)]
    concatenate x2 -> x6, other arithmetic: 1.68 us -> 17.6 us  [the longest x1 13.8 us: own_shards(): jnp.concatenate([projector_grad, output_grad, up_grad], axis=1).astype(low)]
  transfers between devices with their start and end apart: 13 -> 0, of which waited for: 12 -> 0; matrix products, arithmetic and copies ran while one was open for 11% -> 0% of each run, Pallas kernels for 6% -> 0%
where the time goes in v2:
time: 709 us; the launch traced here: 700 us
  Pallas kernels  467 us (66%)
  matrix products  118 us (17%)
  other arithmetic  60.9 us (9%)
  local copies, waits for them, and re-layouts  52.2 us (7%)
    pallas_call x1, Pallas kernels, scatter_grads(): pl.pallas_call(functools.partial(scatter_kernel, None), out_shape=(S((72,...  215 us
    pallas_call x1, Pallas kernels, gather_weights(): pl.pallas_call(gather_kernel, out_shape=(jax.ShapeDtypeStruct((1152, 9216...  178 us
    pallas_call x1, Pallas kernels, attend_backward(): pl.pallas_call(functools.partial(attend_backward_kernel, heads), out_shap...  31.4 us
    dot_general x1, matrix products, own_shards(): jnp.einsum('td,fd->tf', mlp_grad, down_all, preferred_element_type=full)  16.4 us
    pallas_call x1, Pallas kernels, attend_forward(): pl.pallas_call(functools.partial(attend_forward_kernel, heads), out_shape...  14.7 us
    pallas_call x1, Pallas kernels, bias_grid(): pl.pallas_call(grid_kernel, grid=(heads,), in_specs=[pl.BlockSpec((1, chu...  14.5 us

profile of v2, /device:TPU:9, one launch (start us, length us, event | category | flops | bytes accessed | tf_op | source)
XLA Modules:
  0.0 699.5 jit_solution(1552422839159944816)
XLA Ops:
  6.4 3.8 reshape.194
  15.4 177.9 %shard_map.272 = (bf16[1152,9216]{1,0:T(8,128)(2,1)}, bf16[4608,1152]{1,0:T(8,128)(2,1)}, f32[32,16,128]{2,1,0:T(8,128)S(1)}, f32[4,6912]{1,0:T(4,128)S(1)}) custom-call(f32[16,16,128]{2,1,0:T(8,128)S(1)} %pad_maximum_fusion.1.note_ref, bf16[128,6912]{1,0:T(8,128)(2,1)S(1)} %pad.40.mod_ref, bf16[80,9216]{1,0:T(8,128)(2,1)S(1)} %fusion.45.shard_ref, ...), custom_call_target="tpu_custom_call" | custom-call | tf_op jit(solution)/shard_map/pallas_call | solution.py:427
  194.8 8.2 %select_select_fusion = f32[512,6912]{1,0:T(8,128)} fusion(f32[6912]{0:T(1024)S(1)} %get-tuple-element.94, f32[6912]{0:T(1024)S(1)} %get-tuple-element.95, f32[6912]{0:T(1024)S(1)} %get-tuple-element.93, pred[512]{0:T(512)(128)(4,1)S(1)} %get-tuple-element.97, pred[512]{0:T(512)(128)(4,1)S(1)} %get-tuple-element.98), kind=kLoop, calls=%fused_computation.7 | loop fusion | flops 7077888 | bytes 14239744 | tf_op jit(solution)/shard_map/jit(_where)/select_n | solution.py:1033
  207.2 10.0 %add_convert_fusion.packed_ref = bf16[512,3456]{1,0:T(8,128)(2,1)} fusion(bf16[512,1152]{1,0:T(8,128)(2,1)S(1)} %fusion.29, bf16[1152,9216]{1,0:T(8,128)(2,1)} %get-tuple-element.31, f32[3456]{0:T(1024)S(1)} %pad_maximum_fusion.2), kind=kOutput, calls=%fused_computation.25 | convolution fusion | flops 4080402432 | bytes 12695040 | tf_op jit(solution)/shard_map/dot_general | solution.py:1045
  218.1 14.5 %shard_map.273.grid_ref = bf16[16,256,256]{2,1,0:T(8,128)(2,1)} custom-call(f32[16,8,128]{2,1,0:T(8,128)} %bitcast.101, s32[256,256]{1,0:T(8,128)} %buckets_ref.3), custom_call_target="tpu_custom_call" | custom-call | tf_op jit(solution)/shard_map/pallas_call | solution.py:30
  234.1 14.7 %shard_map.274 = (bf16[512,1152]{1,0:T(8,128)(2,1)S(1)}, bf16[768,3456]{1,0:T(8,128)(2,1)}, bf16[3,16,256,256]{3,2,1,0:T(8,128)(2,1)}) custom-call(bf16[512,3456]{1,0:T(8,128)(2,1)} %add_convert_fusion.packed_ref, s32[1,512]{1,0:T(1,128)S(1)} %multiply_add_fusion.frame_row_ref, s32[512,1]{1,0:T(8,128)S(1)} %copy.64.frame_column_ref, ...), custom_call_target="tpu_custom_call" | custom-call | tf_op jit(solution)/shard_map/pallas_call | solution.py:130
  248.9 5.7 fusion.60
  255.9 5.5 convert_reduce_fusion.3
  261.4 13.1 %fusion.9 = f32[512,4608]{1,0:T(8,128)} fusion(bf16[512,1152]{1,0:T(8,128)(2,1)S(1)} %get-tuple-element.109, bf16[1152,9216]{1,0:T(8,128)(2,1)} %get-tuple-element.31), kind=kOutput, calls=%fused_computation.21 | convolution fusion | flops 5435817984 | bytes 21233664 | tf_op jit(solution)/shard_map/dot_general | solution.py:1052
  280.0 16.4 %convert_reduce_fusion = (f32[4608]{0:T(1024)}, bf16[512,4608]{1,0:T(8,128)(2,1)S(1)}) fusion(f32[512,4608]{1,0:T(8,128)} %fusion.9, f32[4608]{0:T(1024)} %add.171, bf16[512,1152]{1,0:T(8,128)(2,1)} %get-tuple-element.100, bf16[4608,1152]{1,0:T(8,128)(2,1)} %get-tuple-element.33), kind=kOutput, calls=%fused_computation.17 | convolution fusion | flops 5490077184 | bytes 25989120 | tf_op jit(solution)/shard_map/td,fd->tf/dot_general | solution.py:1063
  296.4 13.9 %fusion.56 = (f32[512]{0:T(512)S(1)}, f32[512]{0:T(512)S(1)}, f32[512,1152]{1,0:T(8,128)}) fusion(f32[512,6912]{1,0:T(8,128)} %select_select_fusion, f32[512]{0:T(512)S(1)} %add_rsqrt_fusion, f32[512,1152]{1,0:T(8,128)S(1)} %get-tuple-element.107, f32[512]{0:T(512)S(1)} %broadcast_multiply_fusion.4, bf16[512,4608]{1,0:T(8,128)(2,1)S(1)} %get-tuple-element.102, ...), kind=kOutput, calls=%fused_computation.125 | convolution fusion | flops 5439945728 | bytes 22421504 | tf_op jit(solution)/shard_map/tf,df->td/dot_general | solution.py:1066
  311.6 13.0 %convolution_add_fusion = f32[512,1152]{1,0:T(8,128)S(1)} fusion(bf16[4608,1152]{1,0:T(8,128)(2,1)} %get-tuple-element.33, f32[1152]{0:T(1024)} %add.176, f32[512,4608]{1,0:T(8,128)} %fusion.9, f32[4608]{0:T(1024)} %add.171), kind=kOutput, calls=%fused_computation.33 | convolution fusion | flops 5460000768 | bytes 22436352 | tf_op jit(solution)/shard_map/dot_general | solution.py:1055
  324.6 6.2 convert_reduce_fusion.4
  331.9 4.6 convolution_convert_fusion.4.upstream_ref
  336.5 31.4 %shard_map.275 = (bf16[512,3456]{1,0:T(8,128)(2,1)}, f32[256,16,256]{2,1,0:T(8,128)}) custom-call(bf16[768,3456]{1,0:T(8,128)(2,1)} %get-tuple-element.34.placed_ref, bf16[3,16,256,256]{3,2,1,0:T(8,128)(2,1)} %get-tuple-element.35.weights_ref, bf16[512,1152]{1,0:T(8,128)(2,1)} %convolution_convert_fusion.4.upstream_ref, s32[1,512]{1,0:T(1,128)} %copy-done.5, ...), custom_call_target="tpu_custom_call" | custom-call | tf_op jit(solution)/shard_map/pallas_call | solution.py:182
  368.0 11.8 %fusion.57 = (f32[512]{0:T(512)S(1)}, f32[512]{0:T(512)S(1)}, f32[512,6912]{1,0:T(8,128)}, f32[512,1152]{1,0:T(8,128)S(1)}) fusion(f32[512,6912]{1,0:T(8,128)} %select_select_fusion, f32[512]{0:T(512)S(1)} %copy-done.39, f32[512]{0:T(512)S(1)} %copy-done.33, bf16[1,512,1152]{2,1,0:T(8,128)(2,1)S(1)} %copy-done.8, bf16[512,3456]{1,0:T(8,128)(2,1)} %get-tuple-element.36, ...), kind=kOutput, calls=%fused_computation.126 | convolution fusion | flops 4081581056 | bytes 19767296 | tf_op jit(solution)/shard_map/te,de->td/dot_general | solution.py:1090
  379.8 4.2 fusion.35
  391.5 7.8 %select_reduce_fusion.2 = (bf16[6912]{0:T(1024)(128)(2,1)S(1)}, bf16[6912]{0:T(1024)(128)(2,1)S(1)}, bf16[6912]{0:T(1024)(128)(2,1)S(1)}) fusion(f32[512,6912]{1,0:T(8,128)} %fusion.38, pred[512]{0:T(512)(128)(4,1)S(1)} %copy-done.46, pred[512]{0:T(512)(128)(4,1)S(1)} %copy-done.47, pred[512]{0:T(512)(128)(4,1)S(1)} %copy-done.44), kind=kLoop, calls=%fused_computation.6 | loop fusion | flops 21212928 | bytes 14198784 | tf_op jit(solution)/shard_map/reduce_sum | solution.py:1108
  400.3 12.5 %shard_map.276 = f32[128,128]{1,0:T(8,128)} custom-call(f32[256,16,256]{2,1,0:T(8,128)} %get-tuple-element.37.grad_ref, s32[256,256]{1,0:T(8,128)} %buckets_ref.3), custom_call_target="tpu_custom_call" | custom-call | tf_op jit(solution)/shard_map/pallas_call | solution.py:60
  417.3 8.6 %convolution_convert_fusion.1 = bf16[1152,4608]{1,0:T(8,128)(2,1)S(1)} fusion(bf16[512,1152]{1,0:T(8,128)(2,1)S(1)} %copy-done.25, bf16[512,4608]{1,0:T(8,128)(2,1)} %copy-done.49), kind=kOutput, calls=%fused_computation.2 | convolution fusion | flops 5441126400 | bytes 16515072 | tf_op jit(solution)/shard_map/td,tf->df/dot_general | solution.py:1065
  429.2 4.7 convolution_convert_fusion.2
  434.0 13.8 %pad_maximum_fusion.g12_ref = bf16[1152,9216]{1,0:T(8,128)(2,1)} fusion(bf16[1152,4608]{1,0:T(8,128)(2,1)S(1)} %convolution_convert_fusion.1, bf16[1152,1152]{1,0:T(8,128)(2,1)S(1)} %copy-done.17, bf16[1152,3456]{1,0:T(8,128)(2,1)S(1)} %convolution_convert_fusion.2), kind=kLoop, calls=%fused_computation | loop fusion | flops 63700992 | bytes 42467328 | tf_op jit(solution)/shard_map/concatenate | solution.py:1121
  447.8 13.2 %convolution_convert_fusion.g3_ref = bf16[4608,1152]{1,0:T(8,128)(2,1)} fusion(bf16[512,1152]{1,0:T(8,128)(2,1)S(1)} %copy-done.23, f32[512,4608]{1,0:T(8,128)} %fusion.9, f32[4608]{0:T(1024)S(1)} %copy-done.37), kind=kOutput, calls=%fused_computation.1 | convolution fusion | flops 5464719360 | bytes 21252096 | tf_op jit(solution)/shard_map/tf,td->fd/dot_general | solution.py:1062
  461.0 215.5 %shard_map.277 = (f32[72,9216]{1,0:T(8,128)}, f32[288,1152]{1,0:T(8,128)}, f32[200,128]{1,0:T(8,128)}, f32[72,6912]{1,0:T(8,128)}, f32[8,6912]{1,0:T(8,128)}, /*index=5*/f32[16,8,128]{2,1,0:T(8,128)}) custom-call(bf16[32,1152]{1,0:T(8,128)(2,1)} %fusion.49.mg_ref, f32[200,128]{1,0:T(8,128)} %pad_bitcast_fusion.vec_ref, f32[32,16,128]{2,1,0:T(8,128)} %copy-done.4, ...), custom_call_target="tpu_custom_call" | custom-call | tf_op jit(solution)/shard_map/pallas_call | solution.py:744
  (194 shorter events, 67.0 us)
Async XLA Ops:
  15.4 178.4 %copy-start.42 = (s32[1,512]{1,0:T(1,128)S(1)}, s32[1,512]{1,0:T(1,128)}, u32[]{:S(2)}) copy-start(s32[1,512]{1,0:T(1,128)} %param.19) | copy-start | bytes 6148
  193.3 9.7 %copy-start.4 = (f32[32,16,128]{2,1,0:T(8,128)}, f32[32,16,128]{2,1,0:T(8,128)S(1)}, u32[]{:S(2)}) copy-start(f32[32,16,128]{2,1,0:T(8,128)S(1)} %get-tuple-element.30.inbox_ref) | copy-start | bytes 786436
  193.3 13.5 %copy-start.26 = (f32[2,8,8,128]{3,1,2,0:T(8,128)}, f32[2,8,8,128]{3,1,2,0:T(8,128)S(1)}, u32[]{:S(2)}) copy-start(f32[2,8,8,128]{3,1,2,0:T(8,128)S(1)} %copy.92) | copy-start | bytes 196612
  206.8 10.4 %copy-start.21 = (bf16[512,1152]{1,0:T(8,128)(2,1)}, bf16[512,1152]{1,0:T(8,128)(2,1)S(1)}, u32[]{:S(2)}) copy-start(bf16[512,1152]{1,0:T(8,128)(2,1)S(1)} %fusion.29) | copy-start | bytes 3538948
  207.1 10.1 %copy-start.48 = (s32[1,512]{1,0:T(1,128)S(1)}, s32[1,512]{1,0:T(1,128)}, u32[]{:S(2)}) copy-start(s32[1,512]{1,0:T(1,128)} %param.20) | copy-start | bytes 6148
  207.1 10.2 %copy-start.30 = (bf16[16,961]{1,0:T(8,128)(2,1)S(1)}, bf16[16,961]{1,0:T(8,128)(2,1)}, u32[]{:S(2)}) copy-start(bf16[16,961]{1,0:T(8,128)(2,1)} %param.26) | copy-start | bytes 92260
  217.2 31.7 %copy-start.5 = (s32[1,512]{1,0:T(1,128)}, s32[1,512]{1,0:T(1,128)S(1)}, u32[]{:S(2)}) copy-start(s32[1,512]{1,0:T(1,128)S(1)} %multiply_add_fusion.frame_row_ref) | copy-start | bytes 6148
  217.4 31.5 %copy-start.2 = (s32[512,1]{1,0:T(8,128)}, s32[512,1]{1,0:T(8,128)S(1)}, u32[]{:S(2)}) copy-start(s32[512,1]{1,0:T(8,128)S(1)} %copy.64.frame_column_ref) | copy-start | bytes 6148
  234.1 14.8 %copy-start.7 = (bf16[1,512,1152]{2,1,0:T(8,128)(2,1)S(1)}, bf16[1,512,1152]{2,1,0:T(8,128)(2,1)}, u32[]{:S(2)}) copy-start(bf16[1,512,1152]{2,1,0:T(8,128)(2,1)} %param.17) | copy-start | bytes 3538948
  255.9 40.5 %copy-start.34 = (f32[512]{0:T(512)}, f32[512]{0:T(512)S(1)}, u32[]{:S(2)}) copy-start(f32[512]{0:T(512)S(1)} %add_rsqrt_fusion) | copy-start | bytes 6148
  261.4 13.1 %copy-start.24 = (bf16[512,1152]{1,0:T(8,128)(2,1)}, bf16[512,1152]{1,0:T(8,128)(2,1)S(1)}, u32[]{:S(2)}) copy-start(bf16[512,1152]{1,0:T(8,128)(2,1)S(1)} %get-tuple-element.109) | copy-start | bytes 3538948
  296.4 13.9 %copy-start.49 = (bf16[512,4608]{1,0:T(8,128)(2,1)}, bf16[512,4608]{1,0:T(8,128)(2,1)S(1)}, u32[]{:S(2)}) copy-start(bf16[512,4608]{1,0:T(8,128)(2,1)S(1)} %get-tuple-element.102) | copy-start | bytes 14155780
  311.6 13.0 %copy-start.9 = (f32[512,1152]{1,0:T(8,128)S(1)}, f32[512,1152]{1,0:T(8,128)}, u32[]{:S(2)}) copy-start(f32[512,1152]{1,0:T(8,128)} %get-tuple-element.122) | copy-start | bytes 7077892
  311.6 13.0 %copy-start.13 = (bf16[1,512,1152]{2,1,0:T(8,128)(2,1)S(1)}, bf16[1,512,1152]{2,1,0:T(8,128)(2,1)}, u32[]{:S(2)}) copy-start(bf16[1,512,1152]{2,1,0:T(8,128)(2,1)} %param.33) | copy-start | bytes 3538948
  311.6 13.0 %copy-start.35 = (f32[512]{0:T(512)S(1)}, f32[512]{0:T(512)}, u32[]{:S(2)}) copy-start(f32[512]{0:T(512)} %copy-done.34) | copy-start | bytes 6148
  311.6 13.0 %copy-start.40 = (f32[512]{0:T(512)S(1)}, f32[512]{0:T(512)}, u32[]{:S(2)}) copy-start(f32[512]{0:T(512)} %get-tuple-element.124) | copy-start | bytes 6148
  311.6 13.0 %copy-start.41 = (f32[512]{0:T(512)S(1)}, f32[512]{0:T(512)}, u32[]{:S(2)}) copy-start(f32[512]{0:T(512)} %get-tuple-element.125) | copy-start | bytes 6148
  336.5 31.5 %copy-start.8 = (bf16[1,512,1152]{2,1,0:T(8,128)(2,1)S(1)}, bf16[1,512,1152]{2,1,0:T(8,128)(2,1)}, u32[]{:S(2)}) copy-start(bf16[1,512,1152]{2,1,0:T(8,128)(2,1)} %param.17) | copy-start | bytes 3538948
  336.5 31.5 %copy-start.33 = (f32[512]{0:T(512)S(1)}, f32[512]{0:T(512)}, u32[]{:S(2)}) copy-start(f32[512]{0:T(512)} %copy-done.32) | copy-start | bytes 6148
  336.5 31.5 %copy-start.39 = (f32[512]{0:T(512)S(1)}, f32[512]{0:T(512)}, u32[]{:S(2)}) copy-start(f32[512]{0:T(512)} %copy-done.38) | copy-start | bytes 6148
  368.0 11.8 %copy-start.10 = (f32[512,1152]{1,0:T(8,128)S(1)}, f32[512,1152]{1,0:T(8,128)}, u32[]{:S(2)}) copy-start(f32[512,1152]{1,0:T(8,128)} %get-tuple-element.105) | copy-start | bytes 7077892
  433.9 13.9 %copy-start.23 = (bf16[512,1152]{1,0:T(8,128)(2,1)S(1)}, bf16[512,1152]{1,0:T(8,128)(2,1)}, u32[]{:S(2)}) copy-start(bf16[512,1152]{1,0:T(8,128)(2,1)} %get-tuple-element.100) | copy-start | bytes 3538948
  434.0 13.8 %copy-start.37 = (f32[4608]{0:T(1024)S(1)}, f32[4608]{0:T(1024)}, u32[]{:S(2)}) copy-start(f32[4608]{0:T(1024)} %add.171) | copy-start | bytes 55300
  461.0 216.5 %copy-start.29 = (bf16[1,3,1152]{2,1,0:T(4,128)(2,1)S(1)}, bf16[1,3,1152]{2,1,0:T(4,128)(2,1)}, u32[]{:S(2)}) copy-start(bf16[1,3,1152]{2,1,0:T(4,128)(2,1)} %param.18) | copy-start | bytes 20740
  (26 other events, 102.8 us)

commit v3 on v2

--- a/solution.py
+++ b/solution.py
@@ -1,4 +1,5 @@
 import functools
+import math
 
 import jax
 import jax.numpy as jnp
@@ -212,6 +213,43 @@
 full = jnp.float32
 
 
+def nt(left, right):
+    return lax.dot_general(left, right, (((1,), (1,)), ((), ())), preferred_element_type=full)
+
+
+def tn(left, right):
+    return lax.dot_general(left, right, (((0,), (0,)), ((), ())), preferred_element_type=full)
+
+
+def nn(left, right):
+    return lax.dot_general(left, right, (((1,), (0,)), ((), ())), preferred_element_type=full)
+
+
+def head_windows(heads, head_width):
+    found = []
+    for head in range(heads):
+        start = head * head_width
+        base = start // 128 * 128
+        stop = -(-(start + head_width) // 128) * 128
+        found.append((base, stop - base, start - base))
+    return found
+
+
+def lane_mask(rows, width, offset, head_width):
+    lane = lax.broadcasted_iota(jnp.int32, (rows, width), 1)
+    return (lane >= offset) & (lane < offset + head_width)
+
+
+def one_hot(shape, axis, index):
+    return (lax.broadcasted_iota(jnp.int32, shape, axis) == index).astype(full).astype(low)
+
+
+def normalize_rows(values):
+    center = values - jnp.mean(values, axis=-1, keepdims=True)
+    inverse = lax.rsqrt(jnp.mean(center * center, axis=-1, keepdims=True) + norm_epsilon)
+    return center * inverse, inverse
+
+
 class Place:
     def __init__(self):
         self.x = lax.axis_index("stream")
@@ -219,17 +257,30 @@
         self.z = self.d // 4
         self.y = (self.d // 2) % 2
         self.c = self.d % 2
+
     def zz(self, j):
         return (self.z, self.z + 1 - 2 * (self.z % 2), self.z + 2 - 4 * (self.z // 2), 3 - self.z)[j]
+
+    def source(self, i):
+        upper = self.z // 2
+        return (self.z, self.z + 1 - 2 * (self.z % 2), 2 - upper, 3 - 3 * upper)[i]
+
     def chip(self, j=0, yy=0):
         return self.zz(j) * 2 + (self.y if yy == 0 else 1 - self.y)
+
+    def far(self, i, yy=0):
+        return self.source(i) * 2 + (self.y if yy == 0 else 1 - self.y)
+
     def at(self, x=0, y=0, j=0, core=0):
         xx = self.x if x == 0 else 1 - self.x
         cc = self.c if core == 0 else 1 - self.c
         return (xx, self.chip(j, y) * 2 + cc)
 
-def gather_region(place, full_ref, w, chip, part):
-    c, x = place.c, place.x
+    def along(self, z):
+        return (self.x, z * 4 + self.y * 2 + self.c)
+
+
+def gather_region(x, c, full_ref, w, chip, part):
     if w < 2:
         off, size = {"all": (0, 2304), "ad": (1024 * x, 1280), "a": (1280 * x, 1024)}[part]
         col = pl.multiple_of(4608 * w + 2304 * c + off, 128)
@@ -238,208 +289,747 @@
     row = pl.multiple_of(c * 2304 + chip * 288 + off, 16)
     return full_ref[1].at[pl.ds(row, size), :]
 
+
 class Gather:
     def __init__(self, place, full_ref, send, recv):
-        self.place, self.full, self.send, self.recv = place, full_ref, send, recv
-    def copy(self, w, slot, region_src, device):
-        return pltpu.make_async_remote_copy(src_ref=region_src, dst_ref=region_src, send_sem=self.send.at[w, slot],
-            recv_sem=self.recv.at[w, slot], device_id=device, device_id_type=MESH)
-    def region(self, w, chip, part):
-        return gather_region(self.place, self.full, w, chip, part)
-    def desc(self, w, kind, j=0, yy=0, recv=False):
-        p = self.place
-        if kind == "z":
-            return self.copy(w, j - 1, self.region(w, p.chip(j if recv else 0), "ad"), p.at(j=j))
-        if kind == "y":
-            part = "all" if j == 0 else "ad"
-            return self.copy(w, 3 + j, self.region(w, p.chip(j, 1 if recv else 0), part), p.at(y=1))
-        if kind == "x":
-            if recv:
-                return self.copy(w, 7 + 2 * (j - 1) + yy, self.other_a(w, p.chip(j, yy)), p.at(x=1))
-            return self.copy(w, 7 + 2 * (j - 1) + yy, self.region(w, p.chip(j, yy), "a"), p.at(x=1))
-        if kind == "s":
-            slot = 13 + 2 * j + yy - 1
-            if recv:
-                return self.copy(w, slot, self.other_half(w, p.chip(j, yy)), p.at(core=1))
-            return self.copy(w, slot, self.region(w, p.chip(j, yy), "all"), p.at(core=1))
-    def other_a(self, w, chip):
-        q = type("Q", (), {})(); q.c, q.x = self.place.c, 1 - self.place.x
-        return gather_region(q, self.full, w, chip, "a")
-    def other_half(self, w, chip):
-        q = type("Q", (), {})(); q.c, q.x = 1 - self.place.c, self.place.x
-        return gather_region(q, self.full, w, chip, "all")
+        self.p, self.full, self.send, self.recv = place, full_ref, send, recv
+
+    def copy(self, w, out, into, region, device):
+        return pltpu.make_async_remote_copy(
+            src_ref=region,
+            dst_ref=region,
+            send_sem=self.send.at[w, out],
+            recv_sem=self.recv.at[w, into],
+            device_id=device,
+            device_id_type=MESH,
+        )
+
+    def region(self, w, chip, part, x=0, core=0):
+        p = self.p
+        return gather_region(
+            p.x if x == 0 else 1 - p.x, p.c if core == 0 else 1 - p.c, self.full, w, chip, part
+        )
+
+    def along(self, w, out, source, to):
+        p = self.p
+        return self.copy(w, out, source, self.region(w, source * 2 + p.y, "ad"), p.along(to))
+
+    def first(self, w, step):
+        p = self.p
+        to = jnp.clip(p.z + step, 0, 3)
+        return self.along(w, 21 if step > 0 else 22, p.z, to)
+
+    def onward(self, w, i):
+        p = self.p
+        source = p.source(i)
+        to = jnp.clip(jnp.where(source < p.z, p.z + 1, p.z - 1), 0, 3)
+        return self.along(w, i, source, to)
+
+    def over_y(self, w, i, recv=False):
+        p = self.p
+        region = self.region(w, p.far(i, 1 if recv else 0), "all" if i == 0 else "ad")
+        return self.copy(w, 4 + i, 4 + i, region, p.at(y=1))
+
+    def over_x(self, w, i, yy, recv=False):
+        p = self.p
+        slot = 8 + 2 * (i - 1) + yy
+        region = self.region(w, p.far(i, yy), "a", x=1 if recv else 0)
+        return self.copy(w, slot, slot, region, p.at(x=1))
+
+    def over_core(self, w, i, yy, recv=False):
+        p = self.p
+        slot = 13 + 2 * i + yy
+        region = self.region(w, p.far(i, yy), "all", core=1 if recv else 0)
+        return self.copy(w, slot, slot, region, p.at(core=1))
+
     def start(self, w):
-        for j in (1, 2, 3):
-            self.desc(w, "z", j).start()
-        self.desc(w, "y", 0).start()
-    def on_z(self, w, j):
-        self.desc(w, "z", j, recv=True).wait_recv()
-        self.desc(w, "x", j, 0).start()
-        self.desc(w, "y", j).start()
-    def on_y(self, w, j):
-        self.desc(w, "y", j, recv=True).wait_recv()
-        if j == 0:
-            self.desc(w, "s", 0, 1).start()
+        self.start_z(w)
+        self.over_y(w, 0).start()
+
+    def start_z(self, w):
+        p = self.p
+
+        @pl.when(p.z < 3)
+        def _():
+            self.first(w, 1).start()
+
+        @pl.when(p.z > 0)
+        def _():
+            self.first(w, -1).start()
+
+    def start_y(self, w):
+        self.over_y(w, 0).start()
+
+    def inner(self):
+        return (self.p.z == 1) | (self.p.z == 2)
+
+    def on_z(self, w, i):
+        p = self.p
+        self.along(w, i, p.source(i), p.z).wait_recv()
+
+        @pl.when(self.inner())
+        def _():
+            self.onward(w, i).start()
+
+        self.over_y(w, i).start()
+        self.over_x(w, i, 0).start()
+
+    def on_y(self, w, i):
+        self.over_y(w, i, True).wait_recv()
+        if i == 0:
+            self.over_core(w, 0, 1).start()
         else:
-            self.desc(w, "x", j, 1).start()
-    def on_x(self, w, j, yy):
-        self.desc(w, "x", j, yy, recv=True).wait_recv()
-        self.desc(w, "s", j, yy).start()
-    def on_s(self, w, j, yy):
-        self.desc(w, "s", j, yy, recv=True).wait_recv()
+            self.over_x(w, i, 1).start()
+
+    def on_x(self, w, i, yy):
+        self.over_x(w, i, yy, True).wait_recv()
+        self.over_core(w, i, yy).start()
+
+    def on_core(self, w):
+        for i in range(4):
+            for yy in (0, 1):
+                if (i, yy) != (0, 0):
+                    self.over_core(w, i, yy, True).wait_recv()
+
     def finish(self, w):
-        for j in (1, 2, 3):
-            self.desc(w, "z", j).wait_send()
-            self.desc(w, "y", j).wait_send()
+        p = self.p
+
+        @pl.when(p.z < 3)
+        def _():
+            self.first(w, 1).wait_send()
+
+        @pl.when(p.z > 0)
+        def _():
+            self.first(w, -1).wait_send()
+
+        @pl.when(self.inner())
+        def _():
+            for i in (1, 2, 3):
+                self.onward(w, i).wait_send()
+
+        for i in range(4):
+            self.over_y(w, i).wait_send()
             for yy in (0, 1):
-                self.desc(w, "x", j, yy).wait_send()
-                self.desc(w, "s", j, yy).wait_send()
-        self.desc(w, "y", 0).wait_send()
-        self.desc(w, "s", 0, 1).wait_send()
-
-def gather_kernel(note_ref, mod_ref, shard_ref, down_ref, full12_ref, full3_ref, inbox_ref, modulation_ref,
-                  sib, chip, msend, mrecv, csem, csend, crecv, send, recv, part, got0, got1, psend, precv):
+                if i > 0:
+                    self.over_x(w, i, yy).wait_send()
+                if (i, yy) != (0, 0):
+                    self.over_core(w, i, yy).wait_send()
+
+
+def select_rows(modulation_ref, slots, piece, width):
+    span = slice(piece * width, piece * width + width)
+    return jnp.where(
+        slots == 0,
+        modulation_ref[0:1, span],
+        jnp.where(slots == 1, modulation_ref[1:2, span], modulation_ref[2:3, span]),
+    )
+
+
+def forward_kernel(
+    heads,
+    note_ref,
+    bias_note_ref,
+    mod_in,
+    shard_ref,
+    tokens_in,
+    cotangent_in,
+    slots_ref,
+    frame_row_ref,
+    frame_column_ref,
+    table_ref,
+    buckets_ref,
+    down_ref,
+    full12_ref,
+    full3_ref,
+    hidden_one_out,
+    placed_out,
+    weights_out,
+    attended_out,
+    branch_out,
+    middle_out,
+    hidden_two_out,
+    act_out,
+    slope_out,
+    result_out,
+    mlp_grad_out,
+    inbox_ref,
+    modulation_ref,
+    gate_sum_ref,
+    mod_ref,
+    tokens_ref,
+    cotangent_ref,
+    sib,
+    chip_rows,
+    part,
+    got0,
+    got1,
+    bias_box,
+    bias_packed,
+    bias_out,
+    bias_up,
+    bias_down,
+    grid,
+    hidden_one,
+    placed,
+    weights,
+    mixed,
+    attended,
+    branch,
+    middle,
+    hidden_two,
+    act,
+    slope,
+    total,
+    small_out,
+    wide,
+    msend,
+    mrecv,
+    bsend,
+    brecv,
+    csem,
+    csend,
+    crecv,
+    psend,
+    precv,
+    send,
+    recv,
+    wsem,
+    osem,
+    psem,
+    isem,
+):
     place = Place()
     x, d, c = place.x, place.d, place.c
+    rows, width = tokens_ref.shape
+    places = buckets_ref.shape[0]
+    frames = placed.shape[0]
+    head_width = width // heads
+    scale = head_width ** (-0.5)
+    feed = act.shape[1]
+    inputs = [
+        pltpu.make_async_copy(mod_in, mod_ref, isem.at[0]),
+        pltpu.make_async_copy(tokens_in, tokens_ref, isem.at[1]),
+        pltpu.make_async_copy(cotangent_in, cotangent_ref, isem.at[2]),
+    ]
     barrier = pltpu.get_barrier_semaphore()
+
     def peer(t, k):
         return (x if t == 0 else 1 - x, (d + k) % 16)
-    for t in (0, 1):
-        for k in range(16):
-            if (t, k) != (0, 0):
-                pl.semaphore_signal(barrier, inc=1, device_id=peer(t, k), device_id_type=MESH)
-    pl.semaphore_wait(barrier, 31)
-    sib_copy = pltpu.make_async_remote_copy(src_ref=shard_ref, dst_ref=sib, send_sem=csend.at[0], recv_sem=crecv.at[0],
-        device_id=place.at(core=1), device_id_type=MESH)
-    sib_copy.start()
+
+    others = [(t, k) for t in (0, 1) for k in range(16) if (t, k) != (0, 0)]
+    for t, k in others:
+        pl.semaphore_signal(barrier, inc=1, device_id=peer(t, k), device_id_type=MESH)
     mine = full3_ref.at[pl.ds(pl.multiple_of(c * 2304 + place.chip() * 288, 16), 288), :]
     own3 = pltpu.make_async_copy(down_ref, mine, csem.at[0])
     own3.start()
-    theirs = full3_ref.at[pl.ds(pl.multiple_of((1 - c) * 2304 + place.chip() * 288, 16), 288), :]
-    def note(t, k, recv=False):
-        if recv:
+    for cp in inputs:
+        cp.start()
+    inbox_ref[x * 16 + d] = note_ref[d]
+    bias_box[d] = bias_note_ref[...]
+    pl.semaphore_wait(barrier, 31)
+
+    def remote(src, dst, s, r, device):
+        return pltpu.make_async_remote_copy(
+            src_ref=src, dst_ref=dst, send_sem=s, recv_sem=r, device_id=device, device_id_type=MESH
+        )
+
+    half_width = 4 * width
+
+    def sib_copy(w):
+        span = pl.ds(w * half_width, half_width)
+        return remote(
+            shard_ref.at[:, span], sib.at[:, span], csend.at[w], crecv.at[w], place.at(core=1)
+        )
+
+    sib_copy(0).start()
+
+    def note(t, k, recv_side=False):
+        if recv_side:
             src = (x if t == 0 else 1 - x) * 16 + (d + 16 - k) % 16
         else:
             src = x * 16 + d
-        return pltpu.make_async_remote_copy(src_ref=note_ref.at[(d + k) % 16], dst_ref=inbox_ref.at[src],
-            send_sem=msend.at[t, k], recv_sem=mrecv.at[t, k], device_id=peer(t, k), device_id_type=MESH)
-    for t in (0, 1):
-        for k in range(16):
-            if (t, k) != (0, 0):
-                note(t, k).start()
-    inbox_ref[x * 16 + d] = note_ref[d]
-    down_copy = pltpu.make_async_remote_copy(src_ref=down_ref, dst_ref=mine, send_sem=csend.at[1], recv_sem=crecv.at[1],
-        device_id=place.at(core=1), device_id_type=MESH)
-    down_copy.start()
-    sib_copy.wait()
+        return remote(
+            note_ref.at[(d + k) % 16], inbox_ref.at[src], msend.at[t, k], mrecv.at[t, k], peer(t, k)
+        )
+
+    def bias_note(k, recv_side=False):
+        src = (d + 16 - k) % 16 if recv_side else d
+        return remote(bias_note_ref, bias_box.at[src], bsend.at[k], brecv.at[k], peer(0, k))
+
+    for t, k in others:
+        note(t, k).start()
+    sib_copy(1).start()
+    down_copy = remote(down_ref, mine, csend.at[2], crecv.at[2], place.at(core=1))
     columns = 512
-    def assemble(i, _):
-        span = pl.ds(pl.multiple_of(i * columns, columns), columns)
-        own, other = shard_ref[0:72, span].astype(jnp.float32), sib[0:72, span].astype(jnp.float32)
-        top = jnp.where(c == 0, own, other)
-        bottom = jnp.where(c == 0, other, own)
-        chip[:, span] = jnp.concatenate([top, bottom], axis=0).astype(jnp.bfloat16)
-        return 0
-    lax.fori_loop(0, shard_ref.shape[1] // columns, assemble, 0)
-    own12 = pltpu.make_async_copy(chip, full12_ref.at[pl.ds(pl.multiple_of(place.chip() * 144, 16), 144), :], csem.at[1])
-    own12.start()
-    own12.wait()
-    own3.wait()
+
+    def assemble(w):
+        def body(i, _):
+            span = pl.ds(pl.multiple_of(i * columns, columns), columns)
+            own, other = shard_ref[0:72, span].astype(full), sib[0:72, span].astype(full)
+            top = jnp.where(c == 0, own, other)
+            bottom = jnp.where(c == 0, other, own)
+            chip_rows[:, span] = jnp.concatenate([top, bottom], axis=0).astype(low)
+            return 0
+
+        sib_copy(w).wait()
+        first = w * half_width // columns
+        lax.fori_loop(first, first + half_width // columns, body, 0)
+        to = pl.ds(pl.multiple_of(place.chip() * 144, 16), 144)
+        span = pl.ds(w * half_width, half_width)
+        return pltpu.make_async_copy(
+            chip_rows.at[:, span], full12_ref.at[to, span], csem.at[1 + w]
+        )
+
     g = Gather(place, (full12_ref, full3_ref), send, recv)
-    g.start(0)
-    for t in (0, 1):
-        for k in range(16):
-            if (t, k) != (0, 0):
-                note(t, k, recv=True).wait_recv()
-    lhs = inbox_ref[pl.ds(x * 16, 16), 0:8, :].reshape(128, 128).astype(jnp.bfloat16)
-    cols = 768
-    def project(i, _):
-        span = pl.ds(pl.multiple_of(i * cols, cols), cols)
-        out = jnp.dot(lhs, mod_ref[:, span], preferred_element_type=jnp.float32)
+    own1 = assemble(0)
+    own1.start()
+    own1.wait()
+
+    def bias_grid(first, last):
+        def body(h, _):
+            for half in range(places // 128):
+                span = slice(128 * half, 128 * half + 128)
+                index = buckets_ref[:, span]
+                lower, upper = index & 127, index >> 7
+                found = jnp.zeros(index.shape, full)
+                for chunk in range(table_ref.shape[1]):
+                    row = jnp.broadcast_to(table_ref[h, chunk : chunk + 1], index.shape)
+                    value = jnp.take_along_axis(row, lower, axis=1)
+                    found = jnp.where(upper == chunk, value, found)
+                grid[h, :, span] = found.astype(low)
+            return 0
+
+        lax.fori_loop(first, last, body, 0)
+
+    def project_condition():
+        for t, k in others:
+            note(t, k, True).wait_recv()
+        left = inbox_ref[pl.ds(x * 16, 16)].reshape(128, 128).astype(low)
+        cols = 768
+
+        def body(i, _):
+            span = pl.ds(pl.multiple_of(i * cols, cols), cols)
+            out = nn(left, mod_ref[:, span])
+            for chip_at in range(8):
+                for core in range(2):
+                    dest = (chip_at * 2 + core) * 8
+                    part[core, chip_at, :, span] = out[dest : dest + 4]
+            return 0
+
+        lax.fori_loop(0, mod_ref.shape[1] // cols, body, 0)
+        half().start()
+
+    def half():
+        return remote(part.at[1 - c], got0, psend.at[0], precv.at[0], place.at(core=1))
+
+    def share_condition():
+        half().wait()
         for chip_at in range(8):
-            for core in range(2):
-                dest = (chip_at * 2 + core) * 8
-                part[core, chip_at, :, span] = out[dest : dest + 4]
-        return 0
-    lax.fori_loop(0, mod_ref.shape[1] // cols, project, 0)
-    half = pltpu.make_async_remote_copy(src_ref=part.at[1 - c], dst_ref=got0, send_sem=psend.at[0], recv_sem=precv.at[0],
-        device_id=place.at(core=1), device_id_type=MESH)
-    half.start()
-    half.wait()
-    for chip_at in range(8):
-        part[c, chip_at] += got0[chip_at]
+            part[c, chip_at] += got0[chip_at]
+        for k in range(1, 8):
+            share(k).start()
+
     def share(k):
         dest = (place.chip() + k) % 8
-        return pltpu.make_async_remote_copy(src_ref=part.at[c, dest], dst_ref=got1.at[k - 1], send_sem=psend.at[k], recv_sem=precv.at[k],
-            device_id=(x, dest * 2 + c), device_id_type=MESH)
-    for k in range(1, 8):
-        share(k).start()
-    for j in (1, 2, 3):
-        g.on_z(0, j)
-    g.start(1)
-    for k in range(1, 8):
-        share(k).wait_recv()
-    total = part[c, place.chip()]
-    for k in range(1, 8):
-        total += got1[k - 1]
-    modulation_ref[...] = total
+        return remote(
+            part.at[c, dest], got1.at[k - 1], psend.at[k], precv.at[k], (x, dest * 2 + c)
+        )
+
+    def finish_condition():
+        for k in range(1, 16):
+            bias_note(k, True).wait_recv()
+        bias_packed[...] = jnp.zeros_like(bias_packed)
+        for at in range(16):
+            box = bias_box[at]
+            q = 144 * at + (width if at >= 8 else 0)
+            bias_packed[0:1, q : q + 144] = box[1:2, 0:144]
+            bias_out[0:1, 72 * at : 72 * at + 72] = box[2:3, 0:72]
+            u = (at % 2) * (feed // 2) + (at // 2) * 288
+            bias_up[0:1, u : u + 288] = box[3:4, 0:288]
+            bias_down[0:1, 72 * at : 72 * at + 72] = box[4:5, 0:72]
+            modulation_ref[0:1, 432 * at : 432 * at + 432] = box[0:1, 0:432]
+        for k in range(1, 8):
+            share(k).wait_recv()
+        summed = part[c, place.chip()]
+        for k in range(1, 8):
+            summed += got1[k - 1]
+        modulation_ref[...] = summed + modulation_ref[0:1, :]
+
+    def copy_out(n, src, dst):
+        return pltpu.make_async_copy(src, dst, osem.at[n])
+
+    outs = []
+
+    def put(src, dst):
+        cp = copy_out(len(outs), src, dst)
+        cp.start()
+        outs.append(cp)
+
+    step = 64
+
+    def row_loop(first, last, body):
+        def run(i, _):
+            body(pl.ds(pl.multiple_of(i * step, step), step))
+            return 0
+
+        lax.fori_loop(first // step, last // step, run, 0)
+
+    def norm_one(first, last):
+        def body(span):
+            normed, _ = normalize_rows(tokens_ref[span, :].astype(full))
+            slots = slots_ref[span, :]
+            shift = select_rows(modulation_ref, slots, 0, width)
+            grow = select_rows(modulation_ref, slots, 1, width)
+            hidden_one[span, :] = (normed * (1.0 + grow) + shift).astype(low)
+            gate = select_rows(modulation_ref, slots, 5, width)
+            small_out[span, :] = (gate * cotangent_ref[span, :].astype(full)).astype(low)
+
+        row_loop(first, last, body)
+
+    loads = []
+
+    def fetch(src):
+        n = len(loads)
+        cp = pltpu.make_async_copy(src, wide.at[n % 2], wsem.at[n % 2])
+        cp.start()
+        loads.append(cp)
+        return n
+
+    def loaded(n):
+        loads[n].wait()
+        return wide.at[n % 2]
+
+    tile = 384
+
+    def w12(at):
+        return full12_ref.at[:, pl.ds(at, width)]
+
+    def project(n, piece):
+        weight = loaded(n)
+        where = one_hot((frames, rows), 0, frame_row_ref[...])
+
+        def body(i, _):
+            span = pl.ds(pl.multiple_of(i * tile, 128), tile)
+            to = pl.ds(pl.multiple_of(piece * width + i * tile, 128), tile)
+            out = nn(hidden_one[...], weight[:, span]) + bias_packed[0:1, to]
+            placed[:, to] = nn(where, out.astype(low)).astype(low)
+            return 0
+
+        lax.fori_loop(0, width // tile, body, 0)
+
+    windows = head_windows(heads, head_width)
+
+    def attend(first, last):
+        where = one_hot((frames, rows), 0, frame_row_ref[...])
+        filled = nt(jnp.ones((8, rows), low), where)[0:1] > 0.5
+        for head in range(first, last):
+            base, wide_at, offset = windows[head]
+            mask = lane_mask(places, wide_at, offset, head_width)
+            slot = head % 2
+            if head >= 2:
+                weight_copy(head - 2).wait()
+            for image in range(frames // places):
+                at = slice(image * places, image * places + places)
+                spans = [
+                    slice(p * width + base, p * width + base + wide_at) for p in range(3)
+                ]
+                query = placed[at, spans[0]]
+                query = jnp.where(mask, query, jnp.zeros_like(query))
+                scores = nt(query, placed[at, spans[1]]) * scale + grid[head].astype(full)
+                scores = jnp.where(filled[:, at], scores, masked_score)
+                exponent = jnp.exp(scores - jnp.max(scores, axis=-1, keepdims=True))
+                share_of = (exponent / jnp.sum(exponent, axis=-1, keepdims=True)).astype(low)
+                weights[slot, image] = share_of
+                mixture = nn(share_of, placed[at, spans[2]]).astype(low)
+                mixed[at, spans[0]] = jnp.where(mask, mixture, mixed[at, spans[0]])
+            weight_copy(head).start()
+
+    def weight_copy(head):
+        return pltpu.make_async_copy(weights.at[head % 2], weights_out.at[head], psem.at[head % 2])
+
+    def gather_back():
+        back = one_hot((rows, frames), 1, frame_column_ref[...])
+        attended[...] = nn(back, mixed[...]).astype(low)
+
+    def out_project(n):
+        weight = loaded(n)
+
+        def body(i, _):
+            span = pl.ds(pl.multiple_of(i * tile, 128), tile)
+            branch[:, span] = nn(attended[...], weight[:, span]) + bias_out[0:1, span]
+            return 0
+
+        lax.fori_loop(0, width // tile, body, 0)
+
+    def norm_two():
+        def body(span):
+            slots = slots_ref[span, :]
+            gate = select_rows(modulation_ref, slots, 2, width)
+            mid = tokens_ref[span, :].astype(full) + gate * branch[span, :]
+            middle[span, :] = mid
+            normed, _ = normalize_rows(mid)
+            shift = select_rows(modulation_ref, slots, 3, width)
+            grow = select_rows(modulation_ref, slots, 4, width)
+            hidden_two[span, :] = (normed * (1.0 + grow) + shift).astype(low)
+
+        row_loop(0, rows, body)
+
+    root = math.sqrt(2.0 / math.pi)
+
+    def up(n, piece):
+        weight = loaded(n)
+
+        def body(i, _):
+            span = pl.ds(pl.multiple_of(i * tile, 128), tile)
+            to = pl.ds(pl.multiple_of(piece * width + i * tile, 128), tile)
+            v = nn(hidden_two[...], weight[:, span]) + bias_up[0:1, to]
+            square = v * v
+            bend = jnp.tanh(root * (v + 0.044715 * (v * square)))
+            half = 0.5 * (1.0 + bend)
+            act[:, to] = (v * half).astype(low)
+            rise = root * (1.0 + (3.0 * 0.044715) * square)
+            slope[:, to] = (half + 0.5 * v * (1.0 - bend * bend) * rise).astype(low)
+            return 0
+
+        lax.fori_loop(0, width // tile, body, 0)
+
+    def down(n, piece):
+        weight = loaded(n)
+
+        def body(i, _):
+            span = pl.ds(pl.multiple_of(i * tile, 128), tile)
+            out = nn(act[:, piece * width : piece * width + width], weight[:, span])
+            if piece == 0:
+                total[:, span] = out + bias_down[0:1, span]
+            else:
+                total[:, span] += out
+            return 0
+
+        lax.fori_loop(0, width // tile, body, 0)
+
+    def finish_rows():
+        gate_sum_ref[...] = jnp.zeros_like(gate_sum_ref)
+
+        def body(span):
+            slots = slots_ref[span, :]
+            gate = select_rows(modulation_ref, slots, 5, width)
+            out = total[span, :]
+            hidden_one[span, :] = (middle[span, :] + gate * out).astype(low)
+            product = out * cotangent_ref[span, :].astype(full)
+            for slot in range(3):
+                gate_sum_ref[slot : slot + 1, :] += jnp.sum(
+                    jnp.where(slots == slot, product, 0.0), axis=0, keepdims=True
+                )
+
+        row_loop(0, rows, body)
+
+    g.start_z(0)
+    g.start_y(0)
+    own2 = assemble(1)
+    own2.start()
+    for k in range(1, 16):
+        bias_note(k).start()
+    down_copy.start()
+    own3.wait()
+    own2.wait()
+    g.start_z(1)
+    g.on_z(0, 1)
+    g.on_z(1, 1)
+    g.on_z(0, 2)
+    g.on_y(0, 1)
+    g.on_x(1, 1, 0)
+    g.on_z(0, 3)
+    g.start_y(1)
+    inputs[0].wait()
+    project_condition()
+    g.start_z(2)
+    g.on_x(0, 1, 1)
+    g.on_x(0, 1, 0)
+    share_condition()
+    g.on_y(0, 2)
+    bias_grid(0, 6)
+    g.on_y(0, 3)
+    g.on_x(0, 3, 0)
+    bias_grid(6, 9)
+    g.on_x(0, 2, 0)
+    g.on_x(0, 2, 1)
+    g.on_y(1, 1)
+    g.on_z(1, 2)
+    finish_condition()
+    bias_grid(9, 13)
+    inputs[1].wait()
+    inputs[2].wait()
+    norm_one(0, rows // 2)
+    g.on_x(0, 3, 1)
+    g.on_z(1, 3)
+    bias_grid(13, heads)
     g.on_y(0, 0)
-    for j in (1, 2, 3):
-        g.on_y(0, j)
-    for j in (1, 2, 3):
-        g.on_z(1, j)
-    for j in (1, 2, 3):
-        g.on_x(0, j, 0)
+    g.on_core(0)
+    norm_one(rows // 2, rows)
+    put(hidden_one, hidden_one_out)
+    put(small_out, mlp_grad_out)
+    g.on_z(2, 1)
+    g.on_y(1, 2)
+    g.on_y(1, 0)
+    a = fetch(w12(0))
+    b = fetch(w12(width))
+    project(a, 0)
+    a = fetch(w12(2 * width))
+    g.on_z(2, 2)
+    project(b, 1)
+    b = fetch(w12(3 * width))
+    g.on_y(1, 3)
+    g.on_x(1, 1, 1)
+    g.start_y(2)
+    project(a, 2)
+    put(placed, placed_out)
+    mixed[...] = jnp.zeros_like(mixed)
+    attend(0, 3)
+    g.on_z(2, 3)
+    attend(3, 6)
+    attend(6, 10)
+    g.on_x(1, 2, 1)
+    g.on_x(1, 3, 0)
+    g.on_x(1, 2, 0)
+    g.on_y(2, 2)
+    attend(10, 13)
+    g.on_x(2, 2, 0)
+    attend(13, heads)
+    g.on_x(2, 1, 0)
+    g.on_y(2, 1)
+    g.on_x(1, 3, 1)
+    gather_back()
+    put(attended, attended_out)
+    out_project(b)
+    put(branch, branch_out)
+    norm_two()
+    put(middle, middle_out)
+    put(hidden_two, hidden_two_out)
+    g.on_core(1)
+    a = fetch(w12(4 * width))
+    b = fetch(w12(5 * width))
+    g.on_y(2, 3)
+    g.on_x(2, 2, 1)
+    up(a, 0)
+    a = fetch(w12(6 * width))
+    up(b, 1)
+    b = fetch(w12(7 * width))
+    g.on_x(2, 3, 0)
+    g.on_y(2, 0)
+    up(a, 2)
+    g.on_x(2, 1, 1)
+    g.on_x(2, 3, 1)
+    up(b, 3)
+    put(act, act_out)
+    put(slope, slope_out)
+    g.on_core(2)
     down_copy.wait()
-    g.start(2)
-    for j in (1, 2, 3):
-        g.on_x(0, j, 1)
-    g.on_y(1, 0)
-    for j in (1, 2, 3):
-        g.on_y(1, j)
-    for j in (1, 2, 3):
-        g.on_z(2, j)
-    for yy in (0, 1):
-        for j in (1, 2, 3):
-            g.on_x(1, j, yy)
-    g.on_y(2, 0)
-    for j in (1, 2, 3):
-        g.on_y(2, j)
-    for yy in (0, 1):
-        for j in (1, 2, 3):
-            g.on_x(2, j, yy)
+    outs[0].wait()
+    pieces = feed // width
+    a = fetch(full3_ref.at[pl.ds(0, width), :])
+    for piece in range(pieces):
+        if piece + 1 < pieces:
+            b = fetch(full3_ref.at[pl.ds((piece + 1) * width, width), :])
+        down(a, piece)
+        a = b
+    finish_rows()
+    put(hidden_one, result_out)
+    for cp in outs[1:]:
+        cp.wait()
+    weight_copy(heads - 2).wait()
+    weight_copy(heads - 1).wait()
     for w in range(3):
-        for j in range(4):
-            for yy in (0, 1):
-                if (j, yy) != (0, 0):
-                    g.on_s(w, j, yy)
         g.finish(w)
-    for t in (0, 1):
-        for k in range(16):
-            if (t, k) != (0, 0):
-                note(t, k).wait_send()
+    for t, k in others:
+        note(t, k).wait_send()
+    for k in range(1, 16):
+        bias_note(k).wait_send()
     for k in range(1, 8):
         share(k).wait_send()
 
-def gather_weights(notes, modulator, shard12, down):
+
+def forward_pass(heads, notes, bias_note, modulator, shard12, tokens, cotangent, slots, frame, table, buckets, down):
+    rows, width = tokens.shape
+    feed = 4 * width
+    places = buckets.shape[0]
+    frames = 3 * places
     any_, vm = pl.BlockSpec(memory_space=pl.ANY), pl.BlockSpec(memory_space=pltpu.VMEM)
-    width = modulator.shape[1]
+    V, D, S = pltpu.VMEM, pltpu.SemaphoreType.DMA, jax.ShapeDtypeStruct
+    count = table.shape[1]
+    chunks = -(-count // 128)
+    table = jnp.pad(table.astype(full), ((0, 0), (0, chunks * 128 - count)))
+    table = table.reshape(heads, chunks, 128)
     return pl.pallas_call(
-        gather_kernel,
-        out_shape=(jax.ShapeDtypeStruct((1152, 9216), low), jax.ShapeDtypeStruct((4608, 1152), low),
-                   jax.ShapeDtypeStruct((32, 16, 128), full), jax.ShapeDtypeStruct((4, width), full)),
-        in_specs=[vm, vm, vm, any_],
-        out_specs=(any_, any_, vm, vm),
+        functools.partial(forward_kernel, heads),
+        out_shape=(
+            S((width, 2 * feed), low),
+            S((feed, width), low),
+            S((rows, width), low),
+            S((frames, 3 * width), low),
+            S((heads, 3, places, places), low),
+            S((rows, width), low),
+            S((rows, width), full),
+            S((rows, width), full),
+            S((rows, width), low),
+            S((rows, feed), low),
+            S((rows, feed), low),
+            S((rows, width), low),
+            S((rows, width), low),
+            S((32, 8, 128), full),
+            S((4, 6 * width), full),
+            S((8, width), full),
+        ),
+        in_specs=[vm, vm, any_, vm, any_, any_] + [vm] * 6,
+        out_specs=(any_,) * 13 + (vm,) * 3,
         scratch_shapes=[
-            pltpu.VMEM(shard12.shape, low), pltpu.VMEM((144, shard12.shape[1]), low),
-            pltpu.SemaphoreType.DMA((2, 16)), pltpu.SemaphoreType.DMA((2, 16)),
-            pltpu.SemaphoreType.DMA((2,)), pltpu.SemaphoreType.DMA((2,)), pltpu.SemaphoreType.DMA((2,)),
-            pltpu.SemaphoreType.DMA((3, 20)), pltpu.SemaphoreType.DMA((3, 20)),
-            pltpu.VMEM((2, 8, 4, width), full), pltpu.VMEM((8, 4, width), full), pltpu.VMEM((7, 4, width), full),
-            pltpu.SemaphoreType.DMA((8,)), pltpu.SemaphoreType.DMA((8,)),
+            V(modulator.shape, low),
+            V(tokens.shape, low),
+            V(tokens.shape, low),
+            V(shard12.shape, low),
+            V((144, shard12.shape[1]), low),
+            V((2, 8, 4, 6 * width), full),
+            V((8, 4, 6 * width), full),
+            V((7, 4, 6 * width), full),
+            V((16,) + bias_note.shape, full),
+            V((1, 3 * width), full),
+            V((1, width), full),
+            V((1, feed), full),
+            V((1, width), full),
+            V((heads, places, places), low),
+            V((rows, width), low),
+            V((frames, 3 * width), low),
+            V((2, 3, places, places), low),
+            V((frames, width), low),
+            V((rows, width), low),
+            V((rows, width), full),
+            V((rows, width), full),
+            V((rows, width), low),
+            V((rows, feed), low),
+            V((rows, feed), low),
+            V((rows, width), full),
+            V((rows, width), low),
+            V((2, width, width), low),
+            D((2, 16)),
+            D((2, 16)),
+            D((16,)),
+            D((16,)),
+            D((3,)),
+            D((3,)),
+            D((3,)),
+            D((8,)),
+            D((8,)),
+            D((3, 23)),
+            D((3, 23)),
+            D((2,)),
+            D((16,)),
+            D((2,)),
+            D((3,)),
         ],
-        compiler_params=pltpu.CompilerParams(collective_id=0, has_side_effects=True, vmem_limit_bytes=40 * 2**20),
-    )(notes, modulator, shard12, down)
+        compiler_params=pltpu.CompilerParams(
+            collective_id=0, has_side_effects=True, vmem_limit_bytes=63 * 2**20
+        ),
+    )(notes, bias_note, modulator, shard12, tokens, cotangent, slots[:, None], frame[None, :], frame[:, None], table, buckets, down)
+
 
 def feed_order(values, axis, chips):
     shape = values.shape
@@ -671,7 +1261,7 @@
         shape = (devices * 16, devices * 8)
         r, q = lax.broadcasted_iota(jnp.int32, shape, 0), lax.broadcasted_iota(jnp.int32, shape, 1)
         return ((r // 16 == q // 8) & (r % 16 - base == q % 8) & (q % 8 < 3)).astype(full).astype(low)
-    act = inbox_ref[:, 0:8, :].reshape(256, 128).astype(low)
+    act = inbox_ref[...].reshape(256, 128).astype(low)
     cond_total = jnp.zeros((128, 128), full)
     for p in range(6):
         tile = 0 if p >= 2 else 1
@@ -1002,33 +1592,52 @@
         activated.astype(full).reshape(images, devices, shard).transpose(1, 0, 2),
         ((0, 0), (0, 8 - images), (0, 128 - shard)),
     )
-    joined = jnp.concatenate(bias_parts).astype(full)
-    joined = jnp.pad(joined, (0, 1024 - joined.shape[0])).reshape(1, 8, 128)
-    notes = jnp.concatenate([slices, jnp.broadcast_to(joined, (devices, 8, 128))], axis=1)
+    notes = slices
+    bias_note = jnp.stack(
+        [jnp.pad(part.astype(full), (0, 512 - part.shape[0])) for part in bias_parts]
+    )
+    bias_note = jnp.pad(bias_note, ((0, 8 - len(bias_parts)), (0, 0)))
     chips = devices // 2
     shard12 = jnp.pad(
         jnp.concatenate([projector, output_weight, feed_order(up_weight, 1, chips)], axis=1),
         ((0, 8), (0, 0)),
     )
     wide_modulator = jnp.pad(modulator, ((0, 128 - shard), (0, 0)))
-    full12, down_all, inbox, modulation = gather_weights(
-        notes, wide_modulator, shard12, down_weight
-    )
-    bias_all = lax.dynamic_slice(inbox, (stream_index * devices, 8, 0), (devices, 8, 128)).reshape(
-        devices, 1024
-    )
-    bias_full = []
-    start = 0
-    for part in bias_parts:
-        bias_full.append(bias_all[:, start : start + part.shape[0]].reshape(-1))
-        start += part.shape[0]
-    bias_full[3] = feed_order(bias_full[3], 0, chips)
-    modulation = modulation[:3] + bias_full[0]
+    (
+        full12,
+        down_all,
+        hidden_one,
+        placed,
+        weights,
+        attended,
+        branch_attn,
+        middle,
+        hidden_two,
+        activation_low,
+        slope,
+        result,
+        mlp_grad,
+        inbox,
+        modulation,
+        gate_sums,
+    ) = forward_pass(
+        heads,
+        notes,
+        bias_note,
+        wide_modulator,
+        shard12,
+        tokens[0],
+        cotangent[0],
+        slot_ids,
+        slot_ids * image_tokens + places,
+        position_table,
+        buckets,
+        down_weight,
+    )
     packed_width = 3 * model_width
     projector_all = full12[:, :packed_width]
     output_all = full12[:, packed_width : 4 * model_width]
     up_all = full12[:, 4 * model_width :]
-    grid = bias_grid(position_table, buckets)
     local = slot_ids[:, None]
     per_token = jnp.where(
         local == 0, modulation[0:1], jnp.where(local == 1, modulation[1:2], modulation[2:3])
@@ -1037,31 +1646,12 @@
         per_token, 6, axis=1
     )
     normed_one, inverse_one = normalize(inputs)
-    hidden_one = (normed_one * (1.0 + scale_attn) + shift_attn).astype(low)
-    packed_bias = jnp.concatenate(
-        [bias_full[1][:model_width], jnp.zeros((model_width,), full), bias_full[1][model_width:]]
-    )
-    packed = (
-        jnp.dot(hidden_one, projector_all, preferred_element_type=full) + packed_bias
-    ).astype(low)
-    attended, placed, weights = attend_forward(packed, slot_ids, places, grid)
-    branch_attn = jnp.dot(attended, output_all, preferred_element_type=full) + bias_full[2]
-    middle = inputs + gate_attn * branch_attn
     normed_two, inverse_two = normalize(middle)
-    hidden_two = (normed_two * (1.0 + scale_mlp) + shift_mlp).astype(low)
-    up_output = jnp.dot(hidden_two, up_all, preferred_element_type=full) + bias_full[3]
-    activation, gelu_back = jax.vjp(lambda v: jax.nn.gelu(v, approximate=True), up_output)
-    activation_low = activation.astype(low)
-    branch_mlp = jnp.dot(activation_low, down_all, preferred_element_type=full) + bias_full[4]
-    result = (middle + gate_mlp * branch_mlp).astype(low)
-
     upstream = cotangent[0].astype(full)
-    mlp_grad = (gate_mlp * upstream).astype(low)
-    gate_mlp_grad = branch_mlp * upstream
 
     down_grad = jnp.einsum("tf,td->fd", activation_low, mlp_grad, preferred_element_type=full)
     activation_grad = jnp.einsum("td,fd->tf", mlp_grad, down_all, preferred_element_type=full)
-    up_grad_low = gelu_back(activation_grad)[0].astype(low)
+    up_grad_low = (activation_grad * slope.astype(full)).astype(low)
     up_grad = jnp.einsum("td,tf->df", hidden_two, up_grad_low, preferred_element_type=full)
     hidden_two_grad = jnp.einsum(
         "tf,df->td", up_grad_low, up_all, preferred_element_type=full
@@ -1075,7 +1665,7 @@
     attended_grad = jnp.einsum(
         "te,de->td", attn_grad, output_all, preferred_element_type=full
     ).astype(low)
-    packed_grad, grid_grad = attend_backward(placed, weights, attended_grad, slot_ids, places)
+    packed_grad, grid_grad = attend_backward(placed, jnp.swapaxes(weights, 0, 1), attended_grad, slot_ids, places)
     projector_grad = jnp.einsum("td,te->de", hidden_one, packed_grad, preferred_element_type=full)
     table_grad = table_histogram(grid_grad, buckets, bucket_count)
     packed_sums = jnp.sum(packed_grad.astype(full), axis=0)
@@ -1100,13 +1690,13 @@
             gate_attn_grad,
             hidden_two_grad,
             hidden_two_grad * normed_two,
-            gate_mlp_grad,
         ],
         axis=1,
     )
     modulation_grad = jnp.stack(
         [jnp.sum(jnp.where(local == slot, token_mod_grad, 0.0), axis=0) for slot in range(images)]
-    ).astype(low)
+    )
+    modulation_grad = jnp.concatenate([modulation_grad, gate_sums[:images]], axis=1).astype(low)
     mg = modulation_grad.reshape(images, 6, model_width).transpose(1, 0, 2)
     mg = mg.reshape(6 * images, model_width)
     late = 2 * images

time: 709 us -> 615 us (0.87)
  matrix products: 118 us -> 68.6 us
  Pallas kernels: 467 us -> 437 us
  other arithmetic: 60.9 us -> 47.8 us
    dot_general x4 -> x0, matrix products: 41.8 us -> none  [the longest x1 13.1 us: own_shards(): jnp.dot(hidden_two, up_all, preferred_element_type=full) + bias_full[3]]
    pallas_call x3 -> x1, Pallas kernels: 207 us -> 172 us  [forward_pass(): pl.pallas_call(functools.partial(forward_kernel, heads), out_shape=(S((wi...]
where the time goes in v3:
time: 615 us; the launch traced here: 605 us
  Pallas kernels  437 us (71%)
  matrix products  68.6 us (11%)
  local copies, waits for them, and re-layouts  50.2 us (8%)
  other arithmetic  47.8 us (8%)
    pallas_call x1, Pallas kernels, scatter_grads(): pl.pallas_call(functools.partial(scatter_kernel, None), out_shape=(S((72,...  220 us
    pallas_call x1, Pallas kernels, forward_pass(): pl.pallas_call(functools.partial(forward_kernel, heads), out_shape=(S((wi...  172 us
    pallas_call x1, Pallas kernels, attend_backward(): pl.pallas_call(functools.partial(attend_backward_kernel, heads), out_shap...  31.6 us
    concatenate x1, other arithmetic, own_shards(): jnp.concatenate([projector_grad, output_grad, up_grad], axis=1).astype(low)  13.9 us
    dot_general x1, matrix products, own_shards(): jnp.einsum('td,fd->tf', mlp_grad, down_all, preferred_element_type=full)  13.7 us
    pallas_call x1, Pallas kernels, table_histogram(): pl.pallas_call(hist_kernel, grid=(places // step,), in_specs=[pl.BlockSpe...  12.7 us

profile of v3, /device:TPU:9, one launch (start us, length us, event | category | flops | bytes accessed | tf_op | source)
XLA Modules:
  0.0 604.8 jit_solution(16452458704943346423)
XLA Ops:
  6.2 2.5 pad.70.mod_in.mod_ref
  14.9 172.0 %shard_map.272 = (bf16[1152,9216]{1,0:T(8,128)(2,1)}, bf16[4608,1152]{1,0:T(8,128)(2,1)}, bf16[512,1152]{1,0:T(8,128)(2,1)}, bf16[768,3456]{1,0:T(8,128)(2,1)}, ...) custom-call(f32[16,8,128]{2,1,0:T(8,128)} %pad_convert_fusion.note_r, ...), custom_call_target="tpu_custom_call" | custom-call | tf_op jit(solution)/shard_map/pallas_call | solution.py:962
  188.7 8.1 %select_select_fusion = f32[512,6912]{1,0:T(8,128)} fusion(f32[6912]{0:T(1024)S(1)} %get-tuple-element.112, f32[6912]{0:T(1024)S(1)} %get-tuple-element.113, f32[6912]{0:T(1024)S(1)} %get-tuple-element.111, pred[512]{0:T(512)(128)(4,1)S(1)} %get-tuple-element.116, pred[512]{0:T(512)(128)(4,1)S(1)} %get-tuple-element.115), kind=kLoop, calls=%fused_computation.4 | loop fusion | flops 7077888 | bytes 14239744 | tf_op jit(solution)/shard_map/jit(_where)/select_n | solution.py:1642
  197.5 3.1 copy.90
  202.1 13.7 %convert_reduce_fusion = (f32[4608]{0:T(1024)}, bf16[512,4608]{1,0:T(8,128)(2,1)}) fusion(bf16[512,4608]{1,0:T(8,128)(2,1)} %get-tuple-element.42, bf16[512,1152]{1,0:T(8,128)(2,1)S(1)} %copy-done.8, bf16[4608,1152]{1,0:T(8,128)(2,1)} %get-tuple-element.41), kind=kOutput, calls=%fused_computation.10 | convolution fusion | flops 5447609856 | bytes 21252096 | tf_op jit(solution)/shard_map/td,fd->tf/dot_general | solution.py:1653
  215.8 12.0 %fusion.34 = (f32[512]{0:T(512)S(1)}, f32[512]{0:T(512)S(1)}, f32[512,1152]{1,0:T(8,128)S(1)}) fusion(f32[512,6912]{1,0:T(8,128)} %select_select_fusion, f32[512]{0:T(512)S(1)} %add_rsqrt_fusion.1, f32[512,1152]{1,0:T(8,128)S(1)} %copy-done, f32[512]{0:T(512)S(1)} %broadcast_multiply_fusion.5, bf16[512,4608]{1,0:T(8,128)(2,1)} %get-tuple-element.130, ...), kind=kOutput, calls=%fused_computation.94 | convolution fusion | flops 5439945728 | bytes 22421504 | tf_op jit(solution)/shard_map/tf,df->td/dot_general | solution.py:1656
  227.8 3.2 convert_reduce_fusion.4
  232.1 4.6 convolution_convert_fusion.4.upstream_ref
  236.7 31.6 %shard_map.273 = (bf16[512,3456]{1,0:T(8,128)(2,1)}, f32[256,16,256]{2,1,0:T(8,128)}) custom-call(bf16[768,3456]{1,0:T(8,128)(2,1)} %get-tuple-element.45.placed_ref, bf16[3,16,256,256]{3,2,1,0:T(8,128)(2,1)} %bitcast.52, bf16[512,1152]{1,0:T(8,128)(2,1)} %convolution_convert_fusion.4.upstream_ref, s32[1,512]{1,0:T(1,128)} %multiply_add_fusion.2.frame_row_ref, ...), custom_call_target="tpu_custom_call" | custom-call | tf_op jit(solution)/shard_map/pallas_call | solution.py:183
  268.3 11.5 %fusion.35 = (f32[512]{0:T(512)S(1)}, f32[512]{0:T(512)S(1)}, f32[512,5760]{1,0:T(8,128)}, f32[512,1152]{1,0:T(8,128)S(1)}) fusion(f32[512,6912]{1,0:T(8,128)} %select_select_fusion, f32[512]{0:T(512)S(1)} %add_rsqrt_fusion, f32[512]{0:T(512)S(1)} %broadcast_multiply_fusion.2, bf16[1,512,1152]{2,1,0:T(8,128)(2,1)S(1)} %copy-done.1, ...), kind=kOutput, calls=%fused_computation.95 | convolution fusion | flops 4081581056 | bytes 19767296 | tf_op jit(solution)/shard_map/te,de->td/dot_general | solution.py:1680
  279.8 4.2 fusion.18
  284.7 1.7 multiply_dynamic-update-slice_fusion.1
  288.2 2.4 convert_reduce_fusion.3
  290.6 7.1 %select_reduce_fusion.2 = (bf16[5760]{0:T(1024)(128)(2,1)S(1)}, bf16[5760]{0:T(1024)(128)(2,1)S(1)}, bf16[5760]{0:T(1024)(128)(2,1)S(1)}) fusion(f32[512,5760]{1,0:T(8,128)} %get-tuple-element.132, pred[512]{0:T(512)(128)(4,1)S(1)} %copy-done.22, pred[512]{0:T(512)(128)(4,1)S(1)} %copy-done.25, pred[512]{0:T(512)(128)(4,1)S(1)} %copy-done.24), kind=kLoop, calls=%fused_computation.7 | loop fusion | flops 17677440 | bytes 11832576 | tf_op jit(solution)/shard_map/reduce_sum | solution.py:1697
  298.7 12.7 %shard_map.274 = f32[128,128]{1,0:T(8,128)} custom-call(f32[256,16,256]{2,1,0:T(8,128)} %get-tuple-element.50.grad_ref, s32[256,256]{1,0:T(8,128)} %buckets_ref.3), custom_call_target="tpu_custom_call" | custom-call | tf_op jit(solution)/shard_map/pallas_call | solution.py:61
  318.8 8.1 %convolution_convert_fusion.1 = bf16[1152,4608]{1,0:T(8,128)(2,1)S(1)} fusion(bf16[512,1152]{1,0:T(8,128)(2,1)} %get-tuple-element.54, bf16[512,4608]{1,0:T(8,128)(2,1)} %get-tuple-element.130), kind=kOutput, calls=%fused_computation.2 | convolution fusion | flops 5441126400 | bytes 16515072 | tf_op jit(solution)/shard_map/td,tf->df/dot_general | solution.py:1655
  326.9 1.7 convolution_convert_fusion.3
  328.7 4.7 convolution_convert_fusion.2
  333.4 13.9 %pad_maximum_fusion.g12_ref = bf16[1152,9216]{1,0:T(8,128)(2,1)} fusion(bf16[1152,4608]{1,0:T(8,128)(2,1)S(1)} %convolution_convert_fusion.1, bf16[1152,1152]{1,0:T(8,128)(2,1)S(1)} %convolution_convert_fusion.3, bf16[1152,3456]{1,0:T(8,128)(2,1)S(1)} %convolution_convert_fusion.2), kind=kLoop, calls=%fused_computation | loop fusion | flops 63700992 | bytes 42467328 | tf_op jit(solution)/shard_map/concatenate | solution.py:1711
  347.3 12.2 %convolution_convert_fusion.g3_ref = bf16[4608,1152]{1,0:T(8,128)(2,1)} fusion(bf16[512,4608]{1,0:T(8,128)(2,1)} %get-tuple-element.55, bf16[512,1152]{1,0:T(8,128)(2,1)S(1)} %copy-done.10), kind=kOutput, calls=%fused_computation.1 | convolution fusion | flops 5441126400 | bytes 16515072 | tf_op jit(solution)/shard_map/tf,td->fd/dot_general | solution.py:1652
  359.5 220.5 %shard_map.275 = (f32[72,9216]{1,0:T(8,128)}, f32[288,1152]{1,0:T(8,128)}, f32[200,128]{1,0:T(8,128)}, f32[72,6912]{1,0:T(8,128)}, f32[8,6912]{1,0:T(8,128)}, /*index=5*/f32[16,8,128]{2,1,0:T(8,128)}) custom-call(bf16[32,1152]{1,0:T(8,128)(2,1)} %fusion.27.mg_ref, f32[200,128]{1,0:T(8,128)} %pad_bitcast_fusion.vec_ref, ...), custom_call_target="tpu_custom_call" | custom-call | tf_op jit(solution)/shard_map/pallas_call | solution.py:1334
  583.3 2.2 slice.89
  593.5 3.1 reshape.179
  598.9 2.4 copy.99
  (142 shorter events, 44.0 us)
Async XLA Ops:
  0.6 8.1 %copy-start.13 = (bf16[72,4608]{1,0:T(8,128)(2,1)S(1)}, bf16[72,4608]{1,0:T(8,128)(2,1)}, u32[]{:S(2)}) copy-start(bf16[72,4608]{1,0:T(8,128)(2,1)} %param.29) | copy-start | bytes 1990660
  8.8 2.5 copy-start.14
  8.8 2.5 copy-start.15
  10.3 2.2 copy-start.19
  10.3 2.3 copy-start.20
  11.3 2.9 copy-start.18
  188.7 8.1 %copy-start.21 = (pred[512]{0:T(512)(128)(4,1)}, pred[512]{0:T(512)(128)(4,1)S(1)}, u32[]{:S(2)}) copy-start(pred[512]{0:T(512)(128)(4,1)S(1)} %get-tuple-element.115) | copy-start | bytes 1540
  188.7 8.1 %copy-start.23 = (pred[512]{0:T(512)(128)(4,1)}, pred[512]{0:T(512)(128)(4,1)S(1)}, u32[]{:S(2)}) copy-start(pred[512]{0:T(512)(128)(4,1)S(1)} %get-tuple-element.116) | copy-start | bytes 1540
  188.7 8.8 %slice-start = ((s8[6291456]{0:T(1024)(128)(4,1)}), s8[4194304]{0:T(1024)(128)(4,1)S(1)}, s32[]{:S(2)}) async-start(s8[6291456]{0:T(1024)(128)(4,1)} %bitcast.55), calls=%async_computation | async-start | bytes 8388608
  188.7 8.1 %copy-start.1 = (bf16[1,512,1152]{2,1,0:T(8,128)(2,1)S(1)}, bf16[1,512,1152]{2,1,0:T(8,128)(2,1)}, u32[]{:S(2)}) copy-start(bf16[1,512,1152]{2,1,0:T(8,128)(2,1)} %param.17) | copy-start | bytes 3538948
  188.7 8.8 %slice-start.1 = ((s8[6291456]{0:T(1024)(128)(4,1)}), s8[2097152]{0:T(1024)(128)(4,1)S(1)}, s32[]{:S(2)}) async-start(s8[6291456]{0:T(1024)(128)(4,1)} %bitcast.55), calls=%async_computation.1 | async-start | bytes 4194304
  197.5 3.1 copy-start
  215.8 12.1 %copy-start.2 = (bf16[1,512,1152]{2,1,0:T(8,128)(2,1)S(1)}, bf16[1,512,1152]{2,1,0:T(8,128)(2,1)}, u32[]{:S(2)}) copy-start(bf16[1,512,1152]{2,1,0:T(8,128)(2,1)} %param.33) | copy-start | bytes 3538948
  279.8 4.9 copy-start.4
  288.2 2.4 copy-start.22
  288.2 2.4 copy-start.24
  288.2 2.4 copy-start.25
  298.7 15.7 %copy-start.3 = (bf16[512,3456]{1,0:T(8,128)(2,1)S(1)}, bf16[512,3456]{1,0:T(8,128)(2,1)}, u32[]{:S(2)}) copy-start(bf16[512,3456]{1,0:T(8,128)(2,1)} %get-tuple-element.47) | copy-start | bytes 10616836
  318.8 8.1 %copy-start.12 = (bf16[512,1152]{1,0:T(8,128)(2,1)S(1)}, bf16[512,1152]{1,0:T(8,128)(2,1)}, u32[]{:S(2)}) copy-start(bf16[512,1152]{1,0:T(8,128)(2,1)} %copy-done.11) | copy-start | bytes 3538948
  318.8 8.1 %copy-start.27 = (bf16[512,1152]{1,0:T(8,128)(2,1)S(1)}, bf16[512,1152]{1,0:T(8,128)(2,1)}, u32[]{:S(2)}) copy-start(bf16[512,1152]{1,0:T(8,128)(2,1)} %get-tuple-element.53) | copy-start | bytes 3538948
  333.4 13.9 %copy-start.10 = (bf16[512,1152]{1,0:T(8,128)(2,1)S(1)}, bf16[512,1152]{1,0:T(8,128)(2,1)}, u32[]{:S(2)}) copy-start(bf16[512,1152]{1,0:T(8,128)(2,1)} %get-tuple-element.40) | copy-start | bytes 3538948
  359.5 221.5 %copy-start.17 = (bf16[1,3,1152]{2,1,0:T(4,128)(2,1)S(1)}, bf16[1,3,1152]{2,1,0:T(4,128)(2,1)}, u32[]{:S(2)}) copy-start(bf16[1,3,1152]{2,1,0:T(4,128)(2,1)} %param.18) | copy-start | bytes 20740
  580.0 6.9 %copy-start.16 = (f32[200,128]{1,0:T(8,128)S(1)}, f32[200,128]{1,0:T(8,128)}, u32[]{:S(2)}) copy-start(f32[200,128]{1,0:T(8,128)} %get-tuple-element.60) | copy-start | bytes 307204
  596.5 4.8 copy-start.6
  (6 other events, 10.0 us)

commit v4 on v3

--- a/solution.py
+++ b/solution.py
@@ -1031,287 +1031,857 @@
     )(notes, bias_note, modulator, shard12, tokens, cotangent, slots[:, None], frame[None, :], frame[:, None], table, buckets, down)
 
 
-def feed_order(values, axis, chips):
-    shape = values.shape
-    part = shape[axis] // (2 * chips)
-    split = shape[:axis] + (chips, 2, part) + shape[axis + 1 :]
-    return jnp.swapaxes(values.reshape(split), axis, axis + 1).reshape(shape)
-def feed_restore(values, axis, chips):
-    shape = values.shape
-    part = shape[axis] // (2 * chips)
-    split = shape[:axis] + (2, chips, part) + shape[axis + 1 :]
-    return jnp.swapaxes(values.reshape(split), axis, axis + 1).reshape(shape)
-
-
-def rs_part(place, w, part):
-    x = place.x
+def aligned(value, size):
+    return value if isinstance(value, int) else pl.multiple_of(value, size)
+
+
+def scatter_part(x, w, part):
     unit = 768 if w < 2 else 96
-    off, size = {"all": (0, 3), "ad": (x, 2), "a": (2 * x, 1), "o": (2 - 2 * x, 1), "od": (1 - x, 2)}[part]
-    return pl.multiple_of(unit * off, 128 if w < 2 else 16), unit * size
+    off, size = {
+        "all": (0, 3),
+        "ad": (x, 2),
+        "a": (2 * x, 1),
+        "other": (2 - 2 * x, 1),
+    }[part]
+    return unit * off, unit * size
+
 
 class Scatter:
-    def __init__(self, place, acc12, acc3, rx, ry, rz, rf, send, recv):
-        self.p, self.acc12, self.acc3, self.rx, self.ry, self.rz, self.rf, self.send, self.recv = place, acc12, acc3, rx, ry, rz, rf, send, recv
+    def __init__(self, place, acc, over_x, over_y, over_z, ends, send, recv):
+        self.p, self.sums = place, acc
+        self.over_x, self.over_y, self.over_z, self.ends = over_x, over_y, over_z, ends
+        self.send, self.recv = send, recv
+
     def acc(self, w, chip, part):
-        off, size = rs_part(self.p, w, part)
+        off, size = scatter_part(self.p.x, w, part)
         if w < 2:
-            return self.acc12.at[chip, :, pl.ds(2304 * w + off, size)]
-        return self.acc3.at[chip, pl.ds(off, size), :]
-    def land(self, w, kind, i, size=None):
-        b = {"x": self.rx, "y": self.ry, "z": self.rz, "f": self.rf, "Y": self.rf}[kind]
-        if kind == "f":
-            return self.rf[w].at[0]
-        if kind == "Y":
-            return self.rf[w].at[1]
-        return b[w].at[i]
+            rows = pl.ds(aligned(chip * 144, 16), 144)
+            return self.sums[w].at[rows, pl.ds(aligned(off, 128), size)]
+        return self.sums[2].at[pl.ds(aligned(chip * 288 + off, 16), size), :]
+
     def copy(self, w, slot, src, dst, device):
-        return pltpu.make_async_remote_copy(src_ref=src, dst_ref=dst, send_sem=self.send.at[w, slot], recv_sem=self.recv.at[w, slot], device_id=device, device_id_type=MESH)
+        return pltpu.make_async_remote_copy(
+            src_ref=src,
+            dst_ref=dst,
+            send_sem=self.send.at[w, slot],
+            recv_sem=self.recv.at[w, slot],
+            device_id=device,
+            device_id_type=MESH,
+        )
+
     def x(self, w, j, yy):
-        return self.copy(w, 2 * (j - 1) + yy, self.acc(w, self.p.chip(j, yy), "o"), self.land(w, "x", 2 * (j - 1) + yy), self.p.at(x=1))
+        slot = 2 * (j - 1) + yy
+        src = self.acc(w, self.p.chip(j, yy), "other")
+        return self.copy(w, slot, src, self.over_x[w].at[slot], self.p.at(x=1))
+
     def y(self, w, j):
-        return self.copy(w, 5 + j, self.acc(w, self.p.chip(j, 1), "ad"), self.land(w, "y", j - 1), self.p.at(y=1))
-    def Y(self, w):
-        return self.copy(w, 9, self.acc(w, self.p.chip(0, 1), "all"), self.land(w, "Y", 0), self.p.at(y=1))
+        if j == 0:
+            return self.copy(
+                w, 9, self.acc(w, self.p.chip(0, 1), "all"), self.ends[w].at[0], self.p.at(y=1)
+            )
+        src = self.acc(w, self.p.chip(j, 1), "ad")
+        return self.copy(w, 5 + j, src, self.over_y[w].at[j - 1], self.p.at(y=1))
+
     def z(self, w, j):
-        return self.copy(w, 9 + j, self.acc(w, self.p.chip(j, 0), "ad"), self.land(w, "z", j - 1), self.p.at(j=j))
+        src = self.acc(w, self.p.chip(j, 0), "ad")
+        return self.copy(w, 9 + j, src, self.over_z[w].at[j - 1], self.p.at(j=j))
+
     def f(self, w):
-        return self.copy(w, 13, self.acc(w, self.p.chip(0, 0), "all"), self.land(w, "f", 0), self.p.at(x=1))
+        src = self.acc(w, self.p.chip(0, 0), "all")
+        return self.copy(w, 13, src, self.ends[w].at[1], self.p.at(x=1))
+
     def add(self, w, chip, part, land):
         dst = self.acc(w, chip, part)
-        rows = dst.shape[0]
         step = 48
+
         def body(i, _):
-            span = pl.ds(pl.multiple_of(i * step, 16), step)
+            span = pl.ds(aligned(i * step, 16), step)
             dst[span, :] = dst[span, :] + land[span, :]
             return 0
-        lax.fori_loop(0, rows // step, body, 0)
-    def ready(self, w, j, yy):
-        if j > 0:
+
+        lax.fori_loop(0, dst.shape[0] // step, body, 0)
+
+    def start_x(self, w, j):
+        for yy in (1, 0):
             self.x(w, j, yy).start()
-        elif yy == 1:
-            self.Y(w).start()
+
+    def start_y(self, w):
+        self.y(w, 0).start()
+
     def on_x(self, w, j, yy):
         self.x(w, j, yy).wait_recv()
-        self.add(w, self.p.chip(j, yy), "a", self.land(w, "x", 2 * (j - 1) + yy))
+        self.add(w, self.p.chip(j, yy), "a", self.over_x[w].at[2 * (j - 1) + yy])
         if yy == 1:
             self.y(w, j).start()
+
     def on_y(self, w, j):
         self.y(w, j).wait_recv()
-        self.add(w, self.p.chip(j, 0), "ad", self.land(w, "y", j - 1))
-        self.z(w, j).start()
-    def on_Y(self, w):
-        self.Y(w).wait_recv()
-        self.add(w, self.p.chip(0, 0), "all", self.land(w, "Y", 0))
+        if j == 0:
+            self.add(w, self.p.chip(0, 0), "all", self.ends[w].at[0])
+        else:
+            self.add(w, self.p.chip(j, 0), "ad", self.over_y[w].at[j - 1])
+            self.z(w, j).start()
+
     def on_z(self, w, j):
         self.z(w, j).wait_recv()
-        self.add(w, self.p.chip(0, 0), "ad", self.land(w, "z", j - 1))
-    def last(self, w):
+        self.add(w, self.p.chip(0, 0), "ad", self.over_z[w].at[j - 1])
+
+    def start_f(self, w):
         self.f(w).start()
+
     def finish(self, w):
         for j in (1, 2, 3):
             for yy in (0, 1):
                 self.x(w, j, yy).wait_send()
             self.y(w, j).wait_send()
             self.z(w, j).wait_send()
-        self.Y(w).wait_send()
-
-def rs_shapes():
-    V, D = pltpu.VMEM, pltpu.SemaphoreType.DMA
-    a = [V((8, 144, 4608), low), V((8, 288, 1152), low)]
-    rx = [V((6, 144, 768), low), V((6, 144, 768), low), V((6, 96, 1152), low)]
-    ry = [V((3, 144, 1536), low), V((3, 144, 1536), low), V((3, 192, 1152), low)]
-    rz = [V((3, 144, 1536), low), V((3, 144, 1536), low), V((3, 192, 1152), low)]
-    rf = [V((2, 144, 2304), low), V((2, 144, 2304), low), V((2, 288, 1152), low)]
-    return a, rx, ry, rz, rf
-
-def scatter_kernel(sizes, mg_ref, vec_ref, inbox_ref, mod_ref, g12_ref, g3_ref,
-                   out12_ref, out3_ref, vec_out_ref, gmod_ref, gmodsum_ref, cond_ref, *rest):
-    it = iter(rest)
-    take = lambda n: [next(it) for _ in range(n)]
-    acc12, acc3 = take(2)
-    rx, ry, rz, rf = take(3), take(3), take(3), take(3)
-    own12, own3, fin, sibfin = take(4)
-    vbuf, vsum, mgall, cpart = take(4)
-    send, recv, ssend, srecv, lsem, vsend, vrecv, msend, mrecv, csend, crecv, fsend, frecv = take(13)
+        self.y(w, 0).wait_send()
+
+
+def backward_kernel(
+    heads,
+    full12_ref,
+    full3_ref,
+    hidden_one_in,
+    placed_in,
+    weights_in,
+    attended_in,
+    branch_in,
+    middle_in,
+    hidden_two_in,
+    act_in,
+    slope_in,
+    mlp_grad_in,
+    cotangent_in,
+    tokens_in,
+    mod_in,
+    inbox_ref,
+    modulation_ref,
+    gate_sum_ref,
+    slots_ref,
+    frame_row_ref,
+    frame_column_ref,
+    buckets_ref,
+    out12_ref,
+    gmod_ref,
+    tokens_grad_ref,
+    spread_ref,
+    grid_ref,
+    out3_ref,
+    vec_out_ref,
+    gmod_sum_ref,
+    cond_ref,
+    acc0,
+    acc1,
+    acc3,
+    x0,
+    x1,
+    x2,
+    y0,
+    y1,
+    y2,
+    z0,
+    z1,
+    z2,
+    e0,
+    e1,
+    e2,
+    slots3,
+    turned,
+    feed_ref,
+    wide,
+    total,
+    middle,
+    sib_end,
+    vsum,
+    vbuf,
+    msum,
+    mine_ref,
+    cpart,
+    hist,
+    send,
+    recv,
+    ssend,
+    srecv,
+    lsem,
+    wsem,
+    vsend,
+    vrecv,
+    msend,
+    mrecv,
+    csend,
+    crecv,
+    fsend,
+    frecv,
+    psem,
+    gsem,
+    osem,
+):
     place = Place()
     x, d, c, z = place.x, place.d, place.c, place.z
+    rows, feed = feed_ref.shape
+    width = total.shape[1]
+    places = buckets_ref.shape[0]
+    head_width = width // heads
+    frames = 3 * places
+    scale = head_width ** (-0.5)
+    tile = 384
     barrier = pltpu.get_barrier_semaphore()
     for k in range(1, 16):
         pl.semaphore_signal(barrier, inc=1, device_id=(x, (d + k) % 16), device_id_type=MESH)
     pl.semaphore_signal(barrier, inc=1, device_id=place.at(x=1), device_id_type=MESH)
-    pl.semaphore_wait(barrier, 16)
-    s = Scatter(place, acc12, acc3, rx, ry, rz, rf, send, recv)
-    order = [(1, 1), (1, 0), (2, 1), (2, 0), (3, 1), (3, 0), (0, 1), (0, 0)]
-    def sib(w, n, recv_side=False):
-        j, yy = order[n]
-        chip = place.chip(j, yy)
-        cc = 1 - c
-        if w < 2:
-            src = g12_ref.at[pl.ds(pl.multiple_of(chip * 144, 16), 144), pl.ds(pl.multiple_of(4608 * w + 2304 * cc, 128), 2304)]
-            dst = acc12.at[chip, :, pl.ds(2304 * w, 2304)]
+
+    used = []
+
+    def local(src, dst):
+        cp = pltpu.make_async_copy(src, dst, lsem.at[len(used)])
+        used.append(cp)
+        cp.start()
+        return cp
+
+    def remote(src, dst, s, r, device):
+        return pltpu.make_async_remote_copy(
+            src_ref=src, dst_ref=dst, send_sem=s, recv_sem=r, device_id=device, device_id_type=MESH
+        )
+
+    get_act = local(act_in, feed_ref)
+    s = Scatter(
+        place, (acc0, acc1, acc3), (x0, x1, x2), (y0, y1, y2), (z0, z1, z2), (e0, e1, e2), send, recv
+    )
+
+    sent = []
+
+    def to_sibling(w, k, value, dst):
+        n = len(sent)
+        if n >= 2:
+            slot_free(n % 2)
+        slots3[n % 2] = value.astype(low)
+        remote(slots3.at[n % 2], dst, ssend.at[n % 2], srecv.at[w, k], place.at(core=1)).start()
+        sent.append(n)
+
+    def slot_free(n):
+        remote(
+            slots3.at[n], slots3.at[n], ssend.at[n], ssend.at[n], place.at(core=1)
+        ).wait_send()
+
+    def from_sibling(w, k, value, dst):
+        remote(slots3.at[0], dst, ssend.at[0], srecv.at[w, k], place.at(core=1)).wait_recv()
+        half = dst.shape[0] // 2
+        for part in (0, 1):
+            span = pl.ds(part * half, half)
+            dst[span, :] = (value[part * half : part * half + half] + dst[span, :].astype(full)).astype(low)
+
+    def turn(to, src, base):
+        def body(i, _):
+            cols = pl.ds(aligned(base + i * 128, 128), 128)
+            turned[to, pl.ds(aligned(i * 128, 128), 128), :] = src[:, cols].T
+            return 0
+
+        lax.fori_loop(0, width // 128, body, 0)
+
+    def down_group(side, group, mlp_ref):
+        core = 1 - c if side == 0 else c
+        half = 1 - z // 2 if group == 0 else z // 2
+        turn(group, feed_ref, core * (feed // 2) + half * width)
+        for k in range(3):
+            value = nn(turned[group], mlp_ref[:, k * tile : k * tile + tile])
+            dst = acc3.at[pl.ds(aligned(half * width, 16), width), k * tile : k * tile + tile]
+            (from_sibling if side else to_sibling)(2, 3 * group + k, value, dst)
+
+    def column_tile(side, w, k, which):
+        core = 1 - c if side == 0 else c
+        off = (1536 * (1 - x), 768, 1536 * x)[k // 2] + tile * (k % 2)
+        cols = pl.ds(aligned(core * (feed // 2) + off, 128), tile)
+        if not which:
+            left = 0
+        elif isinstance(off, int):
+            left = core if off >= width else 0
         else:
-            src = g3_ref.at[pl.ds(pl.multiple_of(cc * 2304 + chip * 288, 16), 288), :]
-            dst = acc3.at[chip]
-        return pltpu.make_async_remote_copy(src_ref=src, dst_ref=dst, send_sem=ssend.at[w, n], recv_sem=srecv.at[w, n], device_id=place.at(core=1), device_id_type=MESH)
-    def own(w, n):
-        j, yy = order[n]
-        chip = place.chip(j, yy)
-        if w < 2:
-            src = g12_ref.at[pl.ds(pl.multiple_of(chip * 144, 16), 144), pl.ds(pl.multiple_of(4608 * w + 2304 * c, 128), 2304)]
-            dst = own12.at[n % 2]
-        else:
-            src = g3_ref.at[pl.ds(pl.multiple_of(c * 2304 + chip * 288, 16), 288), :]
-            dst = own3.at[n % 2]
-        return pltpu.make_async_copy(src, dst, lsem.at[w, n])
-    def stage0(w):
-        for n in range(8):
-            sib(w, n).start()
-        own(w, 0).start()
-        for n in range(8):
-            if n < 7:
-                own(w, n + 1).start()
-            own(w, n).wait()
-            sib(w, n).wait_recv()
-            j, yy = order[n]
-            s.add(w, place.chip(j, yy), "all", (own12 if w < 2 else own3).at[n % 2])
-            s.ready(w, j, yy)
-    def mids(w):
-        for j in (1, 2, 3):
-            s.on_x(w, j, 1)
-            s.on_x(w, j, 0)
-    def ys(w):
-        for j in (1, 2, 3):
-            s.on_y(w, j)
-        s.on_Y(w)
-    def zs(w):
-        for j in (1, 2, 3):
-            s.on_z(w, j)
-        s.last(w)
+            left = jnp.where(off >= width, core, 0)
+        value = nn(turned[left], feed_ref[:, cols])
+        dst = s.sums[w].at[:, pl.ds(aligned(off, 128), tile)]
+        (from_sibling if side else to_sibling)(w, k, value, dst)
+
+    loads = []
+
+    def load_of(n):
+        which, piece = loads[n]
+        span = pl.ds(piece * width, width)
+        src = full3_ref.at[span, :] if which else full12_ref.at[:, span]
+        return pltpu.make_async_copy(src, wide.at[n % 2], wsem.at[n % 2])
+
+    def fetch(src):
+        loads.append(src)
+        load_of(len(loads) - 1).start()
+        return len(loads) - 1
+
+    def loaded(n):
+        load_of(n).wait()
+        return wide.at[n % 2]
+
+    def w12(piece):
+        return (0, piece)
+
+    def w3(piece):
+        return (1, piece)
+
+    def tiles(body):
+        def run(i, _):
+            body(i * tile)
+            return 0
+
+        lax.fori_loop(0, width // tile, run, 0)
+
+    def span_of(at, size=tile):
+        return pl.ds(aligned(at, 128), size)
+
+    def into_vec(row, value):
+        for i in range(value.shape[1] // 128):
+            vsum[row + i : row + i + 1, :] = value[:, 128 * i : 128 * i + 128]
+
+    step = 64
+
+    def row_loop(first, last, body):
+        def run(i, _):
+            body(pl.ds(aligned(i * step, step), step))
+            return 0
+
+        lax.fori_loop(first // step, last // step, run, 0)
+
+    def piece_sums(row, slots, value):
+        for slot in range(3):
+            msum[row + slot : row + slot + 1, :] += jnp.sum(
+                jnp.where(slots == slot, value, 0.0), axis=0, keepdims=True
+            )
+
+    def back_rows(normed, inverse, upstream):
+        return inverse * (
+            upstream
+            - jnp.mean(upstream, axis=-1, keepdims=True)
+            - normed * jnp.mean(upstream * normed, axis=-1, keepdims=True)
+        )
+
+    def feed_forward(slope_buf, branch_buf, mlp_ref, cotangent_ref, hidden_ref):
+        get_mlp = local(mlp_grad_in, mlp_ref)
+        a = fetch(w3(0))
+        b = fetch(w3(1))
+        get_slope = [local(slope_in.at[:, pl.ds(k * width, width)], slope_buf.at[k]) for k in (0, 1)]
+        get_hidden = local(hidden_two_in, hidden_ref)
+        get_branch = local(branch_in, branch_buf)
+        get_middle = local(middle_in, middle)
+        get_cotangent = local(cotangent_in, cotangent_ref)
+        msum[...] = jnp.zeros_like(msum)
+        msum[9:12, :] = gate_sum_ref[0:3, :]
+        pl.semaphore_wait(barrier, 16)
+        get_act.wait()
+        get_mlp.wait()
+        down_group(0, 0, mlp_ref)
+        down_group(0, 1, mlp_ref)
+        down_group(1, 0, mlp_ref)
+        s.start_x(2, 2)
+        s.start_x(2, 3)
+        down_group(1, 1, mlp_ref)
+        s.start_x(2, 1)
+        s.start_y(2)
+
+        def up_grad(n, piece):
+            weight = loaded(n)
+            get_slope[piece].wait()
+            slope = slope_buf.at[piece % 2]
+
+            def body(at):
+                value = nt(mlp_ref[...], weight[span_of(at), :]) * slope[:, span_of(at)].astype(full)
+                feed_ref[:, span_of(piece * width + at)] = value.astype(low)
+
+            tiles(body)
+            if piece < 2:
+                get_slope.append(
+                    local(slope_in.at[:, pl.ds((piece + 2) * width, width)], slope_buf.at[piece])
+                )
+
+        up_grad(a, 0)
+        a = fetch(w3(2))
+        s.on_x(2, 2, 1)
+        up_grad(b, 1)
+        b = fetch(w3(3))
+        s.on_x(2, 3, 1)
+        s.on_x(2, 2, 0)
+        up_grad(a, 2)
+        a = fetch(w12(4))
+        s.on_x(2, 3, 0)
+        s.on_x(2, 1, 1)
+        up_grad(b, 3)
+        b = fetch(w12(5))
+        s.on_x(2, 1, 0)
+        s.on_y(2, 0)
+        s.on_y(2, 2)
+        get_hidden.wait()
+        turn(0, hidden_ref, 0)
+        for k in range(6):
+            column_tile(0, 1, k, False)
+        s.on_y(2, 3)
+        for k in range(6):
+            column_tile(1, 1, k, False)
+            if k == 1:
+                for j in (2, 3, 1):
+                    s.start_x(1, j)
+        s.start_y(1)
+        s.on_y(2, 1)
+
+        def hidden_grad(n, piece):
+            weight = loaded(n)
+
+            def body(at):
+                value = nt(feed_ref[:, piece * width : piece * width + width], weight[span_of(at), :])
+                if piece == 0:
+                    total[:, span_of(at)] = value
+                else:
+                    total[:, span_of(at)] += value
+
+            tiles(body)
+
+        hidden_grad(a, 0)
+        a = fetch(w12(6))
+        s.on_z(2, 2)
+        hidden_grad(b, 1)
+        b = fetch(w12(7))
+        s.on_z(2, 3)
+        s.on_z(2, 1)
+        s.start_f(2)
+        hidden_grad(a, 2)
+        a = fetch(w12(3))
+        s.on_x(1, 2, 1)
+        hidden_grad(b, 3)
+        s.on_x(1, 3, 1)
+        for piece in range(feed // width):
+            span = slice(piece * width, piece * width + width)
+            into_vec(
+                128 + 27 + 9 * piece, jnp.sum(feed_ref[:, span].astype(full), axis=0, keepdims=True)
+            )
+        into_vec(128 + 63, jnp.sum(mlp_ref[...].astype(full), axis=0, keepdims=True))
+        get_branch.wait()
+        get_middle.wait()
+        get_cotangent.wait()
+
+        def norm_two(span):
+            slots = slots_ref[span, :]
+            normed, inverse = normalize_rows(middle[span, :])
+            grad = total[span, :]
+            grow = select_rows(modulation_ref, slots, 4, width)
+            mid = cotangent_ref[span, :].astype(full) + back_rows(
+                normed, inverse, grad * (1.0 + grow)
+            )
+            middle[span, :] = mid
+            gate = select_rows(modulation_ref, slots, 2, width)
+            feed_ref[span, 3 * width : 4 * width] = (gate * mid).astype(low)
+            piece_sums(0, slots, branch_buf[span, :] * mid)
+            piece_sums(3, slots, grad)
+            piece_sums(6, slots, grad * normed)
+
+        row_loop(0, rows, norm_two)
+        into_vec(
+            128 + 18, jnp.sum(feed_ref[:, 3 * width :].astype(full), axis=0, keepdims=True)
+        )
+        return a
+
+    windows = head_windows(heads, head_width)
+
+    def attention(n, placed, up, weights, grid_part):
+        get_placed = local(placed_in, placed)
+        head_loads = {}
+
+        def get_weights(head):
+            cp = pltpu.make_async_copy(weights_in.at[head], weights.at[head % 2], psem.at[head % 2])
+            cp.start()
+            head_loads[head] = cp
+
+        get_weights(0)
+        get_weights(1)
+        weight = loaded(n)
+
+        def body(at):
+            value = nt(feed_ref[:, 3 * width :], weight[span_of(at), :])
+            where = one_hot((frames, rows), 0, frame_row_ref[...])
+            up[:, span_of(at)] = nn(where, value.astype(low)).astype(low)
+
+        tiles(body)
+        s.on_x(1, 2, 0)
+        s.on_x(1, 3, 0)
+        get_placed.wait()
+
+        def grid_copy(head):
+            return pltpu.make_async_copy(grid_part.at[head % 2], grid_ref.at[head], gsem.at[head % 2])
+
+        def attend(first, last):
+            for head in range(first, last):
+                base, wide_at, offset = windows[head]
+                mask = lane_mask(places, wide_at, offset, head_width)
+                slot = head % 2
+                head_loads[head].wait()
+                if head >= 2:
+                    grid_copy(head - 2).wait()
+                for image in range(frames // places):
+                    at = slice(image * places, image * places + places)
+                    spans = [slice(p * width + base, p * width + base + wide_at) for p in range(3)]
+                    olds = [placed[at, span] for span in spans]
+                    query, key = [jnp.where(mask, t, jnp.zeros_like(t)) for t in olds[:2]]
+                    upstream = up[at, spans[0]]
+                    upstream = jnp.where(mask, upstream, jnp.zeros_like(upstream))
+                    shares = weights[slot, image]
+                    shares_f = shares.astype(full)
+                    share_grads = nt(upstream, olds[2])
+                    inner = jnp.sum(share_grads * shares_f, axis=-1, keepdims=True)
+                    score_f = shares_f * (share_grads - inner)
+                    score = score_f.astype(low)
+                    if image == 0:
+                        grid_part[slot] = score_f
+                    else:
+                        grid_part[slot] += score_f
+                    grads = (
+                        (nn(score, key) * scale).astype(low),
+                        (tn(score, query) * scale).astype(low),
+                        tn(shares, upstream).astype(low),
+                    )
+                    for span, old, grad in zip(spans, olds, grads):
+                        placed[at, span] = jnp.where(mask, grad, old)
+                grid_copy(head).start()
+                if head + 2 < heads:
+                    get_weights(head + 2)
+
+        attend(0, 3)
+        s.on_x(1, 1, 1)
+        s.on_y(1, 2)
+        attend(3, 6)
+        s.on_x(1, 1, 0)
+        s.on_y(1, 3)
+        attend(6, 9)
+        s.on_y(1, 0)
+        s.on_y(1, 1)
+        attend(9, 12)
+        s.on_z(1, 2)
+        s.on_z(1, 3)
+        attend(12, heads)
+        s.on_z(1, 1)
+        s.start_f(1)
+        grid_copy(heads - 2).wait()
+        grid_copy(heads - 1).wait()
+        for piece in range(3):
+
+            def body(at):
+                back = one_hot((rows, frames), 1, frame_column_ref[...])
+                span = span_of(piece * width + at)
+                feed_ref[:, span] = nn(back, placed[:, span]).astype(low)
+
+            tiles(body)
+
+    def projection(tokens_ref, hidden_ref, attended_ref):
+        get_hidden = local(hidden_one_in, hidden_ref)
+        get_attended = local(attended_in, attended_ref)
+        get_tokens = local(tokens_in, tokens_ref)
+        a = fetch(w12(0))
+        b = fetch(w12(1))
+        get_hidden.wait()
+        turn(0, hidden_ref, 0)
+        get_attended.wait()
+        turn(1, attended_ref, 0)
+        for k in range(6):
+            column_tile(0, 0, k, True)
+        for k in range(6):
+            column_tile(1, 0, k, True)
+            if k == 1:
+                for j in (2, 3, 1):
+                    s.start_x(0, j)
+        s.start_y(0)
+
+        def hidden_grad(n, piece):
+            weight = loaded(n)
+
+            def body(at):
+                value = nt(feed_ref[:, piece * width : piece * width + width], weight[span_of(at), :])
+                if piece == 0:
+                    total[:, span_of(at)] = value
+                else:
+                    total[:, span_of(at)] += value
+
+            tiles(body)
+
+        hidden_grad(a, 0)
+        a = fetch(w12(2))
+        s.on_x(0, 2, 1)
+        hidden_grad(b, 1)
+        s.on_x(0, 3, 1)
+        hidden_grad(a, 2)
+        s.on_x(0, 1, 1)
+        for i, piece in ((0, 0), (1, 2)):
+            span = slice(piece * width, piece * width + width)
+            into_vec(128 + 9 * i, jnp.sum(feed_ref[:, span].astype(full), axis=0, keepdims=True))
+        get_tokens.wait()
+
+        def norm_one(span):
+            slots = slots_ref[span, :]
+            normed, inverse = normalize_rows(tokens_ref[span, :].astype(full))
+            grad = total[span, :]
+            grow = select_rows(modulation_ref, slots, 1, width)
+            middle[span, :] += back_rows(normed, inverse, grad * (1.0 + grow))
+            piece_sums(16, slots, grad)
+            piece_sums(19, slots, grad * normed)
+
+        row_loop(0, rows, norm_one)
+
+    def row_of(xx, chip, cc):
+        return (x if xx == 0 else 1 - x) * 16 + chip * 2 + (c if cc == 0 else 1 - c)
+
+    def spread(slot, row, device, src=None):
+        return remote(
+            spread_ref.at[row] if src is None else src,
+            spread_ref.at[row],
+            msend.at[slot],
+            mrecv.at[slot],
+            device,
+        )
+
+    def first(slot, device):
+        return spread(slot, row_of(0, place.chip(), 0), device, mine_ref)
+
+    def mz(j, r=False):
+        if not r:
+            return first(j, place.at(j=j))
+        return spread(j, row_of(0, place.chip(j), 0), place.at(j=j))
+
+    def my(j, r=False):
+        if j == 0 and not r:
+            return first(4, place.at(y=1))
+        return spread(4 + j, row_of(0, place.chip(j, 1 if r else 0), 0), place.at(y=1))
+
+    def mx(j, yy, r=False):
+        if j == 0 and yy == 0 and not r:
+            return first(8, place.at(x=1))
+        row = row_of(1 if r else 0, place.chip(j, yy), 0)
+        return spread(8 + 2 * j + yy, row, place.at(x=1))
+
+    def ms(xx, j, yy, r=False):
+        slot = 16 + xx * 8 + 2 * j + yy
+        if xx == 0 and j == 0 and yy == 0 and not r:
+            return first(slot, place.at(core=1))
+        return spread(slot, row_of(xx, place.chip(j, yy), 1 if r else 0), place.at(core=1))
+
     def vcopy(n):
         if n < 3:
-            dev = (place.at(core=1), place.at(x=1), place.at(y=1))[n]
-            return pltpu.make_async_remote_copy(src_ref=vsum, dst_ref=vbuf.at[n], send_sem=vsend.at[n], recv_sem=vrecv.at[n], device_id=dev, device_id_type=MESH)
-        j = n - 2
-        return pltpu.make_async_remote_copy(src_ref=vsum, dst_ref=vbuf.at[3 + z], send_sem=vsend.at[n], recv_sem=vrecv.at[n], device_id=place.at(j=j), device_id_type=MESH)
-    def vrecv_wait(j):
-        pltpu.make_async_remote_copy(src_ref=vsum, dst_ref=vbuf.at[3 + place.zz(j)], send_sem=vsend.at[2 + j], recv_sem=vrecv.at[2 + j], device_id=place.at(j=j), device_id_type=MESH).wait_recv()
-    def mrow(xx, chip, cc):
-        return (x if xx == 0 else 1 - x) * 16 + chip * 2 + (c if cc == 0 else 1 - c)
-    def mcopy(slot, row, dev):
-        return pltpu.make_async_remote_copy(src_ref=mgall.at[row], dst_ref=mgall.at[row], send_sem=msend.at[slot], recv_sem=mrecv.at[slot], device_id=dev, device_id_type=MESH)
-    def mz(j, r=False):
-        return mcopy(j, mrow(0, place.chip(j if r else 0), 0), place.at(j=j))
-    def my(j, r=False):
-        return mcopy(4 + j, mrow(0, place.chip(j, 1 if r else 0), 0), place.at(y=1))
-    def mx(j, yy, r=False):
-        return mcopy(8 + 2 * j + yy, mrow(1 if r else 0, place.chip(j, yy), 0), place.at(x=1))
-    def ms(xx, j, yy, r=False):
-        return mcopy(16 + xx * 8 + 2 * j + yy, mrow(xx, place.chip(j, yy), 1 if r else 0), place.at(core=1))
-    stage0(2)
-    vsum[...] = vec_ref[...]
-    mgall[x * 16 + d] = mg_ref[...]
-    vcopy(0).start()
+            device = (place.at(core=1), place.at(x=1), place.at(y=1))[n]
+            return remote(vsum, vbuf.at[n], vsend.at[n], vrecv.at[n], device)
+        return remote(vsum, vbuf.at[3 + z], vsend.at[n], vrecv.at[n], place.at(j=n - 2))
+
+    def varrive(j):
+        remote(
+            vsum, vbuf.at[3 + place.zz(j)], vsend.at[2 + j], vrecv.at[2 + j], place.at(j=j)
+        ).wait_recv()
+
+    def histogram(box):
+        span = box.shape[2]
+        parts = places // span
+
+        def get(n):
+            return pltpu.make_async_copy(
+                grid_ref.at[:, pl.ds(n * span, span), :], box.at[n % 2], gsem.at[n % 2]
+            )
+
+        get(0).start()
+        hist[...] = jnp.zeros_like(hist)
+        for n in range(parts):
+            if n + 1 < parts:
+                get(n + 1).start()
+            get(n).wait()
+
+            def body(a8, _):
+                base = aligned(a8 * 8, 8)
+                index8 = buckets_ref[pl.ds(aligned(n * span + base, 8), 8), :]
+                values8 = box[n % 2, :, pl.ds(base, 8), :]
+                out = hist[...]
+                for a in range(8):
+                    index = index8[a : a + 1, :]
+                    lower, upper = index & 127, index >> 7
+                    mask = lax.broadcasted_iota(jnp.int32, (8, places), 0) == upper
+                    values = jnp.where(mask[None], values8[:, a : a + 1, :], 0.0)
+                    left = values.reshape(heads * 8, places).astype(low)
+                    right = one_hot((128, places), 0, lower)
+                    out += nt(left, right)
+                hist[...] = out
+                return 0
+
+            lax.fori_loop(0, span // 8, body, 0)
+
+    def modulator_grads(pieces_ref, mod_ref):
+        get_pieces = local(spread_ref, pieces_ref)
+        get_mod = local(mod_in, mod_ref)
+
+        def place_rows(p, devices):
+            base = 3 * (p - 2) if p >= 2 else 3 * p
+            shape = (devices * 16, devices * 8)
+            r = lax.broadcasted_iota(jnp.int32, shape, 0)
+            q = lax.broadcasted_iota(jnp.int32, shape, 1)
+            same = (r // 16 == q // 8) & (r % 16 - base == q % 8) & (q % 8 < 3)
+            return same.astype(full).astype(low)
+
+        activated = inbox_ref[...].reshape(256, 128).astype(low)
+        get_pieces.wait()
+        get_mod.wait()
+        cond_total = jnp.zeros((128, 128), full)
+        puts = []
+        for p in range(6):
+            half = 0 if p >= 2 else 16
+            span = slice(width * p, width * p + width)
+            pieces = pieces_ref[:, half : half + 16, :].reshape(512, width)
+            where = place_rows(p, 32)
+            left = nn(where, activated).astype(low)
+            total[72 * p : 72 * p + 72, :] = tn(left, pieces)[0:72]
+            puts.append(
+                local(total.at[pl.ds(72 * p, 72), :], gmod_ref.at[:, pl.ds(width * p, width)])
+            )
+            ones = jnp.sum(where.astype(full), axis=1, keepdims=True).astype(low)
+            gmod_sum_ref[:, span] = tn(jnp.broadcast_to(ones, (512, 128)), pieces)[0:8]
+            mine = pieces_ref[pl.ds(x * 16, 16), half : half + 16, :].reshape(256, width)
+            cond_rows = tn(place_rows(p, 16), mine).astype(low)
+            cond_total += nt(cond_rows, mod_ref[:, span])
+        cpart[...] = cond_total.reshape(16, 8, 128)
+        for cp in puts:
+            cp.wait()
+
+    def ccopy(k, r=False):
+        dest = (d + k) % 16
+        src = (d + 16 - k) % 16
+        return remote(
+            cpart.at[dest], cond_ref.at[src if r else d], csend.at[k], crecv.at[k], (x, dest)
+        )
+
+    ends = []
+    three = []
+
+    def end_copy(w):
+        chip = place.chip(0, 0)
+        return remote(
+            s.acc(w, chip, "all"), sib_end.at[w], fsend.at[w], frecv.at[w], place.at(core=1)
+        )
+
+    def final(w):
+        s.f(w).wait()
+        chip = place.chip(0, 0)
+        if w == 2:
+            rows3 = pl.ds(aligned(chip * 288, 16), 288)
+            total[0:288, :] = acc3[rows3, :].astype(full) + e2[1].astype(full)
+            three.append(local(total.at[pl.ds(0, 288), :], out3_ref))
+        else:
+            s.add(w, chip, "all", s.ends[w].at[1])
+            end_copy(w).start()
+
+    def write(w):
+        end_copy(w).wait()
+        own_rows = pl.ds(aligned(place.chip(0, 0) * 144, 16), 144)
+        for piece in range(4):
+            half, k = piece // 2, piece % 2
+            span = slice(width * k, width * k + width)
+            mine = s.sums[w][own_rows, span].astype(full)
+            theirs = sib_end[w, :, span].astype(full)
+            value = jnp.where(c == half, mine, theirs)
+            value = jnp.where(c == 0, value[0:72], value[72:144])
+            at = 4 * w + piece
+            stage, row = (middle, 72 * at) if at < 7 else (total, 432)
+            stage[row : row + 72, :] = value
+            ends.append(
+                local(stage.at[pl.ds(row, 72), :], out12_ref.at[:, pl.ds(width * at, width)])
+            )
+
+    V = pltpu.VMEM
+    picked = []
+    pl.run_scoped(
+        lambda *r: picked.append(feed_forward(*r)),
+        V((2, rows, width), low),
+        V((rows, width), full),
+        V((rows, width), low),
+        V((rows, width), low),
+        V((rows, width), low),
+    )
+    pl.run_scoped(
+        functools.partial(attention, picked[0]),
+        V((frames, 3 * width), low),
+        V((frames, width), low),
+        V((2, 3, places, places), low),
+        V((2, places, places), full),
+    )
+    pl.run_scoped(
+        projection, V((rows, width), low), V((rows, width), low), V((rows, width), low)
+    )
+    mine_ref[...] = msum[...].astype(low)
+    put_mine = local(mine_ref, spread_ref.at[row_of(0, place.chip(), 0)])
     for j in (1, 2, 3):
         mz(j).start()
     my(0).start()
     mx(0, 0).start()
     ms(0, 0, 0).start()
-    vcopy(0).wait()
-    vsum[...] += vbuf[0]
-    vcopy(1).start()
+    put_tokens = local(middle, tokens_grad_ref)
+    s.on_x(0, 2, 0)
+    s.on_x(0, 3, 0)
+    s.on_y(0, 2)
+    s.on_x(0, 1, 0)
     for j in (1, 2, 3):
         mz(j, True).wait_recv()
         my(j).start()
         mx(j, 0).start()
         ms(0, j, 0).start()
-    mids(2)
+    s.on_y(0, 3)
+    final(2)
+    pl.run_scoped(histogram, V((2, heads, 32, places), full))
+    vsum[0:128, :] = hist[...]
+    vcopy(0).start()
+    for j in range(4):
+        my(j, True).wait_recv()
+        mx(j, 1).start()
+        ms(0, j, 1).start()
+    s.on_y(0, 1)
+    s.on_y(0, 0)
+    vcopy(0).wait()
+    vsum[...] += vbuf[0]
+    vcopy(1).start()
+    s.on_z(0, 2)
+    s.on_z(0, 3)
+    s.on_z(0, 1)
+    s.start_f(0)
+    final(1)
+    for yy in (0, 1):
+        for j in range(4):
+            mx(j, yy, True).wait_recv()
+            ms(1, j, yy).start()
     vcopy(1).wait()
     vsum[...] += vbuf[1]
     vcopy(2).start()
-    for j in (0, 1, 2, 3):
-        my(j, True).wait_recv()
-        mx(j, 1).start()
-        ms(0, j, 1).start()
-    stage0(1)
-    ys(2)
+    put_mine.wait()
+    put_tokens.wait()
+    for xx in (0, 1):
+        for yy in (0, 1):
+            for j in range(4):
+                ms(xx, j, yy, True).wait_recv()
     vcopy(2).wait()
     vsum[...] += vbuf[2]
     for j in (1, 2, 3):
         vcopy(2 + j).start()
     vbuf[3 + z] = vsum[...]
-    for yy in (0, 1):
-        for j in range(4):
-            mx(j, yy, True).wait_recv()
-            ms(1, j, yy).start()
-    mids(1)
-    zs(2)
-    stage0(0)
-    ys(1)
-    mids(0)
-    zs(1)
-    for j in (1, 2, 3):
-        vrecv_wait(j)
-    vec_out_ref[...] = vbuf[3] + vbuf[4] + vbuf[5] + vbuf[6]
-    for xx in (0, 1):
-        for yy in (0, 1):
-            for j in range(4):
-                ms(xx, j, yy, True).wait_recv()
-    def place_rows(p, devices):
-        base = 3 * (p - 2) if p >= 2 else 3 * p
-        shape = (devices * 16, devices * 8)
-        r, q = lax.broadcasted_iota(jnp.int32, shape, 0), lax.broadcasted_iota(jnp.int32, shape, 1)
-        return ((r // 16 == q // 8) & (r % 16 - base == q % 8) & (q % 8 < 3)).astype(full).astype(low)
-    act = inbox_ref[...].reshape(256, 128).astype(low)
-    cond_total = jnp.zeros((128, 128), full)
-    for p in range(6):
-        tile = 0 if p >= 2 else 1
-        span = slice(1152 * p, 1152 * p + 1152)
-        pieces = mgall[:, 16 * tile : 16 * tile + 16, :].reshape(512, 1152)
-        where = place_rows(p, 32)
-        left = jnp.dot(where, act, preferred_element_type=full).astype(low)
-        grad = lax.dot_general(left, pieces, (((0,), (0,)), ((), ())), preferred_element_type=full)
-        gmod_ref[:, span] = grad[0:72]
-        ones = jnp.broadcast_to((jnp.sum(where.astype(full), axis=1, keepdims=True)).astype(low), (512, 128))
-        gmodsum_ref[:, span] = lax.dot_general(ones, pieces, (((0,), (0,)), ((), ())), preferred_element_type=full)[0:8]
-        mine = mgall[pl.ds(x * 16, 16), 16 * tile : 16 * tile + 16, :].reshape(256, 1152)
-        rows = lax.dot_general(place_rows(p, 16), mine, (((0,), (0,)), ((), ())), preferred_element_type=full).astype(low)
-        cond_total += lax.dot_general(rows, mod_ref[:, span], (((1,), (1,)), ((), ())), preferred_element_type=full)
-    cpart[...] = cond_total.reshape(16, 8, 128)
-    def ccopy(k, r=False):
-        dest = (d + k) % 16
-        src = (d + 16 - k) % 16
-        return pltpu.make_async_remote_copy(src_ref=cpart.at[dest], dst_ref=cond_ref.at[src if r else d], send_sem=csend.at[k], recv_sem=crecv.at[k], device_id=(x, dest), device_id_type=MESH)
+    three[0].wait()
+    pl.run_scoped(modulator_grads, V((32, 32, width), low), V(mod_in.shape, low))
     for k in range(1, 16):
         ccopy(k).start()
     cond_ref[d] = cpart[d]
-    ys(0)
-    zs(0)
-    def final(w):
-        s.f(w).wait()
-        chip = place.chip(0, 0)
-        if w == 2:
-            out3_ref[...] = acc3[chip].astype(full) + rf[2][0].astype(full)
-        else:
-            span = slice(2304 * w, 2304 * w + 2304)
-            fin[w] = (acc12[chip, :, span].astype(full) + rf[w][0].astype(full)).astype(low)
-            fcopy(w).start()
-    def fcopy(w):
-        return pltpu.make_async_remote_copy(src_ref=fin.at[w], dst_ref=sibfin.at[w], send_sem=fsend.at[w], recv_sem=frecv.at[w], device_id=place.at(core=1), device_id_type=MESH)
-    final(2)
-    final(1)
-    def write(w):
-        fcopy(w).wait()
-        mine, theirs = fin[w].astype(full), sibfin[w].astype(full)
-        mine = jnp.where(c == 0, mine[0:72], mine[72:144])
-        theirs = jnp.where(c == 0, theirs[0:72], theirs[72:144])
-        out12_ref[:, 4608 * w : 4608 * w + 2304] = jnp.where(c == 0, mine, theirs)
-        out12_ref[:, 4608 * w + 2304 : 4608 * w + 4608] = jnp.where(c == 0, theirs, mine)
     write(1)
+    for j in (1, 2, 3):
+        varrive(j)
+    vec_out_ref[...] = vbuf[3] + vbuf[4] + vbuf[5] + vbuf[6]
     final(0)
     write(0)
     for k in range(1, 16):
         ccopy(k, True).wait_recv()
         ccopy(k).wait_send()
+    for cp in ends:
+        cp.wait()
+    for n in range(2):
+        slot_free(n)
     for j in (1, 2, 3):
         vcopy(2 + j).wait_send()
         mz(j).wait_send()
@@ -1323,25 +1893,94 @@
                 ms(xx, j, yy).wait_send()
     for w in range(3):
         s.finish(w)
-        for n in range(8):
-            sib(w, n).wait_send()
-
-def scatter_grads(mg, vec, inbox, mod, g12, g3):
+
+
+def backward_pass(heads, big, small):
     any_, vm = pl.BlockSpec(memory_space=pl.ANY), pl.BlockSpec(memory_space=pltpu.VMEM)
-    a, rx, ry, rz, rf = rs_shapes()
-    V, D = pltpu.VMEM, pltpu.SemaphoreType.DMA
-    S = jax.ShapeDtypeStruct
+    V, D, S = pltpu.VMEM, pltpu.SemaphoreType.DMA, jax.ShapeDtypeStruct
+    rows, width = big[2].shape
+    feed = 4 * width
+    places = small[-1].shape[0]
+    flat = V((3, 144, 1536), low)
+    tall = V((3, 192, width), low)
     return pl.pallas_call(
-        functools.partial(scatter_kernel, None),
-        out_shape=(S((72, 9216), full), S((288, 1152), full), S(vec.shape, full), S((72, 6912), full), S((8, 6912), full), S((16, 8, 128), full)),
-        in_specs=[vm, vm, vm, vm, any_, any_],
-        out_specs=(vm,) * 6,
-        scratch_shapes=a + rx + ry + rz + rf + [
-            V((2, 144, 2304), low), V((2, 288, 1152), low), V((2, 144, 2304), low), V((2, 144, 2304), low),
-            V((7,) + vec.shape, full), V(vec.shape, full), V((32, 32, 1152), low), V((16, 8, 128), full),
-            D((3, 14)), D((3, 14)), D((3, 8)), D((3, 8)), D((3, 8)), D((6,)), D((6,)), D((32,)), D((32,)), D((16,)), D((16,)), D((2,)), D((2,))],
-        compiler_params=pltpu.CompilerParams(collective_id=1, has_side_effects=True, vmem_limit_bytes=63 * 2**20),
-    )(mg, vec, inbox, mod, g12, g3)
+        functools.partial(backward_kernel, heads),
+        out_shape=(
+            S((72, 8 * width), full),
+            S((72, 6 * width), full),
+            S((rows, width), full),
+            S((32, 32, width), low),
+            S((heads, places, places), full),
+            S((288, width), full),
+            S((200, 128), full),
+            S((8, 6 * width), full),
+            S((16, 8, 128), full),
+        ),
+        in_specs=[any_] * len(big) + [vm] * len(small),
+        out_specs=(any_,) * 6 + (vm,) * 3,
+        scratch_shapes=[
+            V((width, 2 * width), low),
+            V((width, 2 * width), low),
+            V((2 * width, width), low),
+            V((6, 144, 768), low),
+            V((6, 144, 768), low),
+            V((6, 96, width), low),
+            flat,
+            flat,
+            tall,
+            flat,
+            flat,
+            tall,
+            V((2, 144, 2 * width), low),
+            V((2, 144, 2 * width), low),
+            V((2, 288, width), low),
+            V((2, width, 384), low),
+            V((2, width, rows), low),
+            V((rows, feed), low),
+            V((2, width, width), low),
+            V((rows, width), full),
+            V((rows, width), full),
+            V((2, 144, 2 * width), low),
+            V((200, 128), full),
+            V((7, 200, 128), full),
+            V((32, width), full),
+            V((32, width), low),
+            V((16, 8, 128), full),
+            V((128, 128), full),
+            D((3, 14)),
+            D((3, 14)),
+            D((2,)),
+            D((3, 6)),
+            D((40,)),
+            D((2,)),
+            D((6,)),
+            D((6,)),
+            D((32,)),
+            D((32,)),
+            D((16,)),
+            D((16,)),
+            D((2,)),
+            D((2,)),
+            D((2,)),
+            D((2,)),
+            D((2,)),
+        ],
+        compiler_params=pltpu.CompilerParams(
+            collective_id=1, has_side_effects=True, vmem_limit_bytes=64 * 2**20
+        ),
+    )(*big, *small)
+
+
+def feed_order(values, axis, chips):
+    shape = values.shape
+    part = shape[axis] // (2 * chips)
+    split = shape[:axis] + (chips, 2, part) + shape[axis + 1 :]
+    return jnp.swapaxes(values.reshape(split), axis, axis + 1).reshape(shape)
+def feed_restore(values, axis, chips):
+    shape = values.shape
+    part = shape[axis] // (2 * chips)
+    split = shape[:axis] + (2, chips, part) + shape[axis + 1 :]
+    return jnp.swapaxes(values.reshape(split), axis, axis + 1).reshape(shape)
 
 
 def shards(
@@ -1598,6 +2237,7 @@
     )
     bias_note = jnp.pad(bias_note, ((0, 8 - len(bias_parts)), (0, 0)))
     chips = devices // 2
+    frame = slot_ids * image_tokens + places
     shard12 = jnp.pad(
         jnp.concatenate([projector, output_weight, feed_order(up_weight, 1, chips)], axis=1),
         ((0, 8), (0, 0)),
@@ -1629,92 +2269,54 @@
         tokens[0],
         cotangent[0],
         slot_ids,
-        slot_ids * image_tokens + places,
+        frame,
         position_table,
         buckets,
         down_weight,
     )
     packed_width = 3 * model_width
-    projector_all = full12[:, :packed_width]
-    output_all = full12[:, packed_width : 4 * model_width]
-    up_all = full12[:, 4 * model_width :]
-    local = slot_ids[:, None]
-    per_token = jnp.where(
-        local == 0, modulation[0:1], jnp.where(local == 1, modulation[1:2], modulation[2:3])
-    )
-    shift_attn, scale_attn, gate_attn, shift_mlp, scale_mlp, gate_mlp = jnp.split(
-        per_token, 6, axis=1
-    )
-    normed_one, inverse_one = normalize(inputs)
-    normed_two, inverse_two = normalize(middle)
-    upstream = cotangent[0].astype(full)
-
-    down_grad = jnp.einsum("tf,td->fd", activation_low, mlp_grad, preferred_element_type=full)
-    activation_grad = jnp.einsum("td,fd->tf", mlp_grad, down_all, preferred_element_type=full)
-    up_grad_low = (activation_grad * slope.astype(full)).astype(low)
-    up_grad = jnp.einsum("td,tf->df", hidden_two, up_grad_low, preferred_element_type=full)
-    hidden_two_grad = jnp.einsum(
-        "tf,df->td", up_grad_low, up_all, preferred_element_type=full
-    )
-    middle_grad = upstream + normalize_back(
-        normed_two, inverse_two, hidden_two_grad * (1.0 + scale_mlp)
-    )
-    attn_grad = (gate_attn * middle_grad).astype(low)
-    gate_attn_grad = branch_attn * middle_grad
-    output_grad = jnp.einsum("td,te->de", attended, attn_grad, preferred_element_type=full)
-    attended_grad = jnp.einsum(
-        "te,de->td", attn_grad, output_all, preferred_element_type=full
-    ).astype(low)
-    packed_grad, grid_grad = attend_backward(placed, jnp.swapaxes(weights, 0, 1), attended_grad, slot_ids, places)
-    projector_grad = jnp.einsum("td,te->de", hidden_one, packed_grad, preferred_element_type=full)
-    table_grad = table_histogram(grid_grad, buckets, bucket_count)
-    packed_sums = jnp.sum(packed_grad.astype(full), axis=0)
-    sums = (
-        table_grad.reshape(-1),
-        packed_sums[:model_width],
-        packed_sums[2 * model_width :],
-        jnp.sum(attn_grad.astype(full), axis=0),
-        jnp.sum(up_grad_low.astype(full), axis=0),
-        jnp.sum(mlp_grad.astype(full), axis=0),
-    )
-    hidden_one_grad = jnp.einsum(
-        "te,de->td", packed_grad, projector_all, preferred_element_type=full
-    )
-    inputs_grad = middle_grad + normalize_back(
-        normed_one, inverse_one, hidden_one_grad * (1.0 + scale_attn)
-    )
-    token_mod_grad = jnp.concatenate(
-        [
-            hidden_one_grad,
-            hidden_one_grad * normed_one,
-            gate_attn_grad,
-            hidden_two_grad,
-            hidden_two_grad * normed_two,
-        ],
-        axis=1,
-    )
-    modulation_grad = jnp.stack(
-        [jnp.sum(jnp.where(local == slot, token_mod_grad, 0.0), axis=0) for slot in range(images)]
-    )
-    modulation_grad = jnp.concatenate([modulation_grad, gate_sums[:images]], axis=1).astype(low)
-    mg = modulation_grad.reshape(images, 6, model_width).transpose(1, 0, 2)
-    mg = mg.reshape(6 * images, model_width)
-    late = 2 * images
-    mg = jnp.concatenate(
-        [
-            jnp.pad(mg[late:], ((0, 16 - 4 * images), (0, 0))),
-            jnp.pad(mg[:late], ((0, 16 - late), (0, 0))),
-        ]
-    )
-    vector = jnp.concatenate(sums)
-    vector = jnp.pad(vector, (0, 25600 - vector.shape[0])).reshape(200, 128)
-    grad12 = jnp.concatenate([projector_grad, output_grad, up_grad], axis=1).astype(low)
-    out12, down_grad, small, modulator_grad, modulator_sums, cond_parts = scatter_grads(
-        mg, vector, inbox, wide_modulator, grad12, down_grad.astype(low)
+    (
+        out12,
+        modulator_grad,
+        inputs_grad,
+        _,
+        _,
+        down_grad,
+        small,
+        modulator_sums,
+        cond_parts,
+    ) = backward_pass(
+        heads,
+        (
+            full12,
+            down_all,
+            hidden_one,
+            placed,
+            weights,
+            attended,
+            branch_attn,
+            middle,
+            hidden_two,
+            activation_low,
+            slope,
+            mlp_grad,
+            cotangent[0],
+            tokens[0],
+            wide_modulator,
+        ),
+        (
+            inbox,
+            modulation,
+            gate_sums,
+            slot_ids[:, None],
+            frame[None, :],
+            frame[:, None],
+            buckets,
+        ),
     )
     small = small.reshape(-1)
-    table_count = heads * bucket_count
-    table_total = small[:table_count].reshape(heads, bucket_count)
+    table_count = 128 * 128
+    table_total = small[:table_count].reshape(heads, -1)[:, :bucket_count]
     bias_grads = []
     start = table_count
     for part in bias_parts[1:]:

time: 615 us -> 491 us (0.80)
  the two profiles are of different devices: /device:TPU:9 before, /device:TPU:0 now
where the time goes in v4:
time: 491 us; the launch traced here: 483 us
  Pallas kernels  441 us (90%)
  local copies, waits for them, and re-layouts  35.9 us (7%)
    pallas_call x1, Pallas kernels, backward_pass(): pl.pallas_call(functools.partial(backward_kernel, heads), out_shape=(S((7...  259 us
    pallas_call x1, Pallas kernels, forward_pass(): pl.pallas_call(functools.partial(forward_kernel, heads), out_shape=(S((wi...  182 us

profile of v4, /device:TPU:0, one launch (start us, length us, event | category | flops | bytes accessed | tf_op | source)
XLA Modules:
  0.0 482.6 jit_solution(6028760844664568708)
XLA Ops:
  0.7 0.9 reshape.101
  6.2 2.5 pad.58.mod_in
  8.8 1.4 reshape.91
  10.3 0.9 reshape.92
  11.3 1.2 fusion.4.shard_ref
  13.5 0.7 multiply_add_fusion.frame_column_ref
  14.9 182.0 %shard_map.272 = (bf16[1152,9216]{1,0:T(8,128)(2,1)}, bf16[4608,1152]{1,0:T(8,128)(2,1)}, bf16[512,1152]{1,0:T(8,128)(2,1)}, bf16[768,3456]{1,0:T(8,128)(2,1)}, ...) custom-call(f32[16,8,128]{2,1,0:T(8,128)} %pad_convert_fusion.note_r, ...), custom_call_target="tpu_custom_call" | custom-call | tf_op jit(solution)/shard_map/pallas_call | solution.py:962
  196.9 259.0 %shard_map.273 = (f32[72,9216]{1,0:T(8,128)}, f32[72,6912]{1,0:T(8,128)}, f32[512,1152]{1,0:T(8,128)}, bf16[32,32,1152]{2,1,0:T(8,128)(2,1)}, f32[16,256,256]{2,...) custom-call(bf16[1152,9216]{1,0:T(8,128)(2,1)} %get-tuple-element.38.full12_, ...), custom_call_target="tpu_custom_call" | custom-call | tf_op jit(solution)/shard_map/pallas_call | solution.py:1906
  455.9 0.9 slice_bitcast_fusion
  456.9 0.7 fusion.9
  458.2 0.9 slice.45
  459.9 2.2 slice.46
  463.4 1.7 slice.51
  465.7 1.4 slice.54
  467.1 1.1 reshape.97
  468.2 0.9 copy.56
  469.1 3.1 reshape.98
  472.2 0.9 slice.55
  474.5 2.4 copy.80
  476.9 1.4 copy.81
  478.3 1.0 copy-done.2
  479.3 1.3 copy.82
  480.6 0.8 copy-done.3
  481.3 1.1 copy.83
  (55 shorter events, 11.1 us)
Async XLA Ops:
  0.6 8.1 %copy-start.4 = (bf16[72,4608]{1,0:T(8,128)(2,1)S(1)}, bf16[72,4608]{1,0:T(8,128)(2,1)}, u32[]{:S(2)}) copy-start(bf16[72,4608]{1,0:T(8,128)(2,1)} %param.29) | copy-start | bytes 1990660
  10.2 1.1 copy-start.5
  10.2 1.1 copy-start.6
  11.3 1.3 copy-start.9
  11.3 1.4 copy-start.10
  11.3 2.9 copy-start.8
  12.7 2.2 copy-start
  455.9 6.2 %copy-start.7 = (f32[200,128]{1,0:T(8,128)S(1)}, f32[200,128]{1,0:T(8,128)}, u32[]{:S(2)}) copy-start(f32[200,128]{1,0:T(8,128)} %get-tuple-element.58) | copy-start | bytes 307204
  472.2 4.7 copy-start.1
  476.9 2.4 copy-start.2
  479.3 2.0 copy-start.3
